TPU v7x, 256 devices: a whole 4x4x8 slice. The times are simulated.
256 devices in a mesh: ctx: 16 (over y, x), exp: 16 (over z, core).
Axes of the slice: x: 4, y: 4, z: 8, core: 2. Of those that a mesh axis runs over, the one named last changes fastest.
Arguments:
- queries: bfloat16 [16, 2048, 4096], P('exp', 'ctx'), may hold values from -0.29882812 to 0.29882812
- keys: bfloat16 [16, 2048, 4096], P('exp', 'ctx'), may hold values from -0.29882812 to 0.29882812
- values: bfloat16 [16, 2048, 4096], P('exp', 'ctx'), may hold values from -0.29882812 to 0.29882812
- out_grad: bfloat16 [16, 2048, 4096], P('exp', 'ctx'), may hold values from -6 to 6
- log_decay: float32 [16, 32, 2048], P('exp', None, 'ctx'), may hold values from -1 to 0
- doc_lengths: int32 [16, 4], P('exp'), may hold values from 1 to 1025, 2048 in all within a row
- moe_input: bfloat16 [2048, 3072], P(('ctx', 'exp')), may hold values from -6 to 6
- moe_grad: bfloat16 [2048, 3072], P(('ctx', 'exp')), may hold values from -6 to 6
- routes: int32 [2048, 2], P(('ctx', 'exp')), may hold values from 0 to 15, all different within a row; in each aligned block of 8 rows (0 to 7, 8 to 15, ...) at most 2 rows name the same one
- gate_weights: float32 [2048, 2], P(('ctx', 'exp')), may hold values from 0.1 to 0.9
- w_gate: bfloat16 [16, 4608, 3072], P('exp', 'ctx'), may hold values from -0.109375 to 0.109375
- w_up: bfloat16 [16, 4608, 3072], P('exp', 'ctx'), may hold values from -0.109375 to 0.109375
- w_down: bfloat16 [16, 4608, 3072], P('exp', 'ctx'), may hold values from -0.09375 to 0.09375
Outputs:
- d_queries: bfloat16 [16, 2048, 4096], P('exp', 'ctx')
- d_keys: bfloat16 [16, 2048, 4096], P('exp', 'ctx')
- d_values: bfloat16 [16, 2048, 4096], P('exp', 'ctx')
- d_moe_input: bfloat16 [2048, 3072], P(('ctx', 'exp'))
Inputs may be any that keep to these rules, and one draw needn't show every extreme that they name: `doc_lengths`: each row sums to 2048 and its longest document has 1025 positions. `routes`: two different experts a row; among the 8 rows of one device no expert is named more than 2 times.
All inputs are finite; a program needn't handle non-finite values.
Results may differ from a plain program's by a relative error of at most 0.02.
Values may be sent and summed in bfloat16 or wider, within the bound.
No kernel may reach another device: no remote copies, remote signals or barrier semaphores. Data moves between devices by JAX's collectives and lax.ppermute only.
A program may use at most 192 MiB of HBM per device.

v0:
```python
import jax
import jax.numpy as jnp
from jax import lax
from jax.sharding import PartitionSpec as P


def prefix(value, axis, combine, identity, reverse):
    size, position = (lax.axis_size(axis), lax.axis_index(axis))
    everything = jax.tree.map(
        lambda part, kind: lax.all_gather(part.astype(kind), axis),
        value,
        (jnp.bfloat16, jnp.bfloat16),
    )
    start = jax.tree.map(
        lambda part, zero: jnp.broadcast_to(jnp.asarray(zero, part.dtype), part.shape),
        value,
        identity,
    )

    def lap(k, before):
        at = size - 1 - k if reverse else k
        reached = at > position if reverse else at < position
        new = combine(
            before, jax.tree.map(lambda part, own: part[at].astype(own.dtype), everything, value)
        )
        return jax.tree.map(lambda a, b: jnp.where(reached, a, b), new, before)

    return lax.fori_loop(0, size, lap, start)


def decay_tables(natural_log_fades, starts):
    segment = jnp.cumsum(starts.astype(jnp.int32))
    running = jnp.cumsum(natural_log_fades, axis=1)
    length = natural_log_fades.shape[1]
    places = jnp.arange(length, dtype=jnp.int32)
    linked = (segment[:, None] == segment[None, :]) & (places[:, None] >= places[None, :])
    spread = jnp.where(linked[None], running[:, :, None] - running[:, None, :], 0.0)
    within = jnp.where(linked[None], jnp.exp(spread), 0.0)
    from_start = jnp.exp(running) * (segment == 0)[None, :]
    to_end = jnp.exp(running[:, -1:] - running) * (segment == segment[-1])[None, :]
    return (within, from_start, to_end, from_start[:, -1])


def local_sums(query_rows, key_rows, value_rows, grad_rows, from_start, to_end):
    keys_end = (key_rows.astype(jnp.float32) * to_end.T[:, :, None]).astype(jnp.bfloat16)
    queries_start = (query_rows.astype(jnp.float32) * from_start.T[:, :, None]).astype(jnp.bfloat16)
    state_local = jnp.einsum(
        "shd,she->hde", keys_end, value_rows, preferred_element_type=jnp.float32
    )
    grad_local = jnp.einsum(
        "uhd,uhe->hde", queries_start, grad_rows, preferred_element_type=jnp.float32
    )
    return (state_local, grad_local)


def block_grads(
    query_rows, key_rows, value_rows, grad_rows, within, from_start, to_end, state_in, carried
):
    state_half = state_in.astype(jnp.bfloat16)
    carried_half = carried.astype(jnp.bfloat16)
    flipped = jnp.swapaxes(within, 1, 2)
    mixed_q = jnp.einsum("the,she->hts", grad_rows, value_rows, preferred_element_type=jnp.float32)
    weight_q = (mixed_q * within).astype(jnp.bfloat16)
    mixed_k = jnp.einsum("the,uhe->htu", value_rows, grad_rows, preferred_element_type=jnp.float32)
    weight_k = (mixed_k * flipped).astype(jnp.bfloat16)
    mixed_v = jnp.einsum("thd,uhd->htu", key_rows, query_rows, preferred_element_type=jnp.float32)
    weight_v = (mixed_v * flipped).astype(jnp.bfloat16)
    grad_q = jnp.einsum("hts,shd->thd", weight_q, key_rows, preferred_element_type=jnp.float32)
    grad_q = grad_q + from_start.T[:, :, None] * jnp.einsum(
        "the,hde->thd", grad_rows, state_half, preferred_element_type=jnp.float32
    )
    grad_k = jnp.einsum("htu,uhd->thd", weight_k, query_rows, preferred_element_type=jnp.float32)
    grad_k = grad_k + to_end.T[:, :, None] * jnp.einsum(
        "the,hde->thd", value_rows, carried_half, preferred_element_type=jnp.float32
    )
    grad_v = jnp.einsum("htu,uhe->the", weight_v, grad_rows, preferred_element_type=jnp.float32)
    grad_v = grad_v + to_end.T[:, :, None] * jnp.einsum(
        "thd,hde->the", key_rows, carried_half, preferred_element_type=jnp.float32
    )
    return (grad_q.astype(jnp.bfloat16), grad_k.astype(jnp.bfloat16), grad_v.astype(jnp.bfloat16))


def forward_combine(earlier, later):
    return (earlier[0] * later[0], later[0][:, None, None] * earlier[1] + later[1])


def backward_combine(earlier, later):
    return (later[0] * earlier[0], later[1] + later[0][:, None, None] * earlier[1])


def slot_table(route_ids, capacity, experts):
    flat_ids = route_ids.reshape(-1)
    route_count = flat_ids.shape[0]
    onehot_ids = (flat_ids[:, None] == jnp.arange(experts, dtype=jnp.int32)[None, :]).astype(
        jnp.int32
    )
    earlier = jnp.cumsum(onehot_ids, axis=0) - onehot_ids
    ranks = jnp.sum(earlier * onehot_ids, axis=1)
    slots = flat_ids * capacity + ranks
    matches = slots[None, :] == jnp.arange(experts * capacity, dtype=jnp.int32)[:, None]
    filled = jnp.any(matches, axis=1)
    sources = jnp.sum(
        jnp.where(matches, jnp.arange(route_count, dtype=jnp.int32)[None, :], 0), axis=1
    )
    return (slots, filled, sources)


def fill_slots(token_rows, scaled_rows, route_ids, capacity, experts):
    slots, filled, sources = slot_table(route_ids, capacity, experts)
    input_slots = jnp.where(
        filled[:, None], token_rows[sources // 2], jnp.zeros((), token_rows.dtype)
    )
    grad_slots = jnp.where(filled[:, None], scaled_rows[sources], jnp.zeros((), scaled_rows.dtype))
    width = token_rows.shape[1]
    return (
        input_slots.reshape(experts, capacity, width),
        grad_slots.reshape(experts, capacity, width),
    )


def scale_grads(grad_rows, gate_rows):
    doubled = jnp.repeat(grad_rows, 2, axis=0).astype(jnp.float32)
    return (gate_rows.reshape(-1)[:, None] * doubled).astype(jnp.bfloat16)


def expert_grads(input_rows, grad_rows, gate_slab, up_slab, down_slab):
    contract = (((1,), (1,)), ((), ()))
    gate_value = lax.dot_general(
        input_rows, gate_slab, contract, preferred_element_type=jnp.float32
    )
    up_value = lax.dot_general(input_rows, up_slab, contract, preferred_element_type=jnp.float32)
    hidden_grad = lax.dot_general(
        grad_rows, down_slab, contract, preferred_element_type=jnp.float32
    )
    sigmoid = jax.nn.sigmoid(gate_value)
    grad_up = (hidden_grad * gate_value * sigmoid).astype(jnp.bfloat16)
    grad_gate = (hidden_grad * up_value * sigmoid * (1.0 + gate_value * (1.0 - sigmoid))).astype(
        jnp.bfloat16
    )
    return jnp.dot(grad_gate, gate_slab, preferred_element_type=jnp.float32) + jnp.dot(
        grad_up, up_slab, preferred_element_type=jnp.float32
    )


def per_device(
    queries,
    keys,
    values,
    out_grad,
    log_decay,
    doc_lengths,
    moe_input,
    moe_grad,
    routes,
    gate_weights,
    w_gate,
    w_up,
    w_down,
):
    length = queries.shape[1]
    width_all = queries.shape[2]
    head_count = log_decay.shape[1]
    head_size = width_all // head_count
    shape_three = (length, head_count, head_size)
    query_rows = queries[0].reshape(shape_three)
    key_rows = keys[0].reshape(shape_three)
    value_rows = values[0].reshape(shape_three)
    grad_rows = out_grad[0].reshape(shape_three)
    lengths_row = doc_lengths[0]
    doc_starts = jnp.cumsum(lengths_row) - lengths_row
    positions = lax.axis_index("ctx") * length + jnp.arange(length, dtype=jnp.int32)
    starts = jnp.any(positions[:, None] == doc_starts[None, :], axis=1)
    within, from_start, to_end, block_decay = decay_tables(log_decay[0], starts)
    state_local, grad_local = local_sums(
        query_rows, key_rows, value_rows, grad_rows, from_start, to_end
    )
    forward = prefix(
        (block_decay, state_local),
        "ctx",
        forward_combine,
        (jnp.ones_like(block_decay), jnp.zeros_like(state_local)),
        False,
    )
    backward = prefix(
        (block_decay, grad_local),
        "ctx",
        backward_combine,
        (jnp.ones_like(block_decay), jnp.zeros_like(grad_local)),
        True,
    )
    grad_q, grad_k, grad_v = block_grads(
        query_rows,
        key_rows,
        value_rows,
        grad_rows,
        within,
        from_start,
        to_end,
        forward[1],
        backward[1],
    )
    experts = lax.axis_size("exp") * w_gate.shape[0]
    tokens_dev = moe_input.shape[0]
    capacity = max(2, 4 * tokens_dev // experts)
    model_width = moe_input.shape[1]
    scaled = scale_grads(moe_grad, gate_weights)
    slots = slot_table(routes, capacity, experts)[0]
    slot_in, slot_grad = fill_slots(moe_input, scaled, routes, capacity, experts)
    arrived_in, arrived_grad = (
        lax.all_to_all(slot_in, "exp", split_axis=0, concat_axis=0, tiled=True),
        lax.all_to_all(slot_grad, "exp", split_axis=0, concat_axis=0, tiled=True),
    )
    gathered_in, gathered_grad = (
        lax.all_gather(arrived_in[None], "ctx", axis=0, tiled=True),
        lax.all_gather(arrived_grad[None], "ctx", axis=0, tiled=True),
    )
    gate_slab = w_gate[0]
    up_slab = w_up[0]
    down_slab = w_down[0]
    term = expert_grads(
        gathered_in.reshape(-1, model_width),
        gathered_grad.reshape(-1, model_width),
        gate_slab,
        up_slab,
        down_slab,
    )
    summed = lax.psum_scatter(
        term.reshape(gathered_in.shape).astype(jnp.bfloat16), "ctx", scatter_dimension=0, tiled=True
    ).astype(jnp.float32)
    returned = lax.all_to_all(
        summed[0].astype(jnp.bfloat16), "exp", split_axis=0, concat_axis=0, tiled=True
    )
    route_rows = returned.reshape(experts * capacity, model_width)[slots].astype(jnp.float32)
    d_moe = route_rows.reshape(tokens_dev, 2, model_width).sum(axis=1).astype(jnp.bfloat16)
    return (
        grad_q.reshape(1, length, width_all),
        grad_k.reshape(1, length, width_all),
        grad_v.reshape(1, length, width_all),
        d_moe,
    )


def solution(mesh):
    placed = (
        P("exp", "ctx", None),
        P("exp", "ctx", None),
        P("exp", "ctx", None),
        P("exp", "ctx", None),
        P("exp", None, "ctx"),
        P("exp", None),
        P(("ctx", "exp"), None),
        P(("ctx", "exp"), None),
        P(("ctx", "exp"), None),
        P(("ctx", "exp"), None),
        P("exp", "ctx", None),
        P("exp", "ctx", None),
        P("exp", "ctx", None),
    )
    return jax.shard_map(
        per_device,
        mesh=mesh,
        in_specs=placed,
        out_specs=(
            P("exp", "ctx", None),
            P("exp", "ctx", None),
            P("exp", "ctx", None),
            P(("ctx", "exp"), None),
        ),
        check_vma=False,
    )
```

profile of v0, /device:TPU:1, one launch (start us, length us, event | category | flops | bytes accessed | tf_op | source)
XLA Modules:
  0.0 567.7 jit_solution(7937445669619896677)
XLA Ops:
  12.7 20.2 %all_to_all.15 = bf16[16,2,3072]{2,1,0:T(2,128)(2,1)} all-to-all(bf16[16,2,3072]{2,1,0:T(2,128)(2,1)S(1)} %get-tuple-element.310), channel_id=1, replica_groups=mesh['ctx'=16,'exp'=16] {'exp'}, dimensions={0} | all-to-all | bytes 393216 | tf_op jit(solution)/shard_map/all_to_all | solution.py:210
  33.0 13.0 %all_to_all.16 = bf16[16,2,3072]{2,1,0:T(2,128)(2,1)} all-to-all(bf16[16,2,3072]{2,1,0:T(2,128)(2,1)S(1)} %get-tuple-element.311), channel_id=1, replica_groups=mesh['ctx'=16,'exp'=16] {'exp'}, dimensions={0} | all-to-all | bytes 393216 | tf_op jit(solution)/shard_map/all_to_all | solution.py:211
  46.1 36.3 %all-gather.16.cloned.1.call-done = bf16[256,2,3072]{2,1,0:T(2,128)(2,1)} async-done(((bf16[16,2,3072]{2,1,0:T(2,128)(2,1)}), bf16[256,2,3072]{2,1,0:T(2,128)(2,1)}) %all-gather.16.cloned.1.call-update) | async-done | bytes 3145744 | tf_op jit(solution)/shard_map/all_gather | solution.py:214
  82.4 7.5 %reshape.286 = bf16[512,3072]{1,0:T(8,128)(2,1)} reshape(bf16[256,2,3072]{2,1,0:T(2,128)(2,1)} %all-gather.16.cloned.1.call-done) | data formatting | bytes 6291456 | tf_op jit(solution)/shard_map/reshape | solution.py:221
  93.5 43.3 %all-gather.14.cloned.1.call-done = bf16[256,2,3072]{2,1,0:T(2,128)(2,1)} async-done(((bf16[16,2,3072]{2,1,0:T(2,128)(2,1)}), bf16[256,2,3072]{2,1,0:T(2,128)(2,1)}) %all-gather.14.cloned.1.call-update) | async-done | bytes 3145744 | tf_op jit(solution)/shard_map/all_gather | solution.py:215
  136.8 7.5 %reshape.285 = bf16[512,3072]{1,0:T(8,128)(2,1)} reshape(bf16[256,2,3072]{2,1,0:T(2,128)(2,1)} %all-gather.14.cloned.1.call-done) | data formatting | bytes 6291456 | tf_op jit(solution)/shard_map/reshape | solution.py:222
  147.9 8.0 %fusion.8 = f32[512,3072]{1,0:T(8,128)} fusion(bf16[1,288,3072]{2,1,0:T(8,128)(2,1)} %param.27, f32[512,288]{0,1:T(8,128)S(1)} %fusion.15, bf16[512,3072]{1,0:T(8,128)(2,1)} %reshape.286, bf16[1,288,3072]{2,1,0:T(8,128)(2,1)S(1)} %copy-done, f32[512,288]{0,1:T(8,128)S(1)} %fusion.10), kind=kOutput, calls=%fused_computation.25 | convolution fusion | flops 1813413888 | bytes 14155776 | tf_op jit(solution)/shard_map/dot_general | solution.py:140
  155.9 6.4 %add_convert_fusion = bf16[512,3072]{1,0:T(8,128)(2,1)} fusion(f32[512,3072]{1,0:T(8,128)} %fusion.8, bf16[1,288,3072]{2,1,0:T(8,128)(2,1)S(1)} %copy-done, f32[512,288]{0,1:T(8,128)S(1)} %fusion.15, f32[512,288]{0,1:T(8,128)S(1)} %fusion.10), kind=kOutput, calls=%fused_computation.9 | convolution fusion | flops 910000128 | bytes 12386304 | tf_op jit(solution)/shard_map/dot_general | solution.py:140
  162.3 6.0 %convert_element_type.197 = bf16[16,16,2,3072]{3,2,1,0:T(2,128)(2,1)S(1)} reshape(bf16[512,3072]{1,0:T(8,128)(2,1)} %add_convert_fusion) | data formatting | bytes 6291456 | tf_op jit(solution)/shard_map/convert_element_type | solution.py:228
  184.3 31.2 %all-reduce = bf16[512]{0:T(512)(128)(2,1)S(1)} all-reduce(bf16[512]{0:T(512)(128)(2,1)S(1)} %dynamic-update-slice), channel_id=2, replica_groups=mesh['ctx'=16,'exp'=16] {'ctx'}, use_global_device_ids=true, to_apply=%add | all-reduce | flops 512 | bytes 2048
  216.9 4.4 fusion.19
  221.3 4.6 fusion.17
  225.9 23.6 %reduce-scatter.4.cloned.1.call-done = bf16[1,16,2,3072]{3,1,2,0:T(8,128)(2,1)} async-done(((bf16[16,16,2,3072]{3,1,2,0:T(8,128)(2,1)}), bf16[1,16,2,3072]{3,1,2,0:T(8,128)(2,1)}) %reduce-scatter.4.cloned.1.call-update) | async-done | bytes 196624
  251.3 9.4 %all-to-all-start.2 = ((bf16[16,2,3072]{2,1,0:T(2,128)(2,1)}), bf16[16,2,3072]{2,1,0:T(2,128)(2,1)S(1)}, u32[]{:S(2)}, u32[]{:S(2)}) async-start(bf16[16,2,3072]{2,1,0:T(2,128)(2,1)} %copy.116), calls=%async_computation.2 | async-start | bytes 393216 | tf_op jit(solution)/shard_map/all_to_all | solution.py:230
  260.7 4.4 fusion.18
  265.1 5.9 %all-to-all-done.2 = bf16[16,2,3072]{2,1,0:T(2,128)(2,1)S(1)} async-done(((bf16[16,2,3072]{2,1,0:T(2,128)(2,1)}), bf16[16,2,3072]{2,1,0:T(2,128)(2,1)S(1)}, u32[]{:S(2)}, u32[]{:S(2)}) %all-to-all-start.2) | async-done | bytes 196640 | tf_op jit(solution)/shard_map/all_to_all | solution.py:230
  272.7 96.9 %all-gather.12.cloned.1.call-done = bf16[512,128,128]{2,1,0:T(8,128)(2,1)} async-done(((bf16[32,128,128]{2,1,0:T(8,128)(2,1)}), bf16[512,128,128]{2,1,0:T(8,128)(2,1)}) %all-gather.12.cloned.1.call-update) | async-done | bytes 16777232 | tf_op jit(solution)/shard_map/all_gather | solution.py:10
  369.7 46.8 %while.31 = (s32[]{:T(128)}, f32[32,128,128]{2,1,0:T(8,128)S(1)}, s32[]{:T(128)}, bf16[16,32,128,128]{3,2,1,0:T(8,128)(2,1)}, bf16[16,32]{1,0:T(8,128)(2,1)}, /*index=5*/s32[]{:T(128)}, s32[]{:T(128)}, s32[]{:T(128)}, s32[]{:T(128)}) while((s32[]{:T(128)}, f32[32,128,128]{2,1,0:T(8,128)S(1)}, s32[]{:T(128)}, ...), condition=%wide.region_7.8_spmd.clone, body=%wide.region_6.7_spmd.clone.sunk | while | flops 2621480 | bytes 5243367 | solution.py:28
  416.5 4.5 fusion.5
  429.0 59.1 %all-gather.10.cloned.1.call-done = bf16[512,128,128]{2,1,0:T(8,128)(2,1)} async-done(((bf16[32,128,128]{2,1,0:T(8,128)(2,1)}), bf16[512,128,128]{2,1,0:T(8,128)(2,1)}) %all-gather.10.cloned.1.call-update) | async-done | bytes 16777232 | tf_op jit(solution)/shard_map/all_gather | solution.py:10
  488.1 67.0 %while.30 = (s32[]{:T(128)}, f32[32,128,128]{2,1,0:T(8,128)}, s32[]{:T(128)}, bf16[16,32]{1,0:T(8,128)(2,1)}, bf16[16,32,128,128]{3,2,1,0:T(8,128)(2,1)}, /*index=5*/s32[]{:T(128)}, s32[]{:T(128)}) while((s32[]{:T(128)}, f32[32,128,128]{2,1,0:T(8,128)}, s32[]{:T(128)}, bf16[16,32]{1,0:T(8,128)(2,1)}, ...), condition=%wide.region_5.6_spmd.clone, body=%wide.region_4.5_spmd.clone.sunk | while | flops 2621476 | bytes 5243305 | solution.py:28
  492.4 3.5 fusion.90
  496.6 3.5 fusion.90
  500.8 3.5 fusion.90
  505.1 3.5 fusion.90
  509.3 3.5 fusion.90
  513.5 3.5 fusion.90
  517.7 3.5 fusion.90
  522.0 3.5 fusion.90
  526.2 3.5 fusion.90
  530.4 3.5 fusion.90
  555.1 3.8 fusion.7
  (157 shorter events, 120.6 us)
Async XLA Ops:
  7.2 140.7 %copy-start = (bf16[1,288,3072]{2,1,0:T(8,128)(2,1)S(1)}, bf16[1,288,3072]{2,1,0:T(8,128)(2,1)}, u32[]{:S(2)}) copy-start(bf16[1,288,3072]{2,1,0:T(8,128)(2,1)} %param.28) | copy-start | bytes 5308420
  7.2 4.2 copy-start.2
  7.2 75.2 %all-gather.16.cloned.1.call-start = ((), (), s32[]{:S(2)}) async-start(), calls=%async_computation.7 | async-start | bytes 3342336 | tf_op jit(solution)/shard_map/all_gather | solution.py:214
  32.9 103.9 %all-gather.14.cloned.1.call-start = ((), (), s32[]{:S(2)}) async-start(), calls=%async_computation.6 | async-start | bytes 3342336 | tf_op jit(solution)/shard_map/all_gather | solution.py:215
  46.0 203.5 %reduce-scatter.4.cloned.1.call-start = ((), (), s32[]{:S(2)}) async-start(), calls=%async_computation.8 | async-start | bytes 3342336
  170.8 0.7 copy-start.12
  170.8 1.9 copy-start.6
  170.8 2.5 copy-start.7
  170.8 198.9 %all-gather.12.cloned.1.call-start = ((), (), s32[]{:S(2)}) async-start(), calls=%async_computation.5 | async-start | bytes 17825792 | tf_op jit(solution)/shard_map/all_gather | solution.py:10
  172.6 1.4 copy-start.10
  174.0 3.1 copy-start.5
  175.2 8.7 %copy-start.8 = (f32[32,128]{1,0:T(8,128)}, f32[32,128]{1,0:T(8,128)S(1)}, u32[]{:S(2)}) copy-start(f32[32,128]{1,0:T(8,128)S(1)} %get-tuple-element.309) | copy-start | bytes 49156
  177.1 311.0 %all-gather.10.cloned.1.call-start = ((), (), s32[]{:S(2)}) async-start(), calls=%async_computation.4 | async-start | bytes 17825792 | tf_op jit(solution)/shard_map/all_gather | solution.py:10
  178.6 3.8 copy-start.4
  180.6 1.8 copy-start.3
  180.6 1.8 copy-start.11
  180.6 2.0 copy-start.13
  251.3 19.7 %all-to-all-start.2 = ((bf16[16,2,3072]{2,1,0:T(2,128)(2,1)}), bf16[16,2,3072]{2,1,0:T(2,128)(2,1)S(1)}, u32[]{:S(2)}, u32[]{:S(2)}) async-start(bf16[16,2,3072]{2,1,0:T(2,128)(2,1)} %copy.116), calls=%async_computation.2 | async-start | bytes 393216 | tf_op jit(solution)/shard_map/all_to_all | solution.py:230
  488.1 67.0 %copy-start.9 = (f32[32,128]{1,0:T(8,128)S(1)}, f32[32,128]{1,0:T(8,128)}, u32[]{:S(2)}) copy-start(f32[32,128]{1,0:T(8,128)} %copy-done.8) | copy-start | bytes 49156
  555.1 6.1 %copy-start.1 = (bf16[1,288,3072]{2,1,0:T(8,128)(2,1)S(1)}, bf16[1,288,3072]{2,1,0:T(8,128)(2,1)}, u32[]{:S(2)}) copy-start(bf16[1,288,3072]{2,1,0:T(8,128)(2,1)} %param.28) | copy-start | bytes 5308420
Sparse Core Ops, SparseCore 0:
  33.0 49.3 all-gather.15
  84.8 51.9 all-gather.13
  170.9 78.5 reduce-scatter.3
  252.3 117.2 all-gather.11
  372.0 116.0 all-gather.9
where the time goes:
time: 570 us; the launch traced here: 568 us
  waiting for transfers between devices  265 us (46%)
  other arithmetic  117 us (21%)
  blocking collectives  64.4 us (11%)
  matrix products  50.2 us (9%)
  local copies, waits for them, and re-layouts  45.2 us (8%)
  between operations  14.8 us (3%)
  starting transfers between devices  9.8 us (2%)
    all_gather x2, waiting for transfers between devices, prefix(): lax.all_gather(part.astype(kind), axis)  156 us
    select_n x32, other arithmetic, lap(): return jax.tree.map(lambda a, b: jnp.where(reached, a, b), new, before)  91.6 us
    all_gather x1, waiting for transfers between devices, per_device(): lax.all_gather(arrived_grad[None], 'ctx', axis=0, tiled=True)  43.3 us
    all_gather x1, waiting for transfers between devices, per_device(): lax.all_gather(arrived_in[None], 'ctx', axis=0, tiled=True)  36.3 us
    unnamed x1, blocking collectives  31.2 us
    unnamed x6, waiting for transfers between devices  23.7 us
    convert_element_type x32, other arithmetic, lap(): part[at].astype(own.dtype)  21.7 us
    all_to_all x1, blocking collectives, per_device(): lax.all_to_all(slot_in, 'exp', split_axis=0, concat_axis=0, tiled=True)  20.2 us
  transfers between devices with their start and end apart: 6, of which 6 were waited for; matrix products, arithmetic and copies ran while one was open for 18% of the time, Pallas kernels for 0%

commit v1 on v0

v1 whole, which is shorter than its diff:
```python
import functools

import jax
import jax.numpy as jnp
from jax import lax
from jax.experimental import pallas as pl
from jax.experimental.pallas import tpu as pltpu
from jax.sharding import PartitionSpec as P

F32 = jnp.float32
BF16 = jnp.bfloat16
NT = (((1,), (1,)), ((), ()))
TN = (((0,), (0,)), ((), ()))
HEADS_STEP = 8
DECAY_ROWS = 16


def dot(a, b, dims=(((1,), (0,)), ((), ()))):
    return lax.dot_general(a, b, dims, preferred_element_type=F32)


def exact_dot(a, b, dims=(((1,), (0,)), ((), ()))):
    return lax.dot_general(
        a, b, dims, precision=lax.Precision.HIGHEST, preferred_element_type=F32
    )


def segments(lengths_ref, place_ref, length, axis):
    shape = (length, 1) if axis == 0 else (1, length)
    base = place_ref[0] * length
    at = lax.broadcasted_iota(jnp.int32, shape, axis) + base
    count = jnp.zeros(shape, jnp.int32)
    start = jnp.int32(0)
    for doc in range(lengths_ref.shape[1]):
        inside = jnp.where(start >= base, 1, 0)
        count = count + jnp.where(at >= start, inside, 0)
        start = start + lengths_ref[0, doc]
    last = jnp.int32(0)
    start = jnp.int32(0)
    for doc in range(lengths_ref.shape[1]):
        last = last + jnp.where((start >= base) & (start < base + length), 1, 0)
        start = start + lengths_ref[0, doc]
    return count, last


def running_sums(log_ref, length):
    logs = log_ref[...]
    low = lax.broadcasted_iota(jnp.int32, (length, length), 0)
    high = lax.broadcasted_iota(jnp.int32, (length, length), 1)
    upper = jnp.where(low <= high, 1.0, 0.0).astype(F32)
    rows = exact_dot(logs, upper)
    return rows, rows.T


def local_kernel(lengths_ref, place_ref, log_ref, q_ref, k_ref, v_ref, g_ref, out_ref):
    length = q_ref.shape[0]
    size = q_ref.shape[1] // HEADS_STEP
    seg, last = segments(lengths_ref, place_ref, length, 0)
    rows, cols = running_sums(log_ref, length)
    first_doc = jnp.where(seg == 0, 1.0, 0.0).astype(F32)
    last_doc = jnp.where(seg == last, 1.0, 0.0).astype(F32)
    whole = jnp.where(last == 0, 1.0, 0.0).astype(F32)
    row_id = lax.broadcasted_iota(jnp.int32, (DECAY_ROWS, size), 0)
    for pair in range(HEADS_STEP // 2):
        pieces = jnp.zeros((DECAY_ROWS, size), F32)
        for own in range(2):
            head = 2 * pair + own
            at = slice(head * size, (head + 1) * size)
            col = cols[:, head : head + 1]
            end = cols[length - 1 : length, head : head + 1]
            from_start = jnp.exp(col) * first_doc
            to_end = jnp.exp(end - col) * last_doc
            keys_end = (k_ref[:, at].astype(F32) * to_end).astype(BF16)
            queries_start = (q_ref[:, at].astype(F32) * from_start).astype(BF16)
            out_ref[pair, own * size : (own + 1) * size, :] = dot(
                keys_end, v_ref[:, at], TN
            ).astype(BF16)
            out_ref[pair, (2 + own) * size : (3 + own) * size, :] = dot(
                queries_start, g_ref[:, at], TN
            ).astype(BF16)
            rest = jnp.broadcast_to(jnp.exp(end) * whole, (DECAY_ROWS, size))
            for part in range(3):
                piece = rest.astype(BF16).astype(F32)
                pieces = jnp.where(row_id == own * 8 + part, piece, pieces)
                rest = rest - piece
        out_ref[pair, 4 * size :, :] = pieces.astype(BF16)


def scan_kernel(in_ref, out_ref):
    blocks = in_ref.shape[0]
    size = in_ref.shape[2]

    def decay(block, own):
        rows = in_ref[block, 4 * size :, :].astype(F32)
        at = own * 8
        return rows[at : at + 1] + rows[at + 1 : at + 2] + rows[at + 2 : at + 3]

    for own in range(2):
        for kind in range(2):
            at = slice((2 * kind + own) * size, (2 * kind + own + 1) * size)
            carry = jnp.zeros((size, size), F32)
            order = range(blocks) if kind == 0 else range(blocks - 1, -1, -1)
            for block in order:
                out_ref[block, at, :] = carry.astype(BF16)
                carry = decay(block, own) * carry + in_ref[block, at, :].astype(F32)


def grads_kernel(
    lengths_ref, place_ref, log_ref, q_ref, k_ref, v_ref, g_ref, s_ref, dq_ref, dk_ref, dv_ref
):
    length = q_ref.shape[0]
    size = q_ref.shape[1] // HEADS_STEP
    seg, last = segments(lengths_ref, place_ref, length, 0)
    seg_row, _ = segments(lengths_ref, place_ref, length, 1)
    rows, cols = running_sums(log_ref, length)
    first_doc = jnp.where(seg == 0, 1.0, 0.0).astype(F32)
    last_doc = jnp.where(seg == last, 1.0, 0.0).astype(F32)
    low = lax.broadcasted_iota(jnp.int32, (length, length), 0)
    high = lax.broadcasted_iota(jnp.int32, (length, length), 1)
    linked = (low >= high) & (seg == seg_row)
    for head in range(HEADS_STEP):
        at = slice(head * size, (head + 1) * size)
        pair, own = head // 2, head % 2
        col = cols[:, head : head + 1]
        end = cols[length - 1 : length, head : head + 1]
        from_start = jnp.exp(col) * first_doc
        to_end = jnp.exp(end - col) * last_doc
        within = jnp.exp(jnp.where(linked, col - rows[head : head + 1, :], -1e9))
        q, k, v, g = q_ref[:, at], k_ref[:, at], v_ref[:, at], g_ref[:, at]
        state = s_ref[pair, own * size : (own + 1) * size, :]
        carried = s_ref[pair, (2 + own) * size : (3 + own) * size, :]
        weight_q = (dot(g, v, NT) * within).astype(BF16)
        weight_v = (dot(q, k, NT) * within).astype(BF16)
        dq_ref[:, at] = (dot(weight_q, k) + from_start * dot(g, state, NT)).astype(BF16)
        dk_ref[:, at] = (dot(weight_q, q, TN) + to_end * dot(v, carried, NT)).astype(BF16)
        dv_ref[:, at] = (dot(weight_v, g, TN) + to_end * dot(k, carried)).astype(BF16)


def slot_numbers(routes_ref):
    tokens, top = routes_ref.shape
    flat = [routes_ref[i, k] for i in range(tokens) for k in range(top)]
    slots = []
    for r, expert in enumerate(flat):
        rank = jnp.int32(0)
        for earlier in flat[:r]:
            rank = rank + jnp.where(earlier == expert, 1, 0)
        slots.append(2 * expert + rank)
    return slots


def fill_kernel(routes_ref, gates_ref, in_ref, grad_ref, out_ref):
    tokens, width = in_ref.shape
    top = routes_ref.shape[1]
    count = out_ref.shape[0]
    slots = slot_numbers(routes_ref)
    row = lax.broadcasted_iota(jnp.int32, (count, tokens), 0)
    col = lax.broadcasted_iota(jnp.int32, (count, tokens), 1)
    row_one = lax.broadcasted_iota(jnp.int32, (count, 1), 0)
    pick = jnp.zeros((count, tokens), F32)
    gate = jnp.zeros((count, 1), F32)
    for r, slot in enumerate(slots):
        pick = jnp.where((row == slot) & (col == r // top), 1.0, pick)
        gate = jnp.where(row_one == slot, gates_ref[r // top, r % top], gate)
    pick = pick.astype(BF16)
    out_ref[:, :width] = dot(pick, in_ref[...]).astype(BF16)
    out_ref[:, width:] = (gate * dot(pick, grad_ref[...])).astype(BF16)


def combine_kernel(routes_ref, rows_ref, out_ref):
    tokens, width = out_ref.shape
    top = routes_ref.shape[1]
    count = rows_ref.shape[0]
    slots = slot_numbers(routes_ref)
    row = lax.broadcasted_iota(jnp.int32, (tokens, count), 0)
    col = lax.broadcasted_iota(jnp.int32, (tokens, count), 1)
    pick = jnp.zeros((tokens, count), F32)
    for r, slot in enumerate(slots):
        pick = jnp.where((col == slot) & (row == r // top), 1.0, pick)
    out_ref[...] = dot(pick.astype(BF16), rows_ref[...]).astype(BF16)


def expert_kernel(x_ref, wg_ref, wu_ref, wd_ref, out_ref):
    width = wg_ref.shape[1]
    x = x_ref[:, :width]
    grad = x_ref[:, width:]
    gate = dot(wg_ref[...], x, NT)
    up = dot(wu_ref[...], x, NT)
    hidden = dot(wd_ref[...], grad, NT)
    sigmoid = jax.nn.sigmoid(gate)
    grad_up = (hidden * gate * sigmoid).astype(BF16)
    grad_gate = (hidden * up * sigmoid * (1.0 + gate * (1.0 - sigmoid))).astype(BF16)
    out_ref[...] = (dot(grad_gate, wg_ref[...], TN) + dot(grad_up, wu_ref[...], TN)).astype(BF16)


def sum_kernel(in_ref, out_ref):
    total = in_ref[0].astype(F32)
    for part in range(1, in_ref.shape[0]):
        total = total + in_ref[part].astype(F32)
    out_ref[...] = total.astype(BF16)


SMEM = pl.BlockSpec(memory_space=pltpu.SMEM)
VMEM = pl.BlockSpec(memory_space=pltpu.VMEM)


def params(mib):
    return pltpu.CompilerParams(vmem_limit_bytes=mib << 20)


def cost(flops, moved):
    return pl.CostEstimate(flops=int(flops), bytes_accessed=int(moved), transcendentals=0)


def per_device(
    queries, keys, values, out_grad, log_decay, doc_lengths, moe_input, moe_grad,
    routes, gate_weights, w_gate, w_up, w_down,
):
    length, width_all = queries.shape[1:]
    heads = log_decay.shape[1]
    size = width_all // heads
    blocks = lax.axis_size("ctx")
    experts = lax.axis_size("exp")
    tokens, width = moe_input.shape
    slots = 2 * experts
    place = lax.axis_index("ctx").astype(jnp.int32).reshape(1)
    q, k, v, g = queries[0], keys[0], values[0], out_grad[0]
    logs = log_decay[0]

    filled = pl.pallas_call(
        fill_kernel,
        out_shape=jax.ShapeDtypeStruct((slots, 2 * width), BF16),
        in_specs=[SMEM, SMEM, VMEM, VMEM],
        out_specs=VMEM,
        compiler_params=params(16),
        cost_estimate=cost(4 * slots * tokens * width, 8 * slots * width),
        name="fill",
    )(routes, gate_weights, moe_input, moe_grad)
    arrived = lax.all_to_all(
        filled.reshape(experts, 2, 2 * width), "exp", split_axis=0, concat_axis=0, tiled=True
    ).reshape(slots, 2 * width)
    gathered = lax.all_gather(arrived, "ctx", axis=0, tiled=True)

    steps = heads // HEADS_STEP
    cols = HEADS_STEP * size
    pairs = HEADS_STEP // 2
    position_spec = pl.BlockSpec((length, cols), lambda i: (0, i))
    log_spec = pl.BlockSpec((HEADS_STEP, length), lambda i: (i, 0))
    sent_rows = 4 * size + DECAY_ROWS
    local = pl.pallas_call(
        local_kernel,
        grid=(steps,),
        out_shape=jax.ShapeDtypeStruct((heads // 2, sent_rows, size), BF16),
        in_specs=[SMEM, SMEM, log_spec] + [position_spec] * 4,
        out_specs=pl.BlockSpec((pairs, sent_rows, size), lambda i: (i, 0, 0)),
        compiler_params=params(24),
        cost_estimate=cost(4 * heads * length * size * size, 12 * length * width_all),
        name="local_sums",
    )(doc_lengths, place, logs, q, k, v, g)
    own_heads = lax.all_to_all(local, "ctx", split_axis=0, concat_axis=0, tiled=True)
    scanned = pl.pallas_call(
        scan_kernel,
        out_shape=jax.ShapeDtypeStruct((blocks, 4 * size, size), BF16),
        in_specs=[VMEM],
        out_specs=VMEM,
        compiler_params=params(24),
        cost_estimate=cost(blocks * 8 * size * size, 16 * blocks * size * size),
        name="scan",
    )(own_heads)
    states = lax.all_to_all(scanned, "ctx", split_axis=0, concat_axis=0, tiled=True)

    hidden = w_gate.shape[1]
    rows = blocks * slots
    row_step = rows // 2
    weight_spec = pl.BlockSpec((hidden, width), lambda i: (0, 0))
    term = pl.pallas_call(
        expert_kernel,
        grid=(rows // row_step,),
        out_shape=jax.ShapeDtypeStruct((rows, width), BF16),
        in_specs=[pl.BlockSpec((row_step, 2 * width), lambda i: (i, 0))] + [weight_spec] * 3,
        out_specs=pl.BlockSpec((row_step, width), lambda i: (i, 0)),
        compiler_params=params(48),
        cost_estimate=cost(10 * rows * hidden * width, 2 * width * (3 * rows + 3 * hidden)),
        name="experts",
    )(gathered, w_gate[0], w_up[0], w_down[0])
    spread = lax.all_to_all(
        term.reshape(blocks, slots, width), "ctx", split_axis=0, concat_axis=0, tiled=True
    )
    summed = pl.pallas_call(
        sum_kernel,
        out_shape=jax.ShapeDtypeStruct((slots, width), BF16),
        in_specs=[VMEM],
        out_specs=VMEM,
        compiler_params=params(24),
        cost_estimate=cost(blocks * slots * width, 2 * (blocks + 1) * slots * width),
        name="sum_slices",
    )(spread)
    returned = lax.all_to_all(
        summed.reshape(experts, 2, width), "exp", split_axis=0, concat_axis=0, tiled=True
    ).reshape(slots, width)
    d_moe = pl.pallas_call(
        combine_kernel,
        out_shape=jax.ShapeDtypeStruct((tokens, width), BF16),
        in_specs=[SMEM, VMEM],
        out_specs=VMEM,
        compiler_params=params(16),
        cost_estimate=cost(2 * slots * tokens * width, 4 * slots * width),
        name="combine",
    )(routes, returned)

    grad_q, grad_k, grad_v = pl.pallas_call(
        grads_kernel,
        grid=(steps,),
        out_shape=[jax.ShapeDtypeStruct((length, width_all), BF16)] * 3,
        in_specs=[SMEM, SMEM, log_spec]
        + [position_spec] * 4
        + [pl.BlockSpec((pairs, 4 * size, size), lambda i: (i, 0, 0))],
        out_specs=[position_spec] * 3,
        compiler_params=params(32),
        cost_estimate=cost(16 * heads * length * size * size, 18 * length * width_all),
        name="attention_grads",
    )(doc_lengths, place, logs, q, k, v, g, states)
    return (grad_q[None], grad_k[None], grad_v[None], d_moe)


def solution(mesh):
    rows = P("exp", "ctx", None)
    tokens = P(("ctx", "exp"), None)
    return jax.shard_map(
        per_device,
        mesh=mesh,
        in_specs=(rows, rows, rows, rows, P("exp", None, "ctx"), P("exp", None))
        + (tokens,) * 4
        + (rows,) * 3,
        out_specs=(rows, rows, rows, tokens),
        check_vma=False,
    )
```

time: 570 us -> 263 us (0.46)
  waiting for transfers between devices: 265 us -> 138 us
  other arithmetic: 117 us -> 0 us
  matrix products: 50.2 us -> 0 us
  blocking collectives: 64.4 us -> 24.5 us
  Pallas kernels: 0 us -> 32.7 us
  local copies, waits for them, and re-layouts: 45.2 us -> 25.4 us
  starting transfers between devices: 9.8 us -> 27.2 us
    all_gather x4 -> x1, waiting for transfers between devices: 236 us -> 68.4 us  [per_device(): gathered = lax.all_gather(arrived, 'ctx', axis=0, tiled=True)]
    select_n x35 -> x0, other arithmetic: 92.1 us -> none  [the longest x32 91.6 us: lap(): return jax.tree.map(lambda a, b: jnp.where(reached, a, b), new, before)]
    all_to_all x1 -> x4, waiting for transfers between devices: 5.92 us -> 69.6 us  [the longest x1 43.2 us: per_device(): lax.all_to_all(term.reshape(blocks, slots, width), 'ctx', split_axis=0, c...]
    dot_general x12 -> x0, matrix products: 50.2 us -> none  [the longest x1 8.04 us: expert_grads(): jnp.dot(grad_gate, gate_slab, preferred_element_type=jnp.float32)]
    pallas_call x0 -> x7, Pallas kernels: none -> 32.7 us  [the longest x1 12.9 us: per_device(): pl.pallas_call(expert_kernel, grid=(rows // row_step,), out_shape=jax.Sha...]
    unnamed x1 -> x0, blocking collectives: 31.2 us -> none
    unnamed x6 -> x1, waiting for transfers between devices: 23.7 us -> 0.02 us
    convert_element_type x36 -> x0, other arithmetic: 22.5 us -> none  [the longest x32 21.7 us: lap(): part[at].astype(own.dtype)]
  transfers between devices with their start and end apart: 6 -> 5, of which waited for: 6 -> 3; matrix products, arithmetic and copies ran while one was open for 18% -> 0% of each run, Pallas kernels for 0% -> 11%
where the time goes in v1:
time: 263 us; the launch traced here: 262 us
  waiting for transfers between devices  138 us (52%)
  Pallas kernels  32.7 us (12%)
  starting transfers between devices  27.2 us (10%)
  local copies, waits for them, and re-layouts  25.4 us (10%)
  blocking collectives  24.5 us (9%)
  between operations  14.2 us (5%)
    all_gather x1, waiting for transfers between devices, per_device(): gathered = lax.all_gather(arrived, 'ctx', axis=0, tiled=True)  68.4 us
    all_to_all x1, waiting for transfers between devices, per_device(): lax.all_to_all(term.reshape(blocks, slots, width), 'ctx', split_axis=0, c...  43.2 us
    all_to_all x1, waiting for transfers between devices, per_device(): lax.all_to_all(scanned, 'ctx', split_axis=0, concat_axis=0, tiled=True)  26.4 us
    all_to_all x1, blocking collectives, per_device(): lax.all_to_all(filled.reshape(experts, 2, 2 * width), 'exp', split_axis=0...  24.5 us
    unnamed x48, local copies, waits for them, and re-layouts  22.7 us
    pallas_call x1, Pallas kernels, per_device(): pl.pallas_call(expert_kernel, grid=(rows // row_step,), out_shape=jax.Sha...  12.9 us
    pallas_call x1, Pallas kernels, per_device(): pl.pallas_call(grads_kernel, grid=(steps,), out_shape=[jax.ShapeDtypeStru...  11.4 us
    all_to_all x1, starting transfers between devices, per_device(): lax.all_to_all(summed.reshape(experts, 2, width), 'exp', split_axis=0, co...  11 us
  transfers between devices with their start and end apart: 5, of which 3 were waited for; matrix products, arithmetic and copies ran while one was open for 0% of the time, Pallas kernels for 11%

profile of v1, /device:TPU:1, one launch (start us, length us, event | category | flops | bytes accessed | tf_op | source)
XLA Modules:
  0.0 262.1 jit_solution(40846106482591457)
XLA Ops:
  7.3 1.5 copy.19.routes_ref
  8.8 1.3 copy.18.gates_ref
  10.1 0.8 copy-done.13
  10.9 0.8 copy-done.14
  13.1 1.0 fill.1
  14.1 1.0 reshape.27
  15.1 24.5 %all_to_all.25 = bf16[16,2,6144]{2,1,0:T(2,128)(2,1)S(1)} all-to-all(bf16[16,2,6144]{2,1,0:T(2,128)(2,1)} %reshape.27), channel_id=1, replica_groups=mesh['ctx'=16,'exp'=16] {'exp'}, dimensions={0} | all-to-all | bytes 786432 | tf_op jit(solution)/shard_map/all_to_all | solution.py:238
  39.6 0.9 reshape.28
  40.6 1.2 copy-done.10
  42.5 4.9 %local_sums.1 = bf16[16,528,128]{2,1,0:T(8,128)(2,1)S(1)} custom-call(s32[1,4]{1,0:T(1,128)S(1)} %copy-done.18, s32[1]{0:T(128)} %bitcast.place_ref, f32[32,128]{1,0:T(8,128)S(1)} %bitcast.21, bf16[128,4096]{1,0:T(8,128)(2,1)S(1)} %bitcast.13, bf16[128,4096]{1,0:T(8,128)(2,1)S(1)} %bitcast.15, bf16[128,4096]{1,0:T(8,128)(2,1)S(1)} %bitcast.17, ...), custom_call_target="tpu_custom_call" | custom-call | flops 268435456 | bytes 6291456 | tf_op jit(solution)/shard_map/local_sums/pallas_call | solution.py:249
  47.4 1.3 copy-done.2
  48.7 6.8 %all-to-all-start = ((bf16[16,528,128]{2,1,0:T(8,128)(2,1)}), bf16[16,528,128]{2,1,0:T(8,128)(2,1)S(1)}, u32[]{:S(2)}, u32[]{:S(2)}) async-start(bf16[16,528,128]{2,1,0:T(8,128)(2,1)} %copy-done.2), calls=%async_computation | async-start | bytes 4325376 | tf_op jit(solution)/shard_map/all_to_all | solution.py:259
  55.5 68.4 %all-gather.2.cloned.1.call-done.x_ref = bf16[512,6144]{1,0:T(8,128)(2,1)} async-done(((bf16[32,6144]{1,0:T(8,128)(2,1)}), bf16[512,6144]{1,0:T(8,128)(2,1)}) %all-gather.2.cloned.1.call-update) | async-done | bytes 6291472 | tf_op jit(solution)/shard_map/all_gather | solution.py:241
  123.9 1.5 copy-done.20
  125.4 1.5 copy-done.21
  126.8 1.5 copy-done.22
  128.3 12.9 %experts.1 = bf16[512,3072]{1,0:T(8,128)(2,1)} custom-call(bf16[512,6144]{1,0:T(8,128)(2,1)} %all-gather.2.cloned.1.call-done.x_ref, bf16[288,3072]{1,0:T(8,128)(2,1)S(1)} %bitcast.23, bf16[288,3072]{1,0:T(8,128)(2,1)S(1)} %bitcast.24, bf16[288,3072]{1,0:T(8,128)(2,1)S(1)} %bitcast.25), custom_call_target="tpu_custom_call" | custom-call | flops 4529848320 | bytes 14745600 | tf_op jit(solution)/shard_map/experts/pallas_call | solution.py:275
  141.3 1.4 copy-done
  142.6 5.0 %all-to-all-start.3 = ((bf16[16,32,3072]{2,1,0:T(8,128)(2,1)}), bf16[16,32,3072]{2,1,0:T(8,128)(2,1)S(1)}, u32[]{:S(2)}, u32[]{:S(2)}) async-start(bf16[16,32,3072]{2,1,0:T(8,128)(2,1)} %bitcast.26), calls=%async_computation.3 | async-start | bytes 6291456 | tf_op jit(solution)/shard_map/all_to_all | solution.py:285
  147.6 1.6 copy-done.1
  149.7 1.3 copy-done.3
  151.1 43.2 %all-to-all-done.3.in_ref = bf16[16,32,3072]{2,1,0:T(8,128)(2,1)S(1)} async-done(((bf16[16,32,3072]{2,1,0:T(8,128)(2,1)}), bf16[16,32,3072]{2,1,0:T(8,128)(2,1)S(1)}, u32[]{:S(2)}, u32[]{:S(2)}) %all-to-all-start.3) | async-done | bytes 3145760 | tf_op jit(solution)/shard_map/all_to_all | solution.py:285
  194.2 4.4 %all-to-all-start.1 = ((bf16[16,512,128]{2,1,0:T(8,128)(2,1)}), bf16[16,512,128]{2,1,0:T(8,128)(2,1)}, u32[]{:S(2)}, u32[]{:S(2)}) async-start(bf16[16,512,128]{2,1,0:T(8,128)(2,1)} %copy-done.3), calls=%async_computation.1 | async-start | bytes 4194304 | tf_op jit(solution)/shard_map/all_to_all | solution.py:269
  199.1 0.7 reshape.30
  199.9 26.4 %all-to-all-done.1.s_ref = bf16[16,512,128]{2,1,0:T(8,128)(2,1)} async-done(((bf16[16,512,128]{2,1,0:T(8,128)(2,1)}), bf16[16,512,128]{2,1,0:T(8,128)(2,1)}, u32[]{:S(2)}, u32[]{:S(2)}) %all-to-all-start.1) | async-done | bytes 2097184 | tf_op jit(solution)/shard_map/all_to_all | solution.py:269
  226.3 11.0 %all-to-all-start.4 = ((bf16[16,2,3072]{2,1,0:T(2,128)(2,1)}), bf16[16,2,3072]{2,1,0:T(2,128)(2,1)S(1)}, u32[]{:S(2)}, u32[]{:S(2)}) async-start(bf16[16,2,3072]{2,1,0:T(2,128)(2,1)} %reshape.30), calls=%async_computation.4 | async-start | bytes 393216 | tf_op jit(solution)/shard_map/all_to_all | solution.py:297
  237.3 1.2 copy-done.5
  238.6 1.2 copy-done.7
  239.8 1.2 copy-done.9
  241.0 1.2 copy-done.11
  242.2 11.4 %attention_grads.1 = (bf16[128,4096]{1,0:T(8,128)(2,1)}, bf16[128,4096]{1,0:T(8,128)(2,1)}, bf16[128,4096]{1,0:T(8,128)(2,1)}) custom-call(s32[1,4]{1,0:T(1,128)S(1)} %copy-done.19, s32[1]{0:T(128)} %bitcast.place_ref, f32[32,128]{1,0:T(8,128)S(1)} %bitcast.22, bf16[128,4096]{1,0:T(8,128)(2,1)S(1)} %bitcast.14, bf16[128,4096]{1,0:T(8,128)(2,1)S(1)} %bitcast.16, ...), custom_call_target="tpu_custom_call" | custom-call | flops 1073741824 | bytes 9437184 | tf_op jit(solution)/shard_map/attention_grads/pallas_call | solution.py:310
  253.7 1.5 combine.1
  (39 shorter events, 3.1 us)
Async XLA Ops:
  7.2 33.4 %copy-start.12 = (f32[1,32,128]{2,1,0:T(8,128)S(1)}, f32[1,32,128]{2,1,0:T(8,128)}, u32[]{:S(2)}) copy-start(f32[1,32,128]{2,1,0:T(8,128)} %param.17) | copy-start | bytes 49156
  7.2 33.4 %copy-start.8 = (bf16[1,128,4096]{2,1,0:T(8,128)(2,1)S(1)}, bf16[1,128,4096]{2,1,0:T(8,128)(2,1)}, u32[]{:S(2)}) copy-start(bf16[1,128,4096]{2,1,0:T(8,128)(2,1)} %param.15) | copy-start | bytes 3145732
  7.2 33.4 %copy-start.6 = (bf16[1,128,4096]{2,1,0:T(8,128)(2,1)S(1)}, bf16[1,128,4096]{2,1,0:T(8,128)(2,1)}, u32[]{:S(2)}) copy-start(bf16[1,128,4096]{2,1,0:T(8,128)(2,1)} %param.14) | copy-start | bytes 3145732
  7.2 33.4 %copy-start.4 = (bf16[1,128,4096]{2,1,0:T(8,128)(2,1)S(1)}, bf16[1,128,4096]{2,1,0:T(8,128)(2,1)}, u32[]{:S(2)}) copy-start(bf16[1,128,4096]{2,1,0:T(8,128)(2,1)} %param.13) | copy-start | bytes 3145732
  7.2 116.7 %all-gather.2.cloned.1.call-start = ((), (), s32[]{:S(2)}) async-start(), calls=%async_computation.5 | async-start | bytes 6684672 | tf_op jit(solution)/shard_map/all_gather | solution.py:241
  10.1 0.8 copy-start.13
  10.9 0.8 copy-start.14
  11.7 0.7 copy-start.15
  12.4 0.7 copy-start.17
  40.6 1.2 copy-start.10
  41.8 0.7 copy-start.18
  47.4 1.3 copy-start.2
  48.7 92.5 %all-to-all-start = ((bf16[16,528,128]{2,1,0:T(8,128)(2,1)}), bf16[16,528,128]{2,1,0:T(8,128)(2,1)S(1)}, u32[]{:S(2)}, u32[]{:S(2)}) async-start(bf16[16,528,128]{2,1,0:T(8,128)(2,1)} %copy-done.2), calls=%async_computation | async-start | bytes 4325376 | tf_op jit(solution)/shard_map/all_to_all | solution.py:259
  123.9 1.5 copy-start.20
  125.4 1.5 copy-start.21
  126.8 1.5 copy-start.22
  141.3 1.4 copy-start
  142.6 51.6 %all-to-all-start.3 = ((bf16[16,32,3072]{2,1,0:T(8,128)(2,1)}), bf16[16,32,3072]{2,1,0:T(8,128)(2,1)S(1)}, u32[]{:S(2)}, u32[]{:S(2)}) async-start(bf16[16,32,3072]{2,1,0:T(8,128)(2,1)} %bitcast.26), calls=%async_computation.3 | async-start | bytes 6291456 | tf_op jit(solution)/shard_map/all_to_all | solution.py:285
  147.6 1.6 copy-start.1
  149.7 1.3 copy-start.3
  194.2 32.0 %all-to-all-start.1 = ((bf16[16,512,128]{2,1,0:T(8,128)(2,1)}), bf16[16,512,128]{2,1,0:T(8,128)(2,1)}, u32[]{:S(2)}, u32[]{:S(2)}) async-start(bf16[16,512,128]{2,1,0:T(8,128)(2,1)} %copy-done.3), calls=%async_computation.1 | async-start | bytes 4194304 | tf_op jit(solution)/shard_map/all_to_all | solution.py:269
  198.7 38.7 %copy-start.19 = (s32[1,4]{1,0:T(1,128)S(1)}, s32[1,4]{1,0:T(1,128)}, u32[]{:S(2)}) copy-start(s32[1,4]{1,0:T(1,128)} %lengths_ref.3) | copy-start | bytes 52
  226.3 27.3 %all-to-all-start.4 = ((bf16[16,2,3072]{2,1,0:T(2,128)(2,1)}), bf16[16,2,3072]{2,1,0:T(2,128)(2,1)S(1)}, u32[]{:S(2)}, u32[]{:S(2)}) async-start(bf16[16,2,3072]{2,1,0:T(2,128)(2,1)} %reshape.30), calls=%async_computation.4 | async-start | bytes 393216 | tf_op jit(solution)/shard_map/all_to_all | solution.py:297
  237.3 1.2 copy-start.5
  238.6 1.2 copy-start.7
  239.8 1.2 copy-start.9
  241.0 1.2 copy-start.11
  242.2 11.5 %copy-start.16 = (s32[8,2]{1,0:T(8,128)S(1)}, s32[8,2]{1,0:T(8,128)}, u32[]{:S(2)}) copy-start(s32[8,2]{1,0:T(8,128)} %copy.19.routes_ref) | copy-start | bytes 196
Sparse Core Ops, SparseCore 0:
  40.7 83.1 all-gather.1

commit v2 on v1

--- a/solution.py
+++ b/solution.py
@@ -13,6 +13,10 @@
 TN = (((0,), (0,)), ((), ()))
 HEADS_STEP = 8
 DECAY_ROWS = 16
+VMEM_MIB = 60
+SIDE = 4
+HALF = 16
+NEAR = (0, -1, 1, 2)
 
 
 def dot(a, b, dims=(((1,), (0,)), ((), ()))):
@@ -86,23 +90,25 @@
         out_ref[pair, 4 * size :, :] = pieces.astype(BF16)
 
 
-def scan_kernel(in_ref, out_ref):
-    blocks = in_ref.shape[0]
-    size = in_ref.shape[2]
-
-    def decay(block, own):
-        rows = in_ref[block, 4 * size :, :].astype(F32)
-        at = own * 8
-        return rows[at : at + 1] + rows[at + 1 : at + 2] + rows[at + 2 : at + 3]
+def scan_kernel(decay_ref, in_ref, out_ref):
+    blocks, size = in_ref.shape[:2]
+    step = pl.program_id(0)
+
+    def run(own, order):
+        carry = jnp.zeros((size, size), F32)
+        for block in order:
+            out_ref[block] = carry.astype(BF16)
+            rows = decay_ref[block].astype(F32)[own * 8 : own * 8 + 3]
+            decay = rows[0:1] + rows[1:2] + rows[2:3]
+            carry = decay * carry + in_ref[block].astype(F32)
 
     for own in range(2):
         for kind in range(2):
-            at = slice((2 * kind + own) * size, (2 * kind + own + 1) * size)
-            carry = jnp.zeros((size, size), F32)
             order = range(blocks) if kind == 0 else range(blocks - 1, -1, -1)
-            for block in order:
-                out_ref[block, at, :] = carry.astype(BF16)
-                carry = decay(block, own) * carry + in_ref[block, at, :].astype(F32)
+
+            @pl.when(step == 2 * kind + own)
+            def _(own=own, order=order):
+                run(own, order)
 
 
 def grads_kernel(
@@ -137,8 +143,8 @@
 
 
 def slot_numbers(routes_ref):
-    tokens, top = routes_ref.shape
-    flat = [routes_ref[i, k] for i in range(tokens) for k in range(top)]
+    top, tokens = routes_ref.shape
+    flat = [routes_ref[k, i] for i in range(tokens) for k in range(top)]
     slots = []
     for r, expert in enumerate(flat):
         rank = jnp.int32(0)
@@ -150,8 +156,8 @@
 
 def fill_kernel(routes_ref, gates_ref, in_ref, grad_ref, out_ref):
     tokens, width = in_ref.shape
-    top = routes_ref.shape[1]
-    count = out_ref.shape[0]
+    top = routes_ref.shape[0]
+    count = 2 * out_ref.shape[0]
     slots = slot_numbers(routes_ref)
     row = lax.broadcasted_iota(jnp.int32, (count, tokens), 0)
     col = lax.broadcasted_iota(jnp.int32, (count, tokens), 1)
@@ -160,15 +166,19 @@
     gate = jnp.zeros((count, 1), F32)
     for r, slot in enumerate(slots):
         pick = jnp.where((row == slot) & (col == r // top), 1.0, pick)
-        gate = jnp.where(row_one == slot, gates_ref[r // top, r % top], gate)
+        gate = jnp.where(row_one == slot, gates_ref[r % top, r // top], gate)
     pick = pick.astype(BF16)
-    out_ref[:, :width] = dot(pick, in_ref[...]).astype(BF16)
-    out_ref[:, width:] = (gate * dot(pick, grad_ref[...])).astype(BF16)
+    rows = dot(pick, in_ref[...]).astype(BF16)
+    grads = (gate * dot(pick, grad_ref[...])).astype(BF16)
+    for expert in range(out_ref.shape[0]):
+        own = slice(2 * expert, 2 * expert + 2)
+        out_ref[expert, :, :width] = rows[own]
+        out_ref[expert, :, width:] = grads[own]
 
 
 def combine_kernel(routes_ref, rows_ref, out_ref):
     tokens, width = out_ref.shape
-    top = routes_ref.shape[1]
+    top = routes_ref.shape[0]
     count = rows_ref.shape[0]
     slots = slot_numbers(routes_ref)
     row = lax.broadcasted_iota(jnp.int32, (tokens, count), 0)
@@ -179,24 +189,147 @@
     out_ref[...] = dot(pick.astype(BF16), rows_ref[...]).astype(BF16)
 
 
-def expert_kernel(x_ref, wg_ref, wu_ref, wd_ref, out_ref):
+def expert_kernel(count, *refs):
+    buffers, weights = refs[:count], refs[count : count + 3]
+    outs = refs[count + 3 : 2 * count + 3]
+    x_ref, wg_ref, wu_ref, wd_ref, x_sem, w_sem = refs[2 * count + 3 :]
+    copies = []
+    at = 0
+    for n, buffer in enumerate(buffers):
+        rows = buffer.shape[0]
+        copies.append(pltpu.make_async_copy(buffer, x_ref.at[pl.ds(at, rows)], x_sem.at[n]))
+        at += rows
+    loads = [
+        pltpu.make_async_copy(weight, held, w_sem.at[n])
+        for n, (weight, held) in enumerate(zip(weights, (wg_ref, wu_ref, wd_ref)))
+    ]
+    for copy in copies + loads:
+        copy.start()
+    for copy in copies:
+        copy.wait()
     width = wg_ref.shape[1]
-    x = x_ref[:, :width]
-    grad = x_ref[:, width:]
-    gate = dot(wg_ref[...], x, NT)
-    up = dot(wu_ref[...], x, NT)
-    hidden = dot(wd_ref[...], grad, NT)
+    loads[0].wait()
+    gate = dot(wg_ref[...], x_ref[:, :width], NT)
     sigmoid = jax.nn.sigmoid(gate)
+    loads[1].wait()
+    up = dot(wu_ref[...], x_ref[:, :width], NT)
+    loads[2].wait()
+    hidden = dot(wd_ref[...], x_ref[:, width:], NT)
     grad_up = (hidden * gate * sigmoid).astype(BF16)
     grad_gate = (hidden * up * sigmoid * (1.0 + gate * (1.0 - sigmoid))).astype(BF16)
-    out_ref[...] = (dot(grad_gate, wg_ref[...], TN) + dot(grad_up, wu_ref[...], TN)).astype(BF16)
-
-
-def sum_kernel(in_ref, out_ref):
-    total = in_ref[0].astype(F32)
-    for part in range(1, in_ref.shape[0]):
-        total = total + in_ref[part].astype(F32)
-    out_ref[...] = total.astype(BF16)
+    term = (dot(grad_gate, wg_ref[...], TN) + dot(grad_up, wu_ref[...], TN)).astype(BF16)
+    at = 0
+    for out in outs:
+        rows = out.shape[0]
+        out[...] = term[at : at + rows]
+        at += rows
+
+
+def expert_rows(buffers, weights):
+    count = len(buffers)
+    hidden, width = weights[0].shape
+    rows = sum(buffer.shape[0] for buffer in buffers)
+    any_spec = pl.BlockSpec(memory_space=pl.ANY)
+    return pl.pallas_call(
+        functools.partial(expert_kernel, count),
+        out_shape=[jax.ShapeDtypeStruct((buffer.shape[0], width), BF16) for buffer in buffers],
+        in_specs=[any_spec] * (count + 3),
+        out_specs=[VMEM] * count,
+        scratch_shapes=[pltpu.VMEM((rows, 2 * width), BF16)]
+        + [pltpu.VMEM((hidden, width), BF16)] * 3
+        + [pltpu.SemaphoreType.DMA((count,)), pltpu.SemaphoreType.DMA((3,))],
+        compiler_params=params(VMEM_MIB),
+        cost_estimate=cost(10 * rows * hidden * width, 2 * width * (3 * rows + 3 * hidden)),
+        name="experts",
+    )(*buffers, *weights)
+
+
+def add_kernel(count, *refs):
+    parts, arrived, outs = refs[:count], refs[count : 2 * count], refs[2 * count :]
+    for n, (part, more, out) in enumerate(zip(parts, arrived, outs)):
+        cut = more.shape[0]
+        at = slice(0, cut) if n % 2 == 0 else slice(cut, 2 * cut)
+        rest = slice(cut, 2 * cut) if n % 2 == 0 else slice(0, cut)
+        out[at, :] = (part[at, :].astype(F32) + more[...].astype(F32)).astype(BF16)
+        out[rest, :] = part[rest, :]
+
+
+def add_halves(parts, arrived):
+    count = len(parts)
+    return pl.pallas_call(
+        functools.partial(add_kernel, count),
+        out_shape=[jax.ShapeDtypeStruct(part.shape, BF16) for part in parts],
+        in_specs=[VMEM] * (2 * count),
+        out_specs=[VMEM] * count,
+        compiler_params=params(VMEM_MIB),
+        cost_estimate=cost(count * parts[0].size, 6 * count * parts[0].size),
+        name="add_halves",
+    )(*parts, *arrived)
+
+
+def own_kernel(group, *refs):
+    groups = len(refs) // (group + len(NEAR))
+    ins, outs = refs[: groups * group], refs[groups * group :]
+    for n in range(groups):
+        total = ins[n * group][...].astype(F32)
+        for ref in ins[n * group + 1 : (n + 1) * group]:
+            total = total + ref[...].astype(F32)
+        total = total.astype(BF16)
+        for piece in range(len(NEAR)):
+            outs[n * len(NEAR) + piece][...] = total[piece * HALF : (piece + 1) * HALF]
+
+
+def add_own(groups):
+    group = len(groups[0])
+    width = groups[0][0].shape[1]
+    count = len(groups) * len(NEAR)
+    outs = pl.pallas_call(
+        functools.partial(own_kernel, group),
+        out_shape=[jax.ShapeDtypeStruct((HALF, width), BF16)] * count,
+        in_specs=[VMEM] * (group * len(groups)),
+        out_specs=[VMEM] * count,
+        compiler_params=params(VMEM_MIB),
+        cost_estimate=cost(count * HALF * width * group, 2 * count * HALF * width * group),
+        name="add_own",
+    )(*[ref for refs in groups for ref in refs])
+    return [list(outs[n * len(NEAR) : (n + 1) * len(NEAR)]) for n in range(len(groups))]
+
+
+def last_kernel(group, *refs):
+    out_ref = refs[-1]
+    for n in range(2):
+        ins = refs[n * group : (n + 1) * group]
+        total = ins[0][...].astype(F32)
+        for ref in ins[1:]:
+            total = total + ref[...].astype(F32)
+        total = total.astype(BF16)
+        for expert in range(HALF // 2):
+            out_ref[n * HALF // 2 + expert] = total[2 * expert : 2 * expert + 2]
+
+
+def add_last(first, second):
+    width = first[0].shape[1]
+    return pl.pallas_call(
+        functools.partial(last_kernel, len(first)),
+        out_shape=jax.ShapeDtypeStruct((HALF, 2, width), BF16),
+        in_specs=[VMEM] * (2 * len(first)),
+        out_specs=VMEM,
+        compiler_params=params(VMEM_MIB),
+        cost_estimate=cost(8 * HALF * width, 20 * HALF * width),
+        name="add_last",
+    )(*first, *second)
+
+
+def along_x(step):
+    return [(SIDE * y + x, SIDE * y + (x + step) % SIDE) for y in range(SIDE) for x in range(SIDE)]
+
+
+def along_y(step):
+    return [(SIDE * y + x, SIDE * ((y + step) % SIDE) + x) for y in range(SIDE) for x in range(SIDE)]
+
+
+def send(array, pairs):
+    return lax.ppermute(array, "ctx", pairs)
 
 
 SMEM = pl.BlockSpec(memory_space=pltpu.SMEM)
@@ -228,18 +361,18 @@
 
     filled = pl.pallas_call(
         fill_kernel,
-        out_shape=jax.ShapeDtypeStruct((slots, 2 * width), BF16),
+        out_shape=jax.ShapeDtypeStruct((experts, 2, 2 * width), BF16),
         in_specs=[SMEM, SMEM, VMEM, VMEM],
         out_specs=VMEM,
-        compiler_params=params(16),
+        compiler_params=params(VMEM_MIB),
         cost_estimate=cost(4 * slots * tokens * width, 8 * slots * width),
         name="fill",
-    )(routes, gate_weights, moe_input, moe_grad)
+    )(routes.T, gate_weights.T, moe_input, moe_grad)
     arrived = lax.all_to_all(
-        filled.reshape(experts, 2, 2 * width), "exp", split_axis=0, concat_axis=0, tiled=True
+        filled, "exp", split_axis=0, concat_axis=0, tiled=True
     ).reshape(slots, 2 * width)
-    gathered = lax.all_gather(arrived, "ctx", axis=0, tiled=True)
-
+
+    logs, filled = lax.optimization_barrier((logs, filled))
     steps = heads // HEADS_STEP
     cols = HEADS_STEP * size
     pairs = HEADS_STEP // 2
@@ -252,60 +385,76 @@
         out_shape=jax.ShapeDtypeStruct((heads // 2, sent_rows, size), BF16),
         in_specs=[SMEM, SMEM, log_spec] + [position_spec] * 4,
         out_specs=pl.BlockSpec((pairs, sent_rows, size), lambda i: (i, 0, 0)),
-        compiler_params=params(24),
+        compiler_params=params(VMEM_MIB),
         cost_estimate=cost(4 * heads * length * size * size, 12 * length * width_all),
         name="local_sums",
     )(doc_lengths, place, logs, q, k, v, g)
+    arrived, _ = lax.optimization_barrier((arrived, local))
+
+    first, second = arrived[:HALF], arrived[HALF:]
+    first_near = [first] + [send(first, along_x(-d)) for d in NEAR[1:]]
+    second_near = [second] + [send(second, along_y(-d)) for d in NEAR[1:]]
+    first_row = jnp.concatenate(first_near)
+    second_col = jnp.concatenate(second_near)
+    weights = (w_gate[0], w_up[0], w_down[0])
+    first_up, first_down = send(first_row, along_y(1)), send(first_row, along_y(-1))
+    second_left, second_right = send(second_col, along_x(1)), send(second_col, along_x(-1))
+    first_own, second_own = expert_rows([first_row, second_col], weights)
+    held = lax.optimization_barrier(
+        (first_up, first_down, second_left, second_right, first_own, second_own, local)
+    )
+    first_up, first_down, second_left, second_right, first_own, second_own, local = held
+
     own_heads = lax.all_to_all(local, "ctx", split_axis=0, concat_axis=0, tiled=True)
+    state_spec = pl.BlockSpec((blocks, size, size), lambda i: (0, i, 0))
     scanned = pl.pallas_call(
         scan_kernel,
+        grid=(4,),
         out_shape=jax.ShapeDtypeStruct((blocks, 4 * size, size), BF16),
-        in_specs=[VMEM],
-        out_specs=VMEM,
-        compiler_params=params(24),
+        in_specs=[
+            pl.BlockSpec((blocks, DECAY_ROWS, size), lambda i: (0, 4 * size // DECAY_ROWS, 0)),
+            state_spec,
+        ],
+        out_specs=state_spec,
+        compiler_params=params(VMEM_MIB),
         cost_estimate=cost(blocks * 8 * size * size, 16 * blocks * size * size),
         name="scan",
-    )(own_heads)
+    )(own_heads, own_heads)
+
+    cut = 2 * HALF
+    far = [
+        send(first_up[:cut], along_y(1)), send(first_down[cut:], along_y(-1)),
+        send(second_left[:cut], along_x(1)), send(second_right[cut:], along_x(-1)),
+    ]
+    near_terms = expert_rows([first_up, first_down, second_left, second_right], weights)
+    far_terms = expert_rows(far, weights)
+    ways = [along_y(1), along_y(-1), along_x(1), along_x(-1)]
+    arrived_far = [send(part, way) for part, way in zip(far_terms, ways)]
+    up, down, left, right = near_terms
+    *arrived_far, scanned = lax.optimization_barrier((*arrived_far, scanned))
     states = lax.all_to_all(scanned, "ctx", split_axis=0, concat_axis=0, tiled=True)
-
-    hidden = w_gate.shape[1]
-    rows = blocks * slots
-    row_step = rows // 2
-    weight_spec = pl.BlockSpec((hidden, width), lambda i: (0, 0))
-    term = pl.pallas_call(
-        expert_kernel,
-        grid=(rows // row_step,),
-        out_shape=jax.ShapeDtypeStruct((rows, width), BF16),
-        in_specs=[pl.BlockSpec((row_step, 2 * width), lambda i: (i, 0))] + [weight_spec] * 3,
-        out_specs=pl.BlockSpec((row_step, width), lambda i: (i, 0)),
-        compiler_params=params(48),
-        cost_estimate=cost(10 * rows * hidden * width, 2 * width * (3 * rows + 3 * hidden)),
-        name="experts",
-    )(gathered, w_gate[0], w_up[0], w_down[0])
-    spread = lax.all_to_all(
-        term.reshape(blocks, slots, width), "ctx", split_axis=0, concat_axis=0, tiled=True
+    halves = add_halves([down, up, right, left], arrived_far)
+    arrived_near = [send(part, way) for part, way in zip(halves, ways)]
+    first_sum, second_sum = add_own(
+        [[first_own] + arrived_near[:2], [second_own] + arrived_near[2:]]
     )
-    summed = pl.pallas_call(
-        sum_kernel,
-        out_shape=jax.ShapeDtypeStruct((slots, width), BF16),
-        in_specs=[VMEM],
-        out_specs=VMEM,
-        compiler_params=params(24),
-        cost_estimate=cost(blocks * slots * width, 2 * (blocks + 1) * slots * width),
-        name="sum_slices",
-    )(spread)
+    first_sum[0], states = lax.optimization_barrier((first_sum[0], states))
+    summed = add_last(
+        first_sum[:1] + [send(part, along_x(d)) for part, d in zip(first_sum[1:], NEAR[1:])],
+        second_sum[:1] + [send(part, along_y(d)) for part, d in zip(second_sum[1:], NEAR[1:])],
+    )
     returned = lax.all_to_all(
-        summed.reshape(experts, 2, width), "exp", split_axis=0, concat_axis=0, tiled=True
+        summed, "exp", split_axis=0, concat_axis=0, tiled=True
     ).reshape(slots, width)
     d_moe = pl.pallas_call(
         combine_kernel,
         out_shape=jax.ShapeDtypeStruct((tokens, width), BF16),
         in_specs=[SMEM, VMEM],
         out_specs=VMEM,
-        compiler_params=params(16),
+        compiler_params=params(VMEM_MIB),
         cost_estimate=cost(2 * slots * tokens * width, 4 * slots * width),
         name="combine",
-    )(routes, returned)
+    )(routes.T, returned)
 
     grad_q, grad_k, grad_v = pl.pallas_call(
         grads_kernel,
@@ -315,7 +464,7 @@
         + [position_spec] * 4
         + [pl.BlockSpec((pairs, 4 * size, size), lambda i: (i, 0, 0))],
         out_specs=[position_spec] * 3,
-        compiler_params=params(32),
+        compiler_params=params(VMEM_MIB),
         cost_estimate=cost(16 * heads * length * size * size, 18 * length * width_all),
         name="attention_grads",
     )(doc_lengths, place, logs, q, k, v, g, states)

time: 263 us -> 208 us (0.79)
  waiting for transfers between devices: 138 us -> 69.2 us
  starting transfers between devices: 27.2 us -> 67.8 us
  Pallas kernels: 32.7 us -> 59 us
  blocking collectives: 24.5 us -> 0 us
  local copies, waits for them, and re-layouts: 25.4 us -> 10.1 us
  between operations: 14.2 us -> 0.89 us
    all_gather x1 -> x0, waiting for transfers between devices: 68.4 us -> none  [per_device(): gathered = lax.all_gather(arrived, 'ctx', axis=0, tiled=True)]
    ppermute x0 -> x28, waiting for transfers between devices: none -> 61.3 us  [send(): return lax.ppermute(array, 'ctx', pairs)]
    ppermute x0 -> x28, starting transfers between devices: none -> 40.5 us  [send(): return lax.ppermute(array, 'ctx', pairs)]
    all_to_all x2, waiting for transfers between devices: 43.2 us -> 7.93 us  [the longest x1 7.93 us: per_device(): lax.all_to_all(filled, 'exp', split_axis=0, concat_axis=0, tiled=True)]
    all_to_all x1, waiting for transfers between devices: 26.4 us -> 0.01 us  [per_device(): lax.all_to_all(scanned, 'ctx', split_axis=0, concat_axis=0, tiled=True)]
    all_to_all x1 -> x0, blocking collectives: 24.5 us -> none  [per_device(): lax.all_to_all(filled.reshape(experts, 2, 2 * width), 'exp', split_axis=0...]
    pallas_call x4 -> x8, Pallas kernels: 14.9 us -> 39 us  [the longest x3 25.7 us: expert_rows(): pl.pallas_call(functools.partial(expert_kernel, count), out_shape=[jax.Sh...]
    unnamed x48, local copies, waits for them, and re-layouts: 22.7 us -> 6.07 us
  transfers between devices with their start and end apart: 5 -> 32, of which waited for: 3 -> 12; matrix products, arithmetic and copies ran while one was open for 0% -> 2% of each run, Pallas kernels for 11% -> 26%
where the time goes in v2:
time: 208 us; the launch traced here: 207 us
  waiting for transfers between devices  69.2 us (33%)
  starting transfers between devices  67.8 us (33%)
  Pallas kernels  59 us (28%)
  local copies, waits for them, and re-layouts  10.1 us (5%)
    ppermute x28, waiting for transfers between devices, send(): return lax.ppermute(array, 'ctx', pairs)  61.3 us
    ppermute x28, starting transfers between devices, send(): return lax.ppermute(array, 'ctx', pairs)  40.5 us
    pallas_call x3, Pallas kernels, expert_rows(): pl.pallas_call(functools.partial(expert_kernel, count), out_shape=[jax.Sh...  25.7 us
    pallas_call x1, Pallas kernels, per_device(): pl.pallas_call(grads_kernel, grid=(steps,), out_shape=[jax.ShapeDtypeStru...  11.5 us
    all_to_all x1, starting transfers between devices, per_device(): lax.all_to_all(filled, 'exp', split_axis=0, concat_axis=0, tiled=True)  9.98 us
    all_to_all x1, waiting for transfers between devices, per_device(): lax.all_to_all(filled, 'exp', split_axis=0, concat_axis=0, tiled=True)  7.93 us
    all_to_all x1, starting transfers between devices, per_device(): lax.all_to_all(local, 'ctx', split_axis=0, concat_axis=0, tiled=True)  7.27 us
    pallas_call x1, Pallas kernels, per_device(): pl.pallas_call(local_kernel, grid=(steps,), out_shape=jax.ShapeDtypeStruc...  6.62 us
  transfers between devices with their start and end apart: 32, of which 12 were waited for; matrix products, arithmetic and copies ran while one was open for 2% of the time, Pallas kernels for 26%

profile of v2, /device:TPU:1, one launch (start us, length us, event | category | flops | bytes accessed | tf_op | source)
XLA Modules:
  0.0 207.2 jit_solution(10911768572430291696)
XLA Ops:
  0.6 2.0 fill.1
  2.6 10.0 %all-to-all-start = ((bf16[16,2,6144]{2,1,0:T(2,128)(2,1)}), bf16[16,2,6144]{2,1,0:T(2,128)(2,1)S(1)}, u32[]{:S(2)}, u32[]{:S(2)}) async-start(bf16[16,2,6144]{2,1,0:T(2,128)(2,1)} %fill.1), calls=%async_computation | async-start | bytes 786432 | tf_op jit(solution)/shard_map/all_to_all | solution.py:371
  12.6 6.6 %local_sums.1 = bf16[16,528,128]{2,1,0:T(8,128)(2,1)} custom-call(s32[1,4]{1,0:T(1,128)} %lengths_ref.3, s32[1]{0:T(128)} %bitcast.place_ref, f32[32,128]{1,0:T(8,128)} %bitcast.31, bf16[128,4096]{1,0:T(8,128)(2,1)} %bitcast.23, bf16[128,4096]{1,0:T(8,128)(2,1)} %bitcast.25, bf16[128,4096]{1,0:T(8,128)(2,1)} %bitcast.27, bf16[128,4096]{1,0:T(8,128)(2,1)} %bitcast.29), custom_call_target="tpu_custom_call" | custom-call | flops 268435456 | bytes 6291456 | tf_op jit(solution)/shard_map/local_sums/pallas_call | solution.py:382
  19.2 7.9 %all-to-all-done = bf16[16,2,6144]{2,1,0:T(2,128)(2,1)S(1)} async-done(((bf16[16,2,6144]{2,1,0:T(2,128)(2,1)}), bf16[16,2,6144]{2,1,0:T(2,128)(2,1)S(1)}, u32[]{:S(2)}, u32[]{:S(2)}) %all-to-all-start) | async-done | bytes 393248 | tf_op jit(solution)/shard_map/all_to_all | solution.py:371
  27.3 2.8 %collective-permute-start.2 = (bf16[16,6144]{1,0:T(8,128)(2,1)S(1)}, bf16[16,6144]{1,0:T(8,128)(2,1)S(1)}, u32[]{:S(2)}, u32[]{:S(2)}) collective-permute-start(bf16[16,6144]{1,0:T(8,128)(2,1)S(1)} %get-tuple-element.87), channel_id=1, source_target_pairs={{0,32},{16,48},{32,0},{48,16},{64,96},{80,112},{96,64},{112,80},{1... | collective-permute-start | bytes 589832 | tf_op jit(solution)/shard_map/ppermute | solution.py:332
  31.6 2.9 %collective-permute-start.7 = (bf16[16,6144]{1,0:T(8,128)(2,1)S(1)}, bf16[16,6144]{1,0:T(8,128)(2,1)S(1)}, u32[]{:S(2)}, u32[]{:S(2)}) collective-permute-start(bf16[16,6144]{1,0:T(8,128)(2,1)S(1)} %get-tuple-element.86), channel_id=1, source_target_pairs={{0,128},{16,144},{32,160},{48,176},{64,192},{80,208},{96,224},{112... | collective-permute-start | bytes 589832 | tf_op jit(solution)/shard_map/ppermute | solution.py:332
  36.9 3.0 %collective-permute-done.1 = bf16[16,6144]{1,0:T(8,128)(2,1)S(1)} collective-permute-done((bf16[16,6144]{1,0:T(8,128)(2,1)S(1)}, bf16[16,6144]{1,0:T(8,128)(2,1)S(1)}, u32[]{:S(2)}, u32[]{:S(2)}) %collective-permute-start.1) | collective-permute-done | bytes 196640 | tf_op jit(solution)/shard_map/ppermute | solution.py:332
  45.2 1.8 collective-permute-start.9
  47.0 8.0 %experts.3 = (bf16[64,3072]{1,0:T(8,128)(2,1)}, bf16[64,3072]{1,0:T(8,128)(2,1)}) custom-call(bf16[64,6144]{1,0:T(8,128)(2,1)} %copy-done.2, bf16[64,6144]{1,0:T(8,128)(2,1)} %copy-done.3, bf16[288,3072]{1,0:T(8,128)(2,1)} %bitcast.14, bf16[288,3072]{1,0:T(8,128)(2,1)} %bitcast.17, bf16[288,3072]{1,0:T(8,128)(2,1)} %bitcast.20), custom_call_target="tpu_custom_call" | custom-call | flops 1132462080 | bytes 7667712 | tf_op jit(solution)/shard_map/experts/pallas_call | solution.py:233
  55.0 5.8 %collective-permute-done.3.refs_0_ = bf16[64,6144]{1,0:T(8,128)(2,1)S(1)} collective-permute-done((bf16[64,6144]{1,0:T(8,128)(2,1)S(1)}, bf16[64,6144]{1,0:T(8,128)(2,1)S(1)}, u32[]{:S(2)}, u32[]{:S(2)}) %collective-permute-start.3) | collective-permute-done | bytes 786464 | tf_op jit(solution)/shard_map/ppermute | solution.py:332
  61.1 2.2 %collective-permute-done.8.refs_2_ = bf16[64,6144]{1,0:T(8,128)(2,1)} collective-permute-done((bf16[64,6144]{1,0:T(8,128)(2,1)S(1)}, bf16[64,6144]{1,0:T(8,128)(2,1)}, u32[]{:S(2)}, u32[]{:S(2)}) %collective-permute-start.8) | collective-permute-done | bytes 786464 | tf_op jit(solution)/shard_map/ppermute | solution.py:332
  63.4 7.3 %all-to-all-start.1 = ((bf16[16,528,128]{2,1,0:T(8,128)(2,1)}), bf16[16,528,128]{2,1,0:T(8,128)(2,1)S(1)}, u32[]{:S(2)}, u32[]{:S(2)}) async-start(bf16[16,528,128]{2,1,0:T(8,128)(2,1)} %local_sums.1), calls=%async_computation.1 | async-start | bytes 4325376 | tf_op jit(solution)/shard_map/all_to_all | solution.py:408
  70.7 1.6 collective-permute-start.10
  79.6 24.8 %collective-permute-done.10.refs_0_ = bf16[32,6144]{1,0:T(8,128)(2,1)S(1)} collective-permute-done((bf16[32,6144]{1,0:T(8,128)(2,1)S(1)}, bf16[32,6144]{1,0:T(8,128)(2,1)S(1)}, u32[]{:S(2)}, u32[]{:S(2)}) %collective-permute-start.10) | collective-permute-done | bytes 393248 | tf_op jit(solution)/shard_map/ppermute | solution.py:332
  104.4 2.7 %collective-permute-done.12.refs_2_ = bf16[32,6144]{1,0:T(8,128)(2,1)S(1)} collective-permute-done((bf16[32,6144]{1,0:T(8,128)(2,1)S(1)}, bf16[32,6144]{1,0:T(8,128)(2,1)S(1)}, u32[]{:S(2)}, u32[]{:S(2)}) %collective-permute-start.12) | collective-permute-done | bytes 393248 | tf_op jit(solution)/shard_map/ppermute | solution.py:332
  108.6 8.0 %experts.5 = (bf16[32,3072]{1,0:T(8,128)(2,1)}, bf16[32,3072]{1,0:T(8,128)(2,1)}, bf16[32,3072]{1,0:T(8,128)(2,1)}, bf16[32,3072]{1,0:T(8,128)(2,1)}) custom-call(bf16[32,6144]{1,0:T(8,128)(2,1)} %copy-done.10, bf16[32,6144]{1,0:T(8,128)(2,1)} %copy-done.11, bf16[32,6144]{1,0:T(8,128)(2,1)} %copy-done.12, bf16[32,6144]{1,0:T(8,128)(2,1)} %copy-done.13, ...), custom_call_target="tpu_custom_call" | custom-call | flops 1132462080 | bytes 7667712 | tf_op jit(solution)/shard_map/experts/pallas_call | solution.py:233
  116.6 1.8 collective-permute-start.14
  119.8 2.6 %collective-permute-start.17 = (bf16[32,3072]{1,0:T(8,128)(2,1)}, bf16[32,3072]{1,0:T(8,128)(2,1)S(1)}, u32[]{:S(2)}, u32[]{:S(2)}) collective-permute-start(bf16[32,3072]{1,0:T(8,128)(2,1)} %get-tuple-element.61), channel_id=1, source_target_pairs={{0,48},{16,0},{32,16},{48,32},{64,112},{80,64},{96,80},{112,96},{1... | collective-permute-start | bytes 589832 | tf_op jit(solution)/shard_map/ppermute | solution.py:332
  123.7 4.1 %scan.1 = bf16[16,512,128]{2,1,0:T(8,128)(2,1)} custom-call(bf16[16,528,128]{2,1,0:T(8,128)(2,1)} %copy-done, bf16[16,528,128]{2,1,0:T(8,128)(2,1)} %copy-done), custom_call_target="tpu_custom_call" | custom-call | flops 2097152 | bytes 4194304 | tf_op jit(solution)/shard_map/scan/pallas_call | solution.py:410
  128.7 4.0 %all-to-all-start.2 = ((bf16[16,512,128]{2,1,0:T(8,128)(2,1)}), bf16[16,512,128]{2,1,0:T(8,128)(2,1)S(1)}, u32[]{:S(2)}, u32[]{:S(2)}) async-start(bf16[16,512,128]{2,1,0:T(8,128)(2,1)} %scan.1), calls=%async_computation.2 | async-start | bytes 4194304 | tf_op jit(solution)/shard_map/all_to_all | solution.py:435
  132.7 9.7 %experts.4 = (bf16[64,3072]{1,0:T(8,128)(2,1)}, bf16[64,3072]{1,0:T(8,128)(2,1)}, bf16[64,3072]{1,0:T(8,128)(2,1)}, bf16[64,3072]{1,0:T(8,128)(2,1)}) custom-call(bf16[64,6144]{1,0:T(8,128)(2,1)} %copy-done.4, bf16[64,6144]{1,0:T(8,128)(2,1)} %copy-done.5, bf16[64,6144]{1,0:T(8,128)(2,1)} %collective-permute-done.8.refs_2_, ...), custom_call_target="tpu_custom_call" | custom-call | flops 2264924160 | bytes 10027008 | tf_op jit(solution)/shard_map/experts/pallas_call | solution.py:233
  142.4 2.8 %add_halves.1 = (bf16[64,3072]{1,0:T(8,128)(2,1)}, bf16[64,3072]{1,0:T(8,128)(2,1)}, bf16[64,3072]{1,0:T(8,128)(2,1)}, bf16[64,3072]{1,0:T(8,128)(2,1)}) custom-call(bf16[64,3072]{1,0:T(8,128)(2,1)} %get-tuple-element.54.refs_0_, bf16[64,3072]{1,0:T(8,128)(2,1)} %get-tuple-element.55.refs_1_, bf16[64,3072]{1,0:T(8,128)(2,1)} %get-tuple-element.56.refs_2_, ...), custom_call_target="tpu_custom_call" | custom-call | flops 786432 | bytes 4718592 | tf_op jit(solution)/shard_map/add_halves/pallas_call | solution.py:259
  150.5 17.3 %collective-permute-done.18.refs_1_ = bf16[64,3072]{1,0:T(8,128)(2,1)S(1)} collective-permute-done((bf16[64,3072]{1,0:T(8,128)(2,1)}, bf16[64,3072]{1,0:T(8,128)(2,1)S(1)}, u32[]{:S(2)}, u32[]{:S(2)}) %collective-permute-start.18) | collective-permute-done | bytes 393248 | tf_op jit(solution)/shard_map/ppermute | solution.py:332
  169.6 2.5 %add_own.1 = (bf16[16,3072]{1,0:T(8,128)(2,1)}, bf16[16,3072]{1,0:T(8,128)(2,1)}, bf16[16,3072]{1,0:T(8,128)(2,1)}, bf16[16,3072]{1,0:T(8,128)(2,1)}, bf16[16,30...) custom-call(bf16[64,3072]{1,0:T(8,128)(2,1)} %get-tuple-element.49.refs_0_, ...), custom_call_target="tpu_custom_call" | custom-call | flops 1179648 | bytes 2359296 | tf_op jit(solution)/shard_map/add_own/pallas_call | solution.py:286
  172.1 2.2 %collective-permute-start.22 = (bf16[16,3072]{1,0:T(8,128)(2,1)}, bf16[16,3072]{1,0:T(8,128)(2,1)S(1)}, u32[]{:S(2)}, u32[]{:S(2)}) collective-permute-start(bf16[16,3072]{1,0:T(8,128)(2,1)} %get-tuple-element.79), channel_id=1, source_target_pairs={{0,48},{16,0},{32,16},{48,32},{64,112},{80,64},{96,80},{112,96},{1... | collective-permute-start | bytes 294920 | tf_op jit(solution)/shard_map/ppermute | solution.py:332
  174.4 2.3 %collective-permute-start.24 = (bf16[16,3072]{1,0:T(8,128)(2,1)}, bf16[16,3072]{1,0:T(8,128)(2,1)S(1)}, u32[]{:S(2)}, u32[]{:S(2)}) collective-permute-start(bf16[16,3072]{1,0:T(8,128)(2,1)} %get-tuple-element.81), channel_id=1, source_target_pairs={{0,32},{16,48},{32,0},{48,16},{64,96},{80,112},{96,64},{112,80},{1... | collective-permute-start | bytes 294920 | tf_op jit(solution)/shard_map/ppermute | solution.py:332
  178.3 2.4 %collective-permute-start.27 = (bf16[16,3072]{1,0:T(8,128)(2,1)}, bf16[16,3072]{1,0:T(8,128)(2,1)S(1)}, u32[]{:S(2)}, u32[]{:S(2)}) collective-permute-start(bf16[16,3072]{1,0:T(8,128)(2,1)} %get-tuple-element.85), channel_id=1, source_target_pairs={{0,128},{16,144},{32,160},{48,176},{64,192},{80,208},{96,224},{112... | collective-permute-start | bytes 294920 | tf_op jit(solution)/shard_map/ppermute | solution.py:332
  180.8 3.4 %collective-permute-done.26.refs_6_ = bf16[16,3072]{1,0:T(8,128)(2,1)S(1)} collective-permute-done((bf16[16,3072]{1,0:T(8,128)(2,1)}, bf16[16,3072]{1,0:T(8,128)(2,1)S(1)}, u32[]{:S(2)}, u32[]{:S(2)}) %collective-permute-start.26) | collective-permute-done | bytes 98336 | tf_op jit(solution)/shard_map/ppermute | solution.py:332
  184.9 2.0 add_last.1
  186.9 6.1 %all-to-all-start.3 = ((bf16[16,2,3072]{2,1,0:T(2,128)(2,1)}), bf16[16,2,3072]{2,1,0:T(2,128)(2,1)S(1)}, u32[]{:S(2)}, u32[]{:S(2)}) async-start(bf16[16,2,3072]{2,1,0:T(2,128)(2,1)} %add_last.1), calls=%async_computation.3 | async-start | bytes 393216 | tf_op jit(solution)/shard_map/all_to_all | solution.py:446
  193.1 11.5 %attention_grads.1 = (bf16[128,4096]{1,0:T(8,128)(2,1)}, bf16[128,4096]{1,0:T(8,128)(2,1)}, bf16[128,4096]{1,0:T(8,128)(2,1)}) custom-call(s32[1,4]{1,0:T(1,128)} %lengths_ref.3, s32[1]{0:T(128)} %bitcast.place_ref, f32[32,128]{1,0:T(8,128)} %bitcast.32, bf16[128,4096]{1,0:T(8,128)(2,1)} %bitcast.24, bf16[128,4096]{1,0:T(8,128)(2,1)} %bitcast.26, ...), custom_call_target="tpu_custom_call" | custom-call | flops 1073741824 | bytes 9437184 | tf_op jit(solution)/shard_map/attention_grads/pallas_call | solution.py:459
  205.3 1.8 combine.1
  (100 shorter events, 32.3 us)
Async XLA Ops:
  2.6 24.5 %all-to-all-start = ((bf16[16,2,6144]{2,1,0:T(2,128)(2,1)}), bf16[16,2,6144]{2,1,0:T(2,128)(2,1)S(1)}, u32[]{:S(2)}, u32[]{:S(2)}) async-start(bf16[16,2,6144]{2,1,0:T(2,128)(2,1)} %fill.1), calls=%async_computation | async-start | bytes 786432 | tf_op jit(solution)/shard_map/all_to_all | solution.py:371
  27.3 8.2 %collective-permute-start.2 = (bf16[16,6144]{1,0:T(8,128)(2,1)S(1)}, bf16[16,6144]{1,0:T(8,128)(2,1)S(1)}, u32[]{:S(2)}, u32[]{:S(2)}) collective-permute-start(bf16[16,6144]{1,0:T(8,128)(2,1)S(1)} %get-tuple-element.87), channel_id=1, source_target_pairs={{0,32},{16,48},{32,0},{48,16},{64,96},{80,112},{96,64},{112,80},{1... | collective-permute-start | bytes 589832 | tf_op jit(solution)/shard_map/ppermute | solution.py:332
  30.1 9.7 %collective-permute-start.1 = (bf16[16,6144]{1,0:T(8,128)(2,1)S(1)}, bf16[16,6144]{1,0:T(8,128)(2,1)S(1)}, u32[]{:S(2)}, u32[]{:S(2)}) collective-permute-start(bf16[16,6144]{1,0:T(8,128)(2,1)S(1)} %get-tuple-element.87), channel_id=1, source_target_pairs={{0,48},{16,0},{32,16},{48,32},{64,112},{80,64},{96,80},{112,96},{1... | collective-permute-start | bytes 589832 | tf_op jit(solution)/shard_map/ppermute | solution.py:332
  31.0 8.9 %collective-permute-start = (bf16[16,6144]{1,0:T(8,128)(2,1)S(1)}, bf16[16,6144]{1,0:T(8,128)(2,1)S(1)}, u32[]{:S(2)}, u32[]{:S(2)}) collective-permute-start(bf16[16,6144]{1,0:T(8,128)(2,1)S(1)} %get-tuple-element.87), channel_id=1, source_target_pairs={{0,16},{16,32},{32,48},{48,0},{64,80},{80,96},{96,112},{112,64},{1... | collective-permute-start | bytes 589832 | tf_op jit(solution)/shard_map/ppermute | solution.py:332
  31.6 11.2 %collective-permute-start.7 = (bf16[16,6144]{1,0:T(8,128)(2,1)S(1)}, bf16[16,6144]{1,0:T(8,128)(2,1)S(1)}, u32[]{:S(2)}, u32[]{:S(2)}) collective-permute-start(bf16[16,6144]{1,0:T(8,128)(2,1)S(1)} %get-tuple-element.86), channel_id=1, source_target_pairs={{0,128},{16,144},{32,160},{48,176},{64,192},{80,208},{96,224},{112... | collective-permute-start | bytes 589832 | tf_op jit(solution)/shard_map/ppermute | solution.py:332
  34.5 9.7 %collective-permute-start.6 = (bf16[16,6144]{1,0:T(8,128)(2,1)S(1)}, bf16[16,6144]{1,0:T(8,128)(2,1)S(1)}, u32[]{:S(2)}, u32[]{:S(2)}) collective-permute-start(bf16[16,6144]{1,0:T(8,128)(2,1)S(1)} %get-tuple-element.86), channel_id=1, source_target_pairs={{0,192},{16,208},{32,224},{48,240},{64,0},{80,16},{96,32},{112,48}... | collective-permute-start | bytes 589832 | tf_op jit(solution)/shard_map/ppermute | solution.py:332
  35.5 8.7 %collective-permute-start.5 = (bf16[16,6144]{1,0:T(8,128)(2,1)S(1)}, bf16[16,6144]{1,0:T(8,128)(2,1)S(1)}, u32[]{:S(2)}, u32[]{:S(2)}) collective-permute-start(bf16[16,6144]{1,0:T(8,128)(2,1)S(1)} %get-tuple-element.86), channel_id=1, source_target_pairs={{0,64},{16,80},{32,96},{48,112},{64,128},{80,144},{96,160},{112,17... | collective-permute-start | bytes 589832 | tf_op jit(solution)/shard_map/ppermute | solution.py:332
  39.9 20.8 %collective-permute-start.3 = (bf16[64,6144]{1,0:T(8,128)(2,1)S(1)}, bf16[64,6144]{1,0:T(8,128)(2,1)S(1)}, u32[]{:S(2)}, u32[]{:S(2)}) collective-permute-start(bf16[64,6144]{1,0:T(8,128)(2,1)S(1)} %pad_maximum_fusion.refs_0_), channel_id=1, source_target_pairs={{0,64},{16,80},{32,96},{48,112},{64,128},{80,144},{96,160},{112,17... | collective-permute-start | bytes 2359304 | tf_op jit(solution)/shard_map/ppermute | solution.py:332
  41.3 19.8 %collective-permute-start.4 = (bf16[64,6144]{1,0:T(8,128)(2,1)S(1)}, bf16[64,6144]{1,0:T(8,128)(2,1)S(1)}, u32[]{:S(2)}, u32[]{:S(2)}) collective-permute-start(bf16[64,6144]{1,0:T(8,128)(2,1)S(1)} %pad_maximum_fusion.refs_0_), channel_id=1, source_target_pairs={{0,192},{16,208},{32,224},{48,240},{64,0},{80,16},{96,32},{112,48}... | collective-permute-start | bytes 2359304 | tf_op jit(solution)/shard_map/ppermute | solution.py:332
  44.3 19.1 %collective-permute-start.8 = (bf16[64,6144]{1,0:T(8,128)(2,1)S(1)}, bf16[64,6144]{1,0:T(8,128)(2,1)}, u32[]{:S(2)}, u32[]{:S(2)}) collective-permute-start(bf16[64,6144]{1,0:T(8,128)(2,1)S(1)} %pad_maximum_fusion.1.refs_1_), channel_id=1, source_target_pairs={{0,16},{16,32},{32,48},{48,0},{64,80},{80,96},{96,112},{112,64},{1... | collective-permute-start | bytes 2359304 | tf_op jit(solution)/shard_map/ppermute | solution.py:332
  45.2 18.2 %collective-permute-start.9 = (bf16[64,6144]{1,0:T(8,128)(2,1)S(1)}, bf16[64,6144]{1,0:T(8,128)(2,1)}, u32[]{:S(2)}, u32[]{:S(2)}) collective-permute-start(bf16[64,6144]{1,0:T(8,128)(2,1)S(1)} %pad_maximum_fusion.1.refs_1_), channel_id=1, source_target_pairs={{0,48},{16,0},{32,16},{48,32},{64,112},{80,64},{96,80},{112,96},{1... | collective-permute-start | bytes 2359304 | tf_op jit(solution)/shard_map/ppermute | solution.py:332
  63.4 59.0 %all-to-all-start.1 = ((bf16[16,528,128]{2,1,0:T(8,128)(2,1)}), bf16[16,528,128]{2,1,0:T(8,128)(2,1)S(1)}, u32[]{:S(2)}, u32[]{:S(2)}) async-start(bf16[16,528,128]{2,1,0:T(8,128)(2,1)} %local_sums.1), calls=%async_computation.1 | async-start | bytes 4325376 | tf_op jit(solution)/shard_map/all_to_all | solution.py:408
  70.7 33.7 %collective-permute-start.10 = (bf16[32,6144]{1,0:T(8,128)(2,1)S(1)}, bf16[32,6144]{1,0:T(8,128)(2,1)S(1)}, u32[]{:S(2)}, u32[]{:S(2)}) collective-permute-start(bf16[32,6144]{1,0:T(8,128)(2,1)S(1)} %slice.20), channel_id=1, source_target_pairs={{0,64},{16,80},{32,96},{48,112},{64,128},{80,144},{96,160},{112,17... | collective-permute-start | bytes 1179656 | tf_op jit(solution)/shard_map/ppermute | solution.py:332
  73.4 31.0 %collective-permute-start.11 = (bf16[32,6144]{1,0:T(8,128)(2,1)S(1)}, bf16[32,6144]{1,0:T(8,128)(2,1)S(1)}, u32[]{:S(2)}, u32[]{:S(2)}) collective-permute-start(bf16[32,6144]{1,0:T(8,128)(2,1)S(1)} %slice.21), channel_id=1, source_target_pairs={{0,192},{16,208},{32,224},{48,240},{64,0},{80,16},{96,32},{112,48}... | collective-permute-start | bytes 1179656 | tf_op jit(solution)/shard_map/ppermute | solution.py:332
  75.8 31.3 %collective-permute-start.12 = (bf16[32,6144]{1,0:T(8,128)(2,1)S(1)}, bf16[32,6144]{1,0:T(8,128)(2,1)S(1)}, u32[]{:S(2)}, u32[]{:S(2)}) collective-permute-start(bf16[32,6144]{1,0:T(8,128)(2,1)S(1)} %slice.22), channel_id=1, source_target_pairs={{0,16},{16,32},{32,48},{48,0},{64,80},{80,96},{96,112},{112,64},{1... | collective-permute-start | bytes 1179656 | tf_op jit(solution)/shard_map/ppermute | solution.py:332
  78.2 28.9 %collective-permute-start.13 = (bf16[32,6144]{1,0:T(8,128)(2,1)S(1)}, bf16[32,6144]{1,0:T(8,128)(2,1)S(1)}, u32[]{:S(2)}, u32[]{:S(2)}) collective-permute-start(bf16[32,6144]{1,0:T(8,128)(2,1)S(1)} %slice.23), channel_id=1, source_target_pairs={{0,48},{16,0},{32,16},{48,32},{64,112},{80,64},{96,80},{112,96},{1... | collective-permute-start | bytes 1179656 | tf_op jit(solution)/shard_map/ppermute | solution.py:332
  116.6 11.2 %collective-permute-start.14 = (bf16[32,3072]{1,0:T(8,128)(2,1)}, bf16[32,3072]{1,0:T(8,128)(2,1)S(1)}, u32[]{:S(2)}, u32[]{:S(2)}) collective-permute-start(bf16[32,3072]{1,0:T(8,128)(2,1)} %get-tuple-element.58), channel_id=1, source_target_pairs={{0,64},{16,80},{32,96},{48,112},{64,128},{80,144},{96,160},{112,17... | collective-permute-start | bytes 589832 | tf_op jit(solution)/shard_map/ppermute | solution.py:332
  118.4 9.4 %collective-permute-start.15 = (bf16[32,3072]{1,0:T(8,128)(2,1)}, bf16[32,3072]{1,0:T(8,128)(2,1)S(1)}, u32[]{:S(2)}, u32[]{:S(2)}) collective-permute-start(bf16[32,3072]{1,0:T(8,128)(2,1)} %get-tuple-element.59), channel_id=1, source_target_pairs={{0,192},{16,208},{32,224},{48,240},{64,0},{80,16},{96,32},{112,48}... | collective-permute-start | bytes 589832 | tf_op jit(solution)/shard_map/ppermute | solution.py:332
  119.7 8.2 %collective-permute-start.16 = (bf16[32,3072]{1,0:T(8,128)(2,1)}, bf16[32,3072]{1,0:T(8,128)(2,1)S(1)}, u32[]{:S(2)}, u32[]{:S(2)}) collective-permute-start(bf16[32,3072]{1,0:T(8,128)(2,1)} %get-tuple-element.60), channel_id=1, source_target_pairs={{0,16},{16,32},{32,48},{48,0},{64,80},{80,96},{96,112},{112,64},{1... | collective-permute-start | bytes 589832 | tf_op jit(solution)/shard_map/ppermute | solution.py:332
  119.8 8.1 %collective-permute-start.17 = (bf16[32,3072]{1,0:T(8,128)(2,1)}, bf16[32,3072]{1,0:T(8,128)(2,1)S(1)}, u32[]{:S(2)}, u32[]{:S(2)}) collective-permute-start(bf16[32,3072]{1,0:T(8,128)(2,1)} %get-tuple-element.61), channel_id=1, source_target_pairs={{0,48},{16,0},{32,16},{48,32},{64,112},{80,64},{96,80},{112,96},{1... | collective-permute-start | bytes 589832 | tf_op jit(solution)/shard_map/ppermute | solution.py:332
  128.7 52.0 %all-to-all-start.2 = ((bf16[16,512,128]{2,1,0:T(8,128)(2,1)}), bf16[16,512,128]{2,1,0:T(8,128)(2,1)S(1)}, u32[]{:S(2)}, u32[]{:S(2)}) async-start(bf16[16,512,128]{2,1,0:T(8,128)(2,1)} %scan.1), calls=%async_computation.2 | async-start | bytes 4194304 | tf_op jit(solution)/shard_map/all_to_all | solution.py:435
  145.2 22.6 %collective-permute-start.18 = (bf16[64,3072]{1,0:T(8,128)(2,1)}, bf16[64,3072]{1,0:T(8,128)(2,1)S(1)}, u32[]{:S(2)}, u32[]{:S(2)}) collective-permute-start(bf16[64,3072]{1,0:T(8,128)(2,1)} %get-tuple-element.67), channel_id=1, source_target_pairs={{0,64},{16,80},{32,96},{48,112},{64,128},{80,144},{96,160},{112,17... | collective-permute-start | bytes 1179656 | tf_op jit(solution)/shard_map/ppermute | solution.py:332
  146.4 21.4 %collective-permute-start.19 = (bf16[64,3072]{1,0:T(8,128)(2,1)}, bf16[64,3072]{1,0:T(8,128)(2,1)S(1)}, u32[]{:S(2)}, u32[]{:S(2)}) collective-permute-start(bf16[64,3072]{1,0:T(8,128)(2,1)} %get-tuple-element.68), channel_id=1, source_target_pairs={{0,192},{16,208},{32,224},{48,240},{64,0},{80,16},{96,32},{112,48}... | collective-permute-start | bytes 1179656 | tf_op jit(solution)/shard_map/ppermute | solution.py:332
  147.8 20.0 %collective-permute-start.20 = (bf16[64,3072]{1,0:T(8,128)(2,1)}, bf16[64,3072]{1,0:T(8,128)(2,1)S(1)}, u32[]{:S(2)}, u32[]{:S(2)}) collective-permute-start(bf16[64,3072]{1,0:T(8,128)(2,1)} %get-tuple-element.70), channel_id=1, source_target_pairs={{0,16},{16,32},{32,48},{48,0},{64,80},{80,96},{96,112},{112,64},{1... | collective-permute-start | bytes 1179656 | tf_op jit(solution)/shard_map/ppermute | solution.py:332
  149.1 18.8 %collective-permute-start.21 = (bf16[64,3072]{1,0:T(8,128)(2,1)}, bf16[64,3072]{1,0:T(8,128)(2,1)S(1)}, u32[]{:S(2)}, u32[]{:S(2)}) collective-permute-start(bf16[64,3072]{1,0:T(8,128)(2,1)} %get-tuple-element.71), channel_id=1, source_target_pairs={{0,48},{16,0},{32,16},{48,32},{64,112},{80,64},{96,80},{112,96},{1... | collective-permute-start | bytes 1179656 | tf_op jit(solution)/shard_map/ppermute | solution.py:332
  172.1 6.2 %collective-permute-start.22 = (bf16[16,3072]{1,0:T(8,128)(2,1)}, bf16[16,3072]{1,0:T(8,128)(2,1)S(1)}, u32[]{:S(2)}, u32[]{:S(2)}) collective-permute-start(bf16[16,3072]{1,0:T(8,128)(2,1)} %get-tuple-element.79), channel_id=1, source_target_pairs={{0,48},{16,0},{32,16},{48,32},{64,112},{80,64},{96,80},{112,96},{1... | collective-permute-start | bytes 294920 | tf_op jit(solution)/shard_map/ppermute | solution.py:332
  174.4 6.4 %collective-permute-start.23 = (bf16[16,3072]{1,0:T(8,128)(2,1)}, bf16[16,3072]{1,0:T(8,128)(2,1)S(1)}, u32[]{:S(2)}, u32[]{:S(2)}) collective-permute-start(bf16[16,3072]{1,0:T(8,128)(2,1)} %get-tuple-element.80), channel_id=1, source_target_pairs={{0,16},{16,32},{32,48},{48,0},{64,80},{80,96},{96,112},{112,64},{1... | collective-permute-start | bytes 294920 | tf_op jit(solution)/shard_map/ppermute | solution.py:332
  174.4 6.4 %collective-permute-start.24 = (bf16[16,3072]{1,0:T(8,128)(2,1)}, bf16[16,3072]{1,0:T(8,128)(2,1)S(1)}, u32[]{:S(2)}, u32[]{:S(2)}) collective-permute-start(bf16[16,3072]{1,0:T(8,128)(2,1)} %get-tuple-element.81), channel_id=1, source_target_pairs={{0,32},{16,48},{32,0},{48,16},{64,96},{80,112},{96,64},{112,80},{1... | collective-permute-start | bytes 294920 | tf_op jit(solution)/shard_map/ppermute | solution.py:332
  176.7 4.1 %collective-permute-start.25 = (bf16[16,3072]{1,0:T(8,128)(2,1)}, bf16[16,3072]{1,0:T(8,128)(2,1)S(1)}, u32[]{:S(2)}, u32[]{:S(2)}) collective-permute-start(bf16[16,3072]{1,0:T(8,128)(2,1)} %get-tuple-element.83), channel_id=1, source_target_pairs={{0,192},{16,208},{32,224},{48,240},{64,0},{80,16},{96,32},{112,48}... | collective-permute-start | bytes 294920 | tf_op jit(solution)/shard_map/ppermute | solution.py:332
  178.3 5.9 %collective-permute-start.26 = (bf16[16,3072]{1,0:T(8,128)(2,1)}, bf16[16,3072]{1,0:T(8,128)(2,1)S(1)}, u32[]{:S(2)}, u32[]{:S(2)}) collective-permute-start(bf16[16,3072]{1,0:T(8,128)(2,1)} %get-tuple-element.84), channel_id=1, source_target_pairs={{0,64},{16,80},{32,96},{48,112},{64,128},{80,144},{96,160},{112,17... | collective-permute-start | bytes 294920 | tf_op jit(solution)/shard_map/ppermute | solution.py:332
  178.3 5.9 %collective-permute-start.27 = (bf16[16,3072]{1,0:T(8,128)(2,1)}, bf16[16,3072]{1,0:T(8,128)(2,1)S(1)}, u32[]{:S(2)}, u32[]{:S(2)}) collective-permute-start(bf16[16,3072]{1,0:T(8,128)(2,1)} %get-tuple-element.85), channel_id=1, source_target_pairs={{0,128},{16,144},{32,160},{48,176},{64,192},{80,208},{96,224},{112... | collective-permute-start | bytes 294920 | tf_op jit(solution)/shard_map/ppermute | solution.py:332
  186.9 17.6 %all-to-all-start.3 = ((bf16[16,2,3072]{2,1,0:T(2,128)(2,1)}), bf16[16,2,3072]{2,1,0:T(2,128)(2,1)S(1)}, u32[]{:S(2)}, u32[]{:S(2)}) async-start(bf16[16,2,3072]{2,1,0:T(2,128)(2,1)} %add_last.1), calls=%async_computation.3 | async-start | bytes 393216 | tf_op jit(solution)/shard_map/all_to_all | solution.py:446
  (24 other events, 66.8 us)

commit v3 on v2

--- a/solution.py
+++ b/solution.py
@@ -14,6 +14,7 @@
 HEADS_STEP = 8
 DECAY_ROWS = 16
 VMEM_MIB = 60
+SMALL_MIB = 16
 SIDE = 4
 HALF = 16
 NEAR = (0, -1, 1, 2)
@@ -191,8 +192,8 @@
 
 def expert_kernel(count, *refs):
     buffers, weights = refs[:count], refs[count : count + 3]
-    outs = refs[count + 3 : 2 * count + 3]
-    x_ref, wg_ref, wu_ref, wd_ref, x_sem, w_sem = refs[2 * count + 3 :]
+    outs = refs[count + 3 : -6]
+    x_ref, wg_ref, wu_ref, wd_ref, x_sem, w_sem = refs[-6:]
     copies = []
     at = 0
     for n, buffer in enumerate(buffers):
@@ -225,16 +226,18 @@
         at += rows
 
 
-def expert_rows(buffers, weights):
+def expert_rows(buffers, weights, outs=None):
     count = len(buffers)
+    sizes = [buffer.shape[0] for buffer in buffers]
+    sizes = sizes if outs is None else [sum(sizes) // outs] * outs
     hidden, width = weights[0].shape
     rows = sum(buffer.shape[0] for buffer in buffers)
     any_spec = pl.BlockSpec(memory_space=pl.ANY)
     return pl.pallas_call(
         functools.partial(expert_kernel, count),
-        out_shape=[jax.ShapeDtypeStruct((buffer.shape[0], width), BF16) for buffer in buffers],
+        out_shape=[jax.ShapeDtypeStruct((size, width), BF16) for size in sizes],
         in_specs=[any_spec] * (count + 3),
-        out_specs=[VMEM] * count,
+        out_specs=[VMEM] * len(sizes),
         scratch_shapes=[pltpu.VMEM((rows, 2 * width), BF16)]
         + [pltpu.VMEM((hidden, width), BF16)] * 3
         + [pltpu.SemaphoreType.DMA((count,)), pltpu.SemaphoreType.DMA((3,))],
@@ -288,7 +291,7 @@
         out_shape=[jax.ShapeDtypeStruct((HALF, width), BF16)] * count,
         in_specs=[VMEM] * (group * len(groups)),
         out_specs=[VMEM] * count,
-        compiler_params=params(VMEM_MIB),
+        compiler_params=params(SMALL_MIB),
         cost_estimate=cost(count * HALF * width * group, 2 * count * HALF * width * group),
         name="add_own",
     )(*[ref for refs in groups for ref in refs])
@@ -314,7 +317,7 @@
         out_shape=jax.ShapeDtypeStruct((HALF, 2, width), BF16),
         in_specs=[VMEM] * (2 * len(first)),
         out_specs=VMEM,
-        compiler_params=params(VMEM_MIB),
+        compiler_params=params(SMALL_MIB),
         cost_estimate=cost(8 * HALF * width, 20 * HALF * width),
         name="add_last",
     )(*first, *second)
@@ -394,17 +397,21 @@
     first, second = arrived[:HALF], arrived[HALF:]
     first_near = [first] + [send(first, along_x(-d)) for d in NEAR[1:]]
     second_near = [second] + [send(second, along_y(-d)) for d in NEAR[1:]]
-    first_row = jnp.concatenate(first_near)
-    second_col = jnp.concatenate(second_near)
+    first_row = [jnp.concatenate(first_near[:2]), jnp.concatenate(first_near[2:])]
+    second_col = [jnp.concatenate(second_near[:2]), jnp.concatenate(second_near[2:])]
     weights = (w_gate[0], w_up[0], w_down[0])
-    first_up, first_down = send(first_row, along_y(1)), send(first_row, along_y(-1))
-    second_left, second_right = send(second_col, along_x(1)), send(second_col, along_x(-1))
-    first_own, second_own = expert_rows([first_row, second_col], weights)
-    held = lax.optimization_barrier(
-        (first_up, first_down, second_left, second_right, first_own, second_own, local)
-    )
-    first_up, first_down, second_left, second_right, first_own, second_own, local = held
-
+    ways = [along_y(1), along_y(-1), along_x(1), along_x(-1)]
+    both = [first_row, first_row, second_col, second_col]
+    early = [send(pair[n % 2], ways[n]) for n, pair in enumerate(both)]
+    far = [send(part, way) for part, way in zip(early, ways)]
+    late = [send(pair[1 - n % 2], ways[n]) for n, pair in enumerate(both)]
+    held = lax.optimization_barrier((*late, *far, local))
+    late, far, local = list(held[:4]), list(held[4:8]), held[8]
+    near = [
+        early[0], late[0], late[1], early[1],
+        early[2], late[2], late[3], early[3],
+    ]
+    *near_terms, first_own, second_own = expert_rows(near + first_row + second_col, weights, 6)
     own_heads = lax.all_to_all(local, "ctx", split_axis=0, concat_axis=0, tiled=True)
     state_spec = pl.BlockSpec((blocks, size, size), lambda i: (0, i, 0))
     scanned = pl.pallas_call(
@@ -416,25 +423,18 @@
             state_spec,
         ],
         out_specs=state_spec,
-        compiler_params=params(VMEM_MIB),
+        compiler_params=params(SMALL_MIB),
         cost_estimate=cost(blocks * 8 * size * size, 16 * blocks * size * size),
         name="scan",
     )(own_heads, own_heads)
 
-    cut = 2 * HALF
-    far = [
-        send(first_up[:cut], along_y(1)), send(first_down[cut:], along_y(-1)),
-        send(second_left[:cut], along_x(1)), send(second_right[cut:], along_x(-1)),
-    ]
-    near_terms = expert_rows([first_up, first_down, second_left, second_right], weights)
     far_terms = expert_rows(far, weights)
-    ways = [along_y(1), along_y(-1), along_x(1), along_x(-1)]
     arrived_far = [send(part, way) for part, way in zip(far_terms, ways)]
     up, down, left, right = near_terms
-    *arrived_far, scanned = lax.optimization_barrier((*arrived_far, scanned))
-    states = lax.all_to_all(scanned, "ctx", split_axis=0, concat_axis=0, tiled=True)
     halves = add_halves([down, up, right, left], arrived_far)
     arrived_near = [send(part, way) for part, way in zip(halves, ways)]
+    *arrived_near, scanned = lax.optimization_barrier((*arrived_near, scanned))
+    states = lax.all_to_all(scanned, "ctx", split_axis=0, concat_axis=0, tiled=True)
     first_sum, second_sum = add_own(
         [[first_own] + arrived_near[:2], [second_own] + arrived_near[2:]]
     )
@@ -451,7 +451,7 @@
         out_shape=jax.ShapeDtypeStruct((tokens, width), BF16),
         in_specs=[SMEM, VMEM],
         out_specs=VMEM,
-        compiler_params=params(VMEM_MIB),
+        compiler_params=params(SMALL_MIB),
         cost_estimate=cost(2 * slots * tokens * width, 4 * slots * width),
         name="combine",
     )(routes.T, returned)

time: 208 us -> 189 us (0.909)
  Pallas kernels: 59 us -> 46.5 us
  local copies, waits for them, and re-layouts: 10.1 us -> 2.48 us
  starting transfers between devices: 67.8 us -> 72 us
  waiting for transfers between devices: 69.2 us -> 66 us
    pallas_call x3 -> x2, Pallas kernels: 25.7 us -> 18.8 us  [expert_rows(): pl.pallas_call(functools.partial(expert_kernel, count), out_shape=[jax.Sh...]
    ppermute x28 -> x32, starting transfers between devices: 40.5 us -> 45.9 us  [send(): return lax.ppermute(array, 'ctx', pairs)]
    unnamed x48 -> x44, local copies, waits for them, and re-layouts: 6.07 us -> 2.2 us
    all_to_all x1, starting transfers between devices: 7.27 us -> 4.07 us  [per_device(): lax.all_to_all(local, 'ctx', split_axis=0, concat_axis=0, tiled=True)]
    ppermute x28 -> x32, waiting for transfers between devices: 61.3 us -> 58.1 us  [send(): return lax.ppermute(array, 'ctx', pairs)]
    slice x4 -> x0, local copies, waits for them, and re-layouts: 3.09 us -> none  [the longest x1 1.02 us: per_device(): first_down[cut:]]
    pallas_call x1, Pallas kernels: 4.09 us -> 1.28 us  [per_device(): pl.pallas_call(scan_kernel, grid=(4,), out_shape=jax.ShapeDtypeStruct((bl...]
  transfers between devices with their start and end apart: 32 -> 36, of which waited for: 12 -> 19; matrix products, arithmetic and copies ran while one was open for 2% -> 0% of each run, Pallas kernels for 26% -> 22%
where the time goes in v3:
time: 189 us; the launch traced here: 188 us
  starting transfers between devices  72 us (38%)
  waiting for transfers between devices  66 us (35%)
  Pallas kernels  46.5 us (25%)
  local copies, waits for them, and re-layouts  2.48 us (1%)
    ppermute x32, waiting for transfers between devices, send(): return lax.ppermute(array, 'ctx', pairs)  58.1 us
    ppermute x32, starting transfers between devices, send(): return lax.ppermute(array, 'ctx', pairs)  45.9 us
    pallas_call x2, Pallas kernels, expert_rows(): pl.pallas_call(functools.partial(expert_kernel, count), out_shape=[jax.Sh...  18.8 us
    pallas_call x1, Pallas kernels, per_device(): pl.pallas_call(grads_kernel, grid=(steps,), out_shape=[jax.ShapeDtypeStru...  11.5 us
    all_to_all x1, starting transfers between devices, per_device(): lax.all_to_all(filled, 'exp', split_axis=0, concat_axis=0, tiled=True)  9.98 us
    all_to_all x1, waiting for transfers between devices, per_device(): lax.all_to_all(filled, 'exp', split_axis=0, concat_axis=0, tiled=True)  7.93 us
    all_to_all x1, starting transfers between devices, per_device(): lax.all_to_all(summed, 'exp', split_axis=0, concat_axis=0, tiled=True)  7.62 us
    pallas_call x1, Pallas kernels, per_device(): pl.pallas_call(local_kernel, grid=(steps,), out_shape=jax.ShapeDtypeStruc...  6.62 us
  transfers between devices with their start and end apart: 36, of which 19 were waited for; matrix products, arithmetic and copies ran while one was open for 0% of the time, Pallas kernels for 22%

profile of v3, /device:TPU:1, one launch (start us, length us, event | category | flops | bytes accessed | tf_op | source)
XLA Modules:
  0.0 188.0 jit_solution(2973003191873593474)
XLA Ops:
  0.6 2.0 %fill.1 = bf16[16,2,6144]{2,1,0:T(2,128)(2,1)} custom-call(s32[2,8]{1,0:T(2,128)} %bitcast.14, f32[2,8]{1,0:T(2,128)} %bitcast.32, bf16[8,3072]{1,0:T(8,128)(2,1)} %in_ref.1, bf16[8,3072]{1,0:T(8,128)(2,1)} %grad_ref.1), custom_call_target="tpu_custom_call" | custom-call | flops 3145728 | bytes 786432 | tf_op jit(solution)/shard_map/fill/pallas_call | solution.py:365
  2.6 10.0 %all-to-all-start = ((bf16[16,2,6144]{2,1,0:T(2,128)(2,1)}), bf16[16,2,6144]{2,1,0:T(2,128)(2,1)S(1)}, u32[]{:S(2)}, u32[]{:S(2)}) async-start(bf16[16,2,6144]{2,1,0:T(2,128)(2,1)} %fill.1), calls=%async_computation | async-start | bytes 786432 | tf_op jit(solution)/shard_map/all_to_all | solution.py:374
  12.6 6.6 %local_sums.1 = bf16[16,528,128]{2,1,0:T(8,128)(2,1)} custom-call(s32[1,4]{1,0:T(1,128)} %lengths_ref.3, s32[1]{0:T(128)} %bitcast.place_ref, f32[32,128]{1,0:T(8,128)} %bitcast.30, bf16[128,4096]{1,0:T(8,128)(2,1)} %bitcast.16, bf16[128,4096]{1,0:T(8,128)(2,1)} %bitcast.18, bf16[128,4096]{1,0:T(8,128)(2,1)} %bitcast.20, bf16[128,4096]{1,0:T(8,128)(2,1)} %bitcast.22), custom_call_target="tpu_custom_call" | custom-call | flops 268435456 | bytes 6291456 | tf_op jit(solution)/shard_map/local_sums/pallas_call | solution.py:385
  19.2 7.9 %all-to-all-done = bf16[16,2,6144]{2,1,0:T(2,128)(2,1)S(1)} async-done(((bf16[16,2,6144]{2,1,0:T(2,128)(2,1)}), bf16[16,2,6144]{2,1,0:T(2,128)(2,1)S(1)}, u32[]{:S(2)}, u32[]{:S(2)}) %all-to-all-start) | async-done | bytes 393248 | tf_op jit(solution)/shard_map/all_to_all | solution.py:374
  27.3 2.8 %collective-permute-start.6 = (bf16[16,6144]{1,0:T(8,128)(2,1)S(1)}, bf16[16,6144]{1,0:T(8,128)(2,1)S(1)}, u32[]{:S(2)}, u32[]{:S(2)}) collective-permute-start(bf16[16,6144]{1,0:T(8,128)(2,1)S(1)} %get-tuple-element.90), channel_id=1, source_target_pairs={{0,192},{16,208},{32,224},{48,240},{64,0},{80,16},{96,32},{112,48}... | collective-permute-start | bytes 589832 | tf_op jit(solution)/shard_map/ppermute | solution.py:335
  31.2 2.5 %collective-permute-start.2 = (bf16[16,6144]{1,0:T(8,128)(2,1)S(1)}, bf16[16,6144]{1,0:T(8,128)(2,1)S(1)}, u32[]{:S(2)}, u32[]{:S(2)}) collective-permute-start(bf16[16,6144]{1,0:T(8,128)(2,1)S(1)} %get-tuple-element.91), channel_id=1, source_target_pairs={{0,48},{16,0},{32,16},{48,32},{64,112},{80,64},{96,80},{112,96},{1... | collective-permute-start | bytes 589832 | tf_op jit(solution)/shard_map/ppermute | solution.py:335
  34.2 4.6 %collective-permute-done.6 = bf16[16,6144]{1,0:T(8,128)(2,1)S(1)} collective-permute-done((bf16[16,6144]{1,0:T(8,128)(2,1)S(1)}, bf16[16,6144]{1,0:T(8,128)(2,1)S(1)}, u32[]{:S(2)}, u32[]{:S(2)}) %collective-permute-start.6) | collective-permute-done | bytes 196640 | tf_op jit(solution)/shard_map/ppermute | solution.py:335
  47.9 2.7 %collective-permute-done.16.refs_7_ = bf16[32,6144]{1,0:T(8,128)(2,1)S(1)} collective-permute-done((bf16[32,6144]{1,0:T(8,128)(2,1)S(1)}, bf16[32,6144]{1,0:T(8,128)(2,1)S(1)}, u32[]{:S(2)}, u32[]{:S(2)}) %collective-permute-start.16) | collective-permute-done | bytes 393248 | tf_op jit(solution)/shard_map/ppermute | solution.py:335
  50.6 3.4 %collective-permute-start.10 = (bf16[32,6144]{1,0:T(8,128)(2,1)S(1)}, bf16[32,6144]{1,0:T(8,128)(2,1)S(1)}, u32[]{:S(2)}, u32[]{:S(2)}) collective-permute-start(bf16[32,6144]{1,0:T(8,128)(2,1)S(1)} %pad_maximum_fusion.1.refs_10_), channel_id=1, source_target_pairs={{0,48},{16,0},{32,16},{48,32},{64,112},{80,64},{96,80},{112,96},{1... | collective-permute-start | bytes 1179656 | tf_op jit(solution)/shard_map/ppermute | solution.py:335
  56.2 2.1 %collective-permute-start.5 = (bf16[32,6144]{1,0:T(8,128)(2,1)S(1)}, bf16[32,6144]{1,0:T(8,128)(2,1)S(1)}, u32[]{:S(2)}, u32[]{:S(2)}) collective-permute-start(bf16[32,6144]{1,0:T(8,128)(2,1)S(1)} %pad_maximum_fusion.refs_8_), channel_id=1, source_target_pairs={{0,192},{16,208},{32,224},{48,240},{64,0},{80,16},{96,32},{112,48}... | collective-permute-start | bytes 1179656 | tf_op jit(solution)/shard_map/ppermute | solution.py:335
  59.6 3.4 %collective-permute-done.8.refs_5_ = bf16[32,6144]{1,0:T(8,128)(2,1)S(1)} collective-permute-done((bf16[32,6144]{1,0:T(8,128)(2,1)S(1)}, bf16[32,6144]{1,0:T(8,128)(2,1)S(1)}, u32[]{:S(2)}, u32[]{:S(2)}) %collective-permute-start.8) | collective-permute-done | bytes 393248 | tf_op jit(solution)/shard_map/ppermute | solution.py:335
  63.0 3.8 %collective-permute-start.13 = (bf16[32,6144]{1,0:T(8,128)(2,1)S(1)}, bf16[32,6144]{1,0:T(8,128)(2,1)}, u32[]{:S(2)}, u32[]{:S(2)}) collective-permute-start(bf16[32,6144]{1,0:T(8,128)(2,1)S(1)} %collective-permute-done.12.refs_3_), channel_id=1, source_target_pairs={{0,192},{16,208},{32,224},{48,240},{64,0},{80,16},{96,32},{112,48}... | collective-permute-start | bytes 1179656 | tf_op jit(solution)/shard_map/ppermute | solution.py:335
  66.8 3.2 %collective-permute-done.17.refs_3_ = bf16[32,6144]{1,0:T(8,128)(2,1)S(1)} collective-permute-done((bf16[32,6144]{1,0:T(8,128)(2,1)S(1)}, bf16[32,6144]{1,0:T(8,128)(2,1)S(1)}, u32[]{:S(2)}, u32[]{:S(2)}) %collective-permute-start.17) | collective-permute-done | bytes 393248 | tf_op jit(solution)/shard_map/ppermute | solution.py:335
  70.0 3.8 %collective-permute-done.15.refs_2_ = bf16[32,6144]{1,0:T(8,128)(2,1)} collective-permute-done((bf16[32,6144]{1,0:T(8,128)(2,1)S(1)}, bf16[32,6144]{1,0:T(8,128)(2,1)}, u32[]{:S(2)}, u32[]{:S(2)}) %collective-permute-start.15) | collective-permute-done | bytes 393248 | tf_op jit(solution)/shard_map/ppermute | solution.py:335
  74.7 2.4 %collective-permute-done.11.refs_0_ = bf16[32,6144]{1,0:T(8,128)(2,1)} collective-permute-done((bf16[32,6144]{1,0:T(8,128)(2,1)S(1)}, bf16[32,6144]{1,0:T(8,128)(2,1)}, u32[]{:S(2)}, u32[]{:S(2)}) %collective-permute-start.11) | collective-permute-done | bytes 393248 | tf_op jit(solution)/shard_map/ppermute | solution.py:335
  77.1 4.1 %all-to-all-start.1 = ((bf16[16,528,128]{2,1,0:T(8,128)(2,1)}), bf16[16,528,128]{2,1,0:T(8,128)(2,1)S(1)}, u32[]{:S(2)}, u32[]{:S(2)}) async-start(bf16[16,528,128]{2,1,0:T(8,128)(2,1)} %local_sums.1), calls=%async_computation.1 | async-start | bytes 4325376 | tf_op jit(solution)/shard_map/all_to_all | solution.py:415
  81.1 8.0 %experts.3 = (bf16[32,3072]{1,0:T(8,128)(2,1)}, bf16[32,3072]{1,0:T(8,128)(2,1)}, bf16[32,3072]{1,0:T(8,128)(2,1)}, bf16[32,3072]{1,0:T(8,128)(2,1)}) custom-call(bf16[32,6144]{1,0:T(8,128)(2,1)} %collective-permute-done.11.refs_0_, bf16[32,6144]{1,0:T(8,128)(2,1)} %collective-permute-done.13.refs_1_, bf16[32,6144]{1,0:T(8,128)(2,1)} %collective-permute-done.15.refs_2_, ...), custom_call_target="tpu_custom_call" | custom-call | flops 1132462080 | bytes 7667712 | tf_op jit(solution)/shard_map/experts/pallas_call | solution.py:236
  94.6 10.8 %experts.2 = (bf16[64,3072]{1,0:T(8,128)(2,1)}, bf16[64,3072]{1,0:T(8,128)(2,1)}, bf16[64,3072]{1,0:T(8,128)(2,1)}, bf16[64,3072]{1,0:T(8,128)(2,1)}, bf16[64,30...) custom-call(bf16[32,6144]{1,0:T(8,128)(2,1)} %copy-done.16, bf16[32,6144]{1,0:T(8,128)(2,1)} %copy-done.19, ...), custom_call_target="tpu_custom_call" | custom-call | flops 3397386240 | bytes 12386304 | tf_op jit(solution)/shard_map/experts/pallas_call | solution.py:236
  105.4 6.0 %collective-permute-done.18.refs_4_ = bf16[32,3072]{1,0:T(8,128)(2,1)S(1)} collective-permute-done((bf16[32,3072]{1,0:T(8,128)(2,1)}, bf16[32,3072]{1,0:T(8,128)(2,1)S(1)}, u32[]{:S(2)}, u32[]{:S(2)}) %collective-permute-start.18) | collective-permute-done | bytes 196640 | tf_op jit(solution)/shard_map/ppermute | solution.py:335
  113.1 2.8 %add_halves.1 = (bf16[64,3072]{1,0:T(8,128)(2,1)}, bf16[64,3072]{1,0:T(8,128)(2,1)}, bf16[64,3072]{1,0:T(8,128)(2,1)}, bf16[64,3072]{1,0:T(8,128)(2,1)}) custom-call(bf16[64,3072]{1,0:T(8,128)(2,1)} %get-tuple-element.54.refs_0_, bf16[64,3072]{1,0:T(8,128)(2,1)} %get-tuple-element.55.refs_1_, bf16[64,3072]{1,0:T(8,128)(2,1)} %get-tuple-element.56.refs_2_, ...), custom_call_target="tpu_custom_call" | custom-call | flops 786432 | bytes 4718592 | tf_op jit(solution)/shard_map/add_halves/pallas_call | solution.py:262
  118.8 1.8 collective-permute-start.24
  124.1 3.4 %collective-permute-done.22.refs_1_ = bf16[64,3072]{1,0:T(8,128)(2,1)S(1)} collective-permute-done((bf16[64,3072]{1,0:T(8,128)(2,1)}, bf16[64,3072]{1,0:T(8,128)(2,1)S(1)}, u32[]{:S(2)}, u32[]{:S(2)}) %collective-permute-start.22) | collective-permute-done | bytes 393248 | tf_op jit(solution)/shard_map/ppermute | solution.py:335
  127.5 2.1 %collective-permute-done.24.refs_4_ = bf16[64,3072]{1,0:T(8,128)(2,1)S(1)} collective-permute-done((bf16[64,3072]{1,0:T(8,128)(2,1)}, bf16[64,3072]{1,0:T(8,128)(2,1)S(1)}, u32[]{:S(2)}, u32[]{:S(2)}) %collective-permute-start.24) | collective-permute-done | bytes 393248 | tf_op jit(solution)/shard_map/ppermute | solution.py:335
  130.3 4.4 %all-to-all-start.2 = ((bf16[16,512,128]{2,1,0:T(8,128)(2,1)}), bf16[16,512,128]{2,1,0:T(8,128)(2,1)}, u32[]{:S(2)}, u32[]{:S(2)}) async-start(bf16[16,512,128]{2,1,0:T(8,128)(2,1)} %copy-done), calls=%async_computation.2 | async-start | bytes 4194304 | tf_op jit(solution)/shard_map/all_to_all | solution.py:437
  136.0 2.5 %collective-permute-start.26 = (bf16[16,3072]{1,0:T(8,128)(2,1)S(1)}, bf16[16,3072]{1,0:T(8,128)(2,1)S(1)}, u32[]{:S(2)}, u32[]{:S(2)}) collective-permute-start(bf16[16,3072]{1,0:T(8,128)(2,1)S(1)} %get-tuple-element.83), channel_id=1, source_target_pairs={{0,48},{16,0},{32,16},{48,32},{64,112},{80,64},{96,80},{112,96},{1... | collective-permute-start | bytes 294920 | tf_op jit(solution)/shard_map/ppermute | solution.py:335
  138.5 1.8 collective-permute-start.28
  140.3 2.4 %collective-permute-start.29 = (bf16[16,3072]{1,0:T(8,128)(2,1)S(1)}, bf16[16,3072]{1,0:T(8,128)(2,1)S(1)}, u32[]{:S(2)}, u32[]{:S(2)}) collective-permute-start(bf16[16,3072]{1,0:T(8,128)(2,1)S(1)} %get-tuple-element.87), channel_id=1, source_target_pairs={{0,192},{16,208},{32,224},{48,240},{64,0},{80,16},{96,32},{112,48}... | collective-permute-start | bytes 294920 | tf_op jit(solution)/shard_map/ppermute | solution.py:335
  142.8 17.4 %collective-permute-done.26.refs_1_ = bf16[16,3072]{1,0:T(8,128)(2,1)S(1)} collective-permute-done((bf16[16,3072]{1,0:T(8,128)(2,1)S(1)}, bf16[16,3072]{1,0:T(8,128)(2,1)S(1)}, u32[]{:S(2)}, u32[]{:S(2)}) %collective-permute-start.26) | collective-permute-done | bytes 98336 | tf_op jit(solution)/shard_map/ppermute | solution.py:335
  160.2 2.7 %collective-permute-start.31 = (bf16[16,3072]{1,0:T(8,128)(2,1)S(1)}, bf16[16,3072]{1,0:T(8,128)(2,1)S(1)}, u32[]{:S(2)}, u32[]{:S(2)}) collective-permute-start(bf16[16,3072]{1,0:T(8,128)(2,1)S(1)} %get-tuple-element.89), channel_id=1, source_target_pairs={{0,128},{16,144},{32,160},{48,176},{64,192},{80,208},{96,224},{112... | collective-permute-start | bytes 294920 | tf_op jit(solution)/shard_map/ppermute | solution.py:335
  163.9 2.6 %collective-permute-done.31.refs_7_ = bf16[16,3072]{1,0:T(8,128)(2,1)S(1)} collective-permute-done((bf16[16,3072]{1,0:T(8,128)(2,1)S(1)}, bf16[16,3072]{1,0:T(8,128)(2,1)S(1)}, u32[]{:S(2)}, u32[]{:S(2)}) %collective-permute-start.31) | collective-permute-done | bytes 98336 | tf_op jit(solution)/shard_map/ppermute | solution.py:335
  167.3 7.6 %all-to-all-start.3 = ((bf16[16,2,3072]{2,1,0:T(2,128)(2,1)}), bf16[16,2,3072]{2,1,0:T(2,128)(2,1)S(1)}, u32[]{:S(2)}, u32[]{:S(2)}) async-start(bf16[16,2,3072]{2,1,0:T(2,128)(2,1)} %add_last.1), calls=%async_computation.3 | async-start | bytes 393216 | tf_op jit(solution)/shard_map/all_to_all | solution.py:446
  175.0 11.5 %attention_grads.1 = (bf16[128,4096]{1,0:T(8,128)(2,1)}, bf16[128,4096]{1,0:T(8,128)(2,1)}, bf16[128,4096]{1,0:T(8,128)(2,1)}) custom-call(s32[1,4]{1,0:T(1,128)} %lengths_ref.3, s32[1]{0:T(128)} %bitcast.place_ref, f32[32,128]{1,0:T(8,128)} %bitcast.31, bf16[128,4096]{1,0:T(8,128)(2,1)} %bitcast.17, bf16[128,4096]{1,0:T(8,128)(2,1)} %bitcast.19, ...), custom_call_target="tpu_custom_call" | custom-call | flops 1073741824 | bytes 9437184 | tf_op jit(solution)/shard_map/attention_grads/pallas_call | solution.py:459
  (101 shorter events, 34.1 us)
Async XLA Ops:
  2.6 24.5 %all-to-all-start = ((bf16[16,2,6144]{2,1,0:T(2,128)(2,1)}), bf16[16,2,6144]{2,1,0:T(2,128)(2,1)S(1)}, u32[]{:S(2)}, u32[]{:S(2)}) async-start(bf16[16,2,6144]{2,1,0:T(2,128)(2,1)} %fill.1), calls=%async_computation | async-start | bytes 786432 | tf_op jit(solution)/shard_map/all_to_all | solution.py:374
  27.3 11.4 %collective-permute-start.6 = (bf16[16,6144]{1,0:T(8,128)(2,1)S(1)}, bf16[16,6144]{1,0:T(8,128)(2,1)S(1)}, u32[]{:S(2)}, u32[]{:S(2)}) collective-permute-start(bf16[16,6144]{1,0:T(8,128)(2,1)S(1)} %get-tuple-element.90), channel_id=1, source_target_pairs={{0,192},{16,208},{32,224},{48,240},{64,0},{80,16},{96,32},{112,48}... | collective-permute-start | bytes 589832 | tf_op jit(solution)/shard_map/ppermute | solution.py:335
  30.5 12.2 %collective-permute-start.9 = (bf16[16,6144]{1,0:T(8,128)(2,1)S(1)}, bf16[16,6144]{1,0:T(8,128)(2,1)S(1)}, u32[]{:S(2)}, u32[]{:S(2)}) collective-permute-start(bf16[16,6144]{1,0:T(8,128)(2,1)S(1)} %get-tuple-element.90), channel_id=1, source_target_pairs={{0,64},{16,80},{32,96},{48,112},{64,128},{80,144},{96,160},{112,17... | collective-permute-start | bytes 589832 | tf_op jit(solution)/shard_map/ppermute | solution.py:335
  31.2 12.9 %collective-permute-start.2 = (bf16[16,6144]{1,0:T(8,128)(2,1)S(1)}, bf16[16,6144]{1,0:T(8,128)(2,1)S(1)}, u32[]{:S(2)}, u32[]{:S(2)}) collective-permute-start(bf16[16,6144]{1,0:T(8,128)(2,1)S(1)} %get-tuple-element.91), channel_id=1, source_target_pairs={{0,48},{16,0},{32,16},{48,32},{64,112},{80,64},{96,80},{112,96},{1... | collective-permute-start | bytes 589832 | tf_op jit(solution)/shard_map/ppermute | solution.py:335
  33.7 10.4 %collective-permute-start.3 = (bf16[16,6144]{1,0:T(8,128)(2,1)S(1)}, bf16[16,6144]{1,0:T(8,128)(2,1)S(1)}, u32[]{:S(2)}, u32[]{:S(2)}) collective-permute-start(bf16[16,6144]{1,0:T(8,128)(2,1)S(1)} %get-tuple-element.91), channel_id=1, source_target_pairs={{0,32},{16,48},{32,0},{48,16},{64,96},{80,112},{96,64},{112,80},{1... | collective-permute-start | bytes 589832 | tf_op jit(solution)/shard_map/ppermute | solution.py:335
  40.0 10.6 %collective-permute-start.16 = (bf16[32,6144]{1,0:T(8,128)(2,1)S(1)}, bf16[32,6144]{1,0:T(8,128)(2,1)S(1)}, u32[]{:S(2)}, u32[]{:S(2)}) collective-permute-start(bf16[32,6144]{1,0:T(8,128)(2,1)S(1)} %constant_dynamic-update-slice_fusion.2.refs_11_), channel_id=1, source_target_pairs={{0,48},{16,0},{32,16},{48,32},{64,112},{80,64},{96,80},{112,96},{1... | collective-permute-start | bytes 1179656 | tf_op jit(solution)/shard_map/ppermute | solution.py:335
  42.8 11.8 %collective-permute-start.14 = (bf16[32,6144]{1,0:T(8,128)(2,1)S(1)}, bf16[32,6144]{1,0:T(8,128)(2,1)S(1)}, u32[]{:S(2)}, u32[]{:S(2)}) collective-permute-start(bf16[32,6144]{1,0:T(8,128)(2,1)S(1)} %pad_maximum_fusion.1.refs_10_), channel_id=1, source_target_pairs={{0,16},{16,32},{32,48},{48,0},{64,80},{80,96},{96,112},{112,64},{1... | collective-permute-start | bytes 1179656 | tf_op jit(solution)/shard_map/ppermute | solution.py:335
  44.1 12.1 %collective-permute-start.12 = (bf16[32,6144]{1,0:T(8,128)(2,1)S(1)}, bf16[32,6144]{1,0:T(8,128)(2,1)S(1)}, u32[]{:S(2)}, u32[]{:S(2)}) collective-permute-start(bf16[32,6144]{1,0:T(8,128)(2,1)S(1)} %constant_dynamic-update-slice_fusion.refs_9_), channel_id=1, source_target_pairs={{0,192},{16,208},{32,224},{48,240},{64,0},{80,16},{96,32},{112,48}... | collective-permute-start | bytes 1179656 | tf_op jit(solution)/shard_map/ppermute | solution.py:335
  46.6 11.8 %collective-permute-start.1 = (bf16[32,6144]{1,0:T(8,128)(2,1)S(1)}, bf16[32,6144]{1,0:T(8,128)(2,1)S(1)}, u32[]{:S(2)}, u32[]{:S(2)}) collective-permute-start(bf16[32,6144]{1,0:T(8,128)(2,1)S(1)} %pad_maximum_fusion.refs_8_), channel_id=1, source_target_pairs={{0,64},{16,80},{32,96},{48,112},{64,128},{80,144},{96,160},{112,17... | collective-permute-start | bytes 1179656 | tf_op jit(solution)/shard_map/ppermute | solution.py:335
  47.9 15.1 %collective-permute-start.8 = (bf16[32,6144]{1,0:T(8,128)(2,1)S(1)}, bf16[32,6144]{1,0:T(8,128)(2,1)S(1)}, u32[]{:S(2)}, u32[]{:S(2)}) collective-permute-start(bf16[32,6144]{1,0:T(8,128)(2,1)S(1)} %constant_dynamic-update-slice_fusion.2.refs_11_), channel_id=1, source_target_pairs={{0,16},{16,32},{32,48},{48,0},{64,80},{80,96},{96,112},{112,64},{1... | collective-permute-start | bytes 1179656 | tf_op jit(solution)/shard_map/ppermute | solution.py:335
  50.6 12.4 %collective-permute-start.10 = (bf16[32,6144]{1,0:T(8,128)(2,1)S(1)}, bf16[32,6144]{1,0:T(8,128)(2,1)S(1)}, u32[]{:S(2)}, u32[]{:S(2)}) collective-permute-start(bf16[32,6144]{1,0:T(8,128)(2,1)S(1)} %pad_maximum_fusion.1.refs_10_), channel_id=1, source_target_pairs={{0,48},{16,0},{32,16},{48,32},{64,112},{80,64},{96,80},{112,96},{1... | collective-permute-start | bytes 1179656 | tf_op jit(solution)/shard_map/ppermute | solution.py:335
  54.6 12.2 %collective-permute-start.4 = (bf16[32,6144]{1,0:T(8,128)(2,1)S(1)}, bf16[32,6144]{1,0:T(8,128)(2,1)S(1)}, u32[]{:S(2)}, u32[]{:S(2)}) collective-permute-start(bf16[32,6144]{1,0:T(8,128)(2,1)S(1)} %constant_dynamic-update-slice_fusion.refs_9_), channel_id=1, source_target_pairs={{0,64},{16,80},{32,96},{48,112},{64,128},{80,144},{96,160},{112,17... | collective-permute-start | bytes 1179656 | tf_op jit(solution)/shard_map/ppermute | solution.py:335
  56.2 10.6 %collective-permute-start.5 = (bf16[32,6144]{1,0:T(8,128)(2,1)S(1)}, bf16[32,6144]{1,0:T(8,128)(2,1)S(1)}, u32[]{:S(2)}, u32[]{:S(2)}) collective-permute-start(bf16[32,6144]{1,0:T(8,128)(2,1)S(1)} %pad_maximum_fusion.refs_8_), channel_id=1, source_target_pairs={{0,192},{16,208},{32,224},{48,240},{64,0},{80,16},{96,32},{112,48}... | collective-permute-start | bytes 1179656 | tf_op jit(solution)/shard_map/ppermute | solution.py:335
  58.4 11.6 %collective-permute-start.17 = (bf16[32,6144]{1,0:T(8,128)(2,1)S(1)}, bf16[32,6144]{1,0:T(8,128)(2,1)S(1)}, u32[]{:S(2)}, u32[]{:S(2)}) collective-permute-start(bf16[32,6144]{1,0:T(8,128)(2,1)S(1)} %collective-permute-done.16.refs_7_), channel_id=1, source_target_pairs={{0,48},{16,0},{32,16},{48,32},{64,112},{80,64},{96,80},{112,96},{1... | collective-permute-start | bytes 1179656 | tf_op jit(solution)/shard_map/ppermute | solution.py:335
  63.0 10.8 %collective-permute-start.15 = (bf16[32,6144]{1,0:T(8,128)(2,1)S(1)}, bf16[32,6144]{1,0:T(8,128)(2,1)}, u32[]{:S(2)}, u32[]{:S(2)}) collective-permute-start(bf16[32,6144]{1,0:T(8,128)(2,1)S(1)} %collective-permute-done.14.refs_4_), channel_id=1, source_target_pairs={{0,16},{16,32},{32,48},{48,0},{64,80},{80,96},{96,112},{112,64},{1... | collective-permute-start | bytes 1179656 | tf_op jit(solution)/shard_map/ppermute | solution.py:335
  63.0 11.6 %collective-permute-start.13 = (bf16[32,6144]{1,0:T(8,128)(2,1)S(1)}, bf16[32,6144]{1,0:T(8,128)(2,1)}, u32[]{:S(2)}, u32[]{:S(2)}) collective-permute-start(bf16[32,6144]{1,0:T(8,128)(2,1)S(1)} %collective-permute-done.12.refs_3_), channel_id=1, source_target_pairs={{0,192},{16,208},{32,224},{48,240},{64,0},{80,16},{96,32},{112,48}... | collective-permute-start | bytes 1179656 | tf_op jit(solution)/shard_map/ppermute | solution.py:335
  66.8 10.3 %collective-permute-start.11 = (bf16[32,6144]{1,0:T(8,128)(2,1)S(1)}, bf16[32,6144]{1,0:T(8,128)(2,1)}, u32[]{:S(2)}, u32[]{:S(2)}) collective-permute-start(bf16[32,6144]{1,0:T(8,128)(2,1)S(1)} %collective-permute-done.1.refs_0_), channel_id=1, source_target_pairs={{0,64},{16,80},{32,96},{48,112},{64,128},{80,144},{96,160},{112,17... | collective-permute-start | bytes 1179656 | tf_op jit(solution)/shard_map/ppermute | solution.py:335
  77.1 44.4 %all-to-all-start.1 = ((bf16[16,528,128]{2,1,0:T(8,128)(2,1)}), bf16[16,528,128]{2,1,0:T(8,128)(2,1)S(1)}, u32[]{:S(2)}, u32[]{:S(2)}) async-start(bf16[16,528,128]{2,1,0:T(8,128)(2,1)} %local_sums.1), calls=%async_computation.1 | async-start | bytes 4325376 | tf_op jit(solution)/shard_map/all_to_all | solution.py:415
  89.1 22.3 %collective-permute-start.18 = (bf16[32,3072]{1,0:T(8,128)(2,1)}, bf16[32,3072]{1,0:T(8,128)(2,1)S(1)}, u32[]{:S(2)}, u32[]{:S(2)}) collective-permute-start(bf16[32,3072]{1,0:T(8,128)(2,1)} %get-tuple-element.62), channel_id=1, source_target_pairs={{0,64},{16,80},{32,96},{48,112},{64,128},{80,144},{96,160},{112,17... | collective-permute-start | bytes 589832 | tf_op jit(solution)/shard_map/ppermute | solution.py:335
  90.6 20.9 %collective-permute-start.19 = (bf16[32,3072]{1,0:T(8,128)(2,1)}, bf16[32,3072]{1,0:T(8,128)(2,1)S(1)}, u32[]{:S(2)}, u32[]{:S(2)}) collective-permute-start(bf16[32,3072]{1,0:T(8,128)(2,1)} %get-tuple-element.63), channel_id=1, source_target_pairs={{0,192},{16,208},{32,224},{48,240},{64,0},{80,16},{96,32},{112,48}... | collective-permute-start | bytes 589832 | tf_op jit(solution)/shard_map/ppermute | solution.py:335
  91.9 20.5 %collective-permute-start.20 = (bf16[32,3072]{1,0:T(8,128)(2,1)}, bf16[32,3072]{1,0:T(8,128)(2,1)S(1)}, u32[]{:S(2)}, u32[]{:S(2)}) collective-permute-start(bf16[32,3072]{1,0:T(8,128)(2,1)} %get-tuple-element.64), channel_id=1, source_target_pairs={{0,16},{16,32},{32,48},{48,0},{64,80},{80,96},{96,112},{112,64},{1... | collective-permute-start | bytes 589832 | tf_op jit(solution)/shard_map/ppermute | solution.py:335
  93.3 19.1 %collective-permute-start.21 = (bf16[32,3072]{1,0:T(8,128)(2,1)}, bf16[32,3072]{1,0:T(8,128)(2,1)S(1)}, u32[]{:S(2)}, u32[]{:S(2)}) collective-permute-start(bf16[32,3072]{1,0:T(8,128)(2,1)} %get-tuple-element.65), channel_id=1, source_target_pairs={{0,48},{16,0},{32,16},{48,32},{64,112},{80,64},{96,80},{112,96},{1... | collective-permute-start | bytes 589832 | tf_op jit(solution)/shard_map/ppermute | solution.py:335
  115.9 11.6 %collective-permute-start.22 = (bf16[64,3072]{1,0:T(8,128)(2,1)}, bf16[64,3072]{1,0:T(8,128)(2,1)S(1)}, u32[]{:S(2)}, u32[]{:S(2)}) collective-permute-start(bf16[64,3072]{1,0:T(8,128)(2,1)} %get-tuple-element.66), channel_id=1, source_target_pairs={{0,64},{16,80},{32,96},{48,112},{64,128},{80,144},{96,160},{112,17... | collective-permute-start | bytes 1179656 | tf_op jit(solution)/shard_map/ppermute | solution.py:335
  117.6 9.9 %collective-permute-start.23 = (bf16[64,3072]{1,0:T(8,128)(2,1)}, bf16[64,3072]{1,0:T(8,128)(2,1)S(1)}, u32[]{:S(2)}, u32[]{:S(2)}) collective-permute-start(bf16[64,3072]{1,0:T(8,128)(2,1)} %get-tuple-element.67), channel_id=1, source_target_pairs={{0,192},{16,208},{32,224},{48,240},{64,0},{80,16},{96,32},{112,48}... | collective-permute-start | bytes 1179656 | tf_op jit(solution)/shard_map/ppermute | solution.py:335
  118.8 10.8 %collective-permute-start.24 = (bf16[64,3072]{1,0:T(8,128)(2,1)}, bf16[64,3072]{1,0:T(8,128)(2,1)S(1)}, u32[]{:S(2)}, u32[]{:S(2)}) collective-permute-start(bf16[64,3072]{1,0:T(8,128)(2,1)} %get-tuple-element.68), channel_id=1, source_target_pairs={{0,16},{16,32},{32,48},{48,0},{64,80},{80,96},{96,112},{112,64},{1... | collective-permute-start | bytes 1179656 | tf_op jit(solution)/shard_map/ppermute | solution.py:335
  130.3 32.5 %all-to-all-start.2 = ((bf16[16,512,128]{2,1,0:T(8,128)(2,1)}), bf16[16,512,128]{2,1,0:T(8,128)(2,1)}, u32[]{:S(2)}, u32[]{:S(2)}) async-start(bf16[16,512,128]{2,1,0:T(8,128)(2,1)} %copy-done), calls=%async_computation.2 | async-start | bytes 4194304 | tf_op jit(solution)/shard_map/all_to_all | solution.py:437
  136.0 24.1 %collective-permute-start.26 = (bf16[16,3072]{1,0:T(8,128)(2,1)S(1)}, bf16[16,3072]{1,0:T(8,128)(2,1)S(1)}, u32[]{:S(2)}, u32[]{:S(2)}) collective-permute-start(bf16[16,3072]{1,0:T(8,128)(2,1)S(1)} %get-tuple-element.83), channel_id=1, source_target_pairs={{0,48},{16,0},{32,16},{48,32},{64,112},{80,64},{96,80},{112,96},{1... | collective-permute-start | bytes 294920 | tf_op jit(solution)/shard_map/ppermute | solution.py:335
  138.5 25.4 %collective-permute-start.27 = (bf16[16,3072]{1,0:T(8,128)(2,1)S(1)}, bf16[16,3072]{1,0:T(8,128)(2,1)S(1)}, u32[]{:S(2)}, u32[]{:S(2)}) collective-permute-start(bf16[16,3072]{1,0:T(8,128)(2,1)S(1)} %get-tuple-element.84), channel_id=1, source_target_pairs={{0,16},{16,32},{32,48},{48,0},{64,80},{80,96},{96,112},{112,64},{1... | collective-permute-start | bytes 294920 | tf_op jit(solution)/shard_map/ppermute | solution.py:335
  138.5 25.4 %collective-permute-start.28 = (bf16[16,3072]{1,0:T(8,128)(2,1)S(1)}, bf16[16,3072]{1,0:T(8,128)(2,1)S(1)}, u32[]{:S(2)}, u32[]{:S(2)}) collective-permute-start(bf16[16,3072]{1,0:T(8,128)(2,1)S(1)} %get-tuple-element.85), channel_id=1, source_target_pairs={{0,32},{16,48},{32,0},{48,16},{64,96},{80,112},{96,64},{112,80},{1... | collective-permute-start | bytes 294920 | tf_op jit(solution)/shard_map/ppermute | solution.py:335
  140.3 23.6 %collective-permute-start.29 = (bf16[16,3072]{1,0:T(8,128)(2,1)S(1)}, bf16[16,3072]{1,0:T(8,128)(2,1)S(1)}, u32[]{:S(2)}, u32[]{:S(2)}) collective-permute-start(bf16[16,3072]{1,0:T(8,128)(2,1)S(1)} %get-tuple-element.87), channel_id=1, source_target_pairs={{0,192},{16,208},{32,224},{48,240},{64,0},{80,16},{96,32},{112,48}... | collective-permute-start | bytes 294920 | tf_op jit(solution)/shard_map/ppermute | solution.py:335
  142.7 21.2 %collective-permute-start.30 = (bf16[16,3072]{1,0:T(8,128)(2,1)S(1)}, bf16[16,3072]{1,0:T(8,128)(2,1)S(1)}, u32[]{:S(2)}, u32[]{:S(2)}) collective-permute-start(bf16[16,3072]{1,0:T(8,128)(2,1)S(1)} %get-tuple-element.88), channel_id=1, source_target_pairs={{0,64},{16,80},{32,96},{48,112},{64,128},{80,144},{96,160},{112,17... | collective-permute-start | bytes 294920 | tf_op jit(solution)/shard_map/ppermute | solution.py:335
  167.3 19.1 %all-to-all-start.3 = ((bf16[16,2,3072]{2,1,0:T(2,128)(2,1)}), bf16[16,2,3072]{2,1,0:T(2,128)(2,1)S(1)}, u32[]{:S(2)}, u32[]{:S(2)}) async-start(bf16[16,2,3072]{2,1,0:T(2,128)(2,1)} %add_last.1), calls=%async_computation.3 | async-start | bytes 393216 | tf_op jit(solution)/shard_map/all_to_all | solution.py:446
  (25 other events, 320.4 us)

commit v4 on v3

--- a/solution.py
+++ b/solution.py
@@ -192,33 +192,37 @@
 
 def expert_kernel(count, *refs):
     buffers, weights = refs[:count], refs[count : count + 3]
-    outs = refs[count + 3 : -6]
-    x_ref, wg_ref, wu_ref, wd_ref, x_sem, w_sem = refs[-6:]
+    outs = refs[count + 3 : -5]
+    x_ref, both_ref, wd_ref, x_sem, w_sem = refs[-5:]
+    hidden_units = wd_ref.shape[0]
     copies = []
     at = 0
     for n, buffer in enumerate(buffers):
         rows = buffer.shape[0]
         copies.append(pltpu.make_async_copy(buffer, x_ref.at[pl.ds(at, rows)], x_sem.at[n]))
         at += rows
+    places = (
+        both_ref.at[pl.ds(0, hidden_units)], both_ref.at[pl.ds(hidden_units, hidden_units)], wd_ref
+    )
     loads = [
         pltpu.make_async_copy(weight, held, w_sem.at[n])
-        for n, (weight, held) in enumerate(zip(weights, (wg_ref, wu_ref, wd_ref)))
+        for n, (weight, held) in enumerate(zip(weights, places))
     ]
     for copy in copies + loads:
         copy.start()
     for copy in copies:
         copy.wait()
-    width = wg_ref.shape[1]
+    width = wd_ref.shape[1]
     loads[0].wait()
-    gate = dot(wg_ref[...], x_ref[:, :width], NT)
+    loads[1].wait()
+    gate_up = dot(both_ref[...], x_ref[:, :width], NT)
+    gate, up = gate_up[:hidden_units], gate_up[hidden_units:]
     sigmoid = jax.nn.sigmoid(gate)
-    loads[1].wait()
-    up = dot(wu_ref[...], x_ref[:, :width], NT)
     loads[2].wait()
     hidden = dot(wd_ref[...], x_ref[:, width:], NT)
     grad_up = (hidden * gate * sigmoid).astype(BF16)
     grad_gate = (hidden * up * sigmoid * (1.0 + gate * (1.0 - sigmoid))).astype(BF16)
-    term = (dot(grad_gate, wg_ref[...], TN) + dot(grad_up, wu_ref[...], TN)).astype(BF16)
+    term = dot(jnp.concatenate([grad_gate, grad_up]), both_ref[...], TN).astype(BF16)
     at = 0
     for out in outs:
         rows = out.shape[0]
@@ -239,7 +243,7 @@
         in_specs=[any_spec] * (count + 3),
         out_specs=[VMEM] * len(sizes),
         scratch_shapes=[pltpu.VMEM((rows, 2 * width), BF16)]
-        + [pltpu.VMEM((hidden, width), BF16)] * 3
+        + [pltpu.VMEM((2 * hidden, width), BF16), pltpu.VMEM((hidden, width), BF16)]
         + [pltpu.SemaphoreType.DMA((count,)), pltpu.SemaphoreType.DMA((3,))],
         compiler_params=params(VMEM_MIB),
         cost_estimate=cost(10 * rows * hidden * width, 2 * width * (3 * rows + 3 * hidden)),

time: 189 us -> 189 us (level)
  no operation moved by 1% of the time
where the time goes in v4:
time: 189 us; the launch traced here: 188 us
  starting transfers between devices  72.1 us (38%)
  waiting for transfers between devices  67.3 us (36%)
  Pallas kernels  45.2 us (24%)
  local copies, waits for them, and re-layouts  2.48 us (1%)
    ppermute x32, waiting for transfers between devices, send(): return lax.ppermute(array, 'ctx', pairs)  59.3 us
    ppermute x32, starting transfers between devices, send(): return lax.ppermute(array, 'ctx', pairs)  45.9 us
    pallas_call x2, Pallas kernels, expert_rows(): pl.pallas_call(functools.partial(expert_kernel, count), out_shape=[jax.Sh...  17.6 us
    pallas_call x1, Pallas kernels, per_device(): pl.pallas_call(grads_kernel, grid=(steps,), out_shape=[jax.ShapeDtypeStru...  11.5 us
    all_to_all x1, starting transfers between devices, per_device(): lax.all_to_all(filled, 'exp', split_axis=0, concat_axis=0, tiled=True)  9.98 us
    all_to_all x1, waiting for transfers between devices, per_device(): lax.all_to_all(filled, 'exp', split_axis=0, concat_axis=0, tiled=True)  7.93 us
    all_to_all x1, starting transfers between devices, per_device(): lax.all_to_all(summed, 'exp', split_axis=0, concat_axis=0, tiled=True)  7.62 us
    pallas_call x1, Pallas kernels, per_device(): pl.pallas_call(local_kernel, grid=(steps,), out_shape=jax.ShapeDtypeStruc...  6.62 us
  transfers between devices with their start and end apart: 36, of which 19 were waited for; matrix products, arithmetic and copies ran while one was open for 0% of the time, Pallas kernels for 22%

profile of v4, /device:TPU:1, one launch (start us, length us, event | category | flops | bytes accessed | tf_op | source)
XLA Modules:
  0.0 188.0 jit_solution(7469846479486821897)
XLA Ops:
  0.6 2.0 %fill.1 = bf16[16,2,6144]{2,1,0:T(2,128)(2,1)} custom-call(s32[2,8]{1,0:T(2,128)} %bitcast.14, f32[2,8]{1,0:T(2,128)} %bitcast.32, bf16[8,3072]{1,0:T(8,128)(2,1)} %in_ref.1, bf16[8,3072]{1,0:T(8,128)(2,1)} %grad_ref.1), custom_call_target="tpu_custom_call" | custom-call | flops 3145728 | bytes 786432 | tf_op jit(solution)/shard_map/fill/pallas_call | solution.py:369
  2.6 10.0 %all-to-all-start = ((bf16[16,2,6144]{2,1,0:T(2,128)(2,1)}), bf16[16,2,6144]{2,1,0:T(2,128)(2,1)S(1)}, u32[]{:S(2)}, u32[]{:S(2)}) async-start(bf16[16,2,6144]{2,1,0:T(2,128)(2,1)} %fill.1), calls=%async_computation | async-start | bytes 786432 | tf_op jit(solution)/shard_map/all_to_all | solution.py:378
  12.6 6.6 %local_sums.1 = bf16[16,528,128]{2,1,0:T(8,128)(2,1)} custom-call(s32[1,4]{1,0:T(1,128)} %lengths_ref.3, s32[1]{0:T(128)} %bitcast.place_ref, f32[32,128]{1,0:T(8,128)} %bitcast.30, bf16[128,4096]{1,0:T(8,128)(2,1)} %bitcast.16, bf16[128,4096]{1,0:T(8,128)(2,1)} %bitcast.18, bf16[128,4096]{1,0:T(8,128)(2,1)} %bitcast.20, bf16[128,4096]{1,0:T(8,128)(2,1)} %bitcast.22), custom_call_target="tpu_custom_call" | custom-call | flops 268435456 | bytes 6291456 | tf_op jit(solution)/shard_map/local_sums/pallas_call | solution.py:389
  19.2 7.9 %all-to-all-done = bf16[16,2,6144]{2,1,0:T(2,128)(2,1)S(1)} async-done(((bf16[16,2,6144]{2,1,0:T(2,128)(2,1)}), bf16[16,2,6144]{2,1,0:T(2,128)(2,1)S(1)}, u32[]{:S(2)}, u32[]{:S(2)}) %all-to-all-start) | async-done | bytes 393248 | tf_op jit(solution)/shard_map/all_to_all | solution.py:378
  27.3 2.8 %collective-permute-start.6 = (bf16[16,6144]{1,0:T(8,128)(2,1)S(1)}, bf16[16,6144]{1,0:T(8,128)(2,1)S(1)}, u32[]{:S(2)}, u32[]{:S(2)}) collective-permute-start(bf16[16,6144]{1,0:T(8,128)(2,1)S(1)} %get-tuple-element.90), channel_id=1, source_target_pairs={{0,192},{16,208},{32,224},{48,240},{64,0},{80,16},{96,32},{112,48}... | collective-permute-start | bytes 589832 | tf_op jit(solution)/shard_map/ppermute | solution.py:339
  31.2 2.5 %collective-permute-start.2 = (bf16[16,6144]{1,0:T(8,128)(2,1)S(1)}, bf16[16,6144]{1,0:T(8,128)(2,1)S(1)}, u32[]{:S(2)}, u32[]{:S(2)}) collective-permute-start(bf16[16,6144]{1,0:T(8,128)(2,1)S(1)} %get-tuple-element.91), channel_id=1, source_target_pairs={{0,48},{16,0},{32,16},{48,32},{64,112},{80,64},{96,80},{112,96},{1... | collective-permute-start | bytes 589832 | tf_op jit(solution)/shard_map/ppermute | solution.py:339
  34.2 4.6 %collective-permute-done.6 = bf16[16,6144]{1,0:T(8,128)(2,1)S(1)} collective-permute-done((bf16[16,6144]{1,0:T(8,128)(2,1)S(1)}, bf16[16,6144]{1,0:T(8,128)(2,1)S(1)}, u32[]{:S(2)}, u32[]{:S(2)}) %collective-permute-start.6) | collective-permute-done | bytes 196640 | tf_op jit(solution)/shard_map/ppermute | solution.py:339
  47.9 2.7 %collective-permute-done.16.refs_7_ = bf16[32,6144]{1,0:T(8,128)(2,1)S(1)} collective-permute-done((bf16[32,6144]{1,0:T(8,128)(2,1)S(1)}, bf16[32,6144]{1,0:T(8,128)(2,1)S(1)}, u32[]{:S(2)}, u32[]{:S(2)}) %collective-permute-start.16) | collective-permute-done | bytes 393248 | tf_op jit(solution)/shard_map/ppermute | solution.py:339
  50.6 3.4 %collective-permute-start.10 = (bf16[32,6144]{1,0:T(8,128)(2,1)S(1)}, bf16[32,6144]{1,0:T(8,128)(2,1)S(1)}, u32[]{:S(2)}, u32[]{:S(2)}) collective-permute-start(bf16[32,6144]{1,0:T(8,128)(2,1)S(1)} %pad_maximum_fusion.1.refs_10_), channel_id=1, source_target_pairs={{0,48},{16,0},{32,16},{48,32},{64,112},{80,64},{96,80},{112,96},{1... | collective-permute-start | bytes 1179656 | tf_op jit(solution)/shard_map/ppermute | solution.py:339
  56.2 2.1 %collective-permute-start.5 = (bf16[32,6144]{1,0:T(8,128)(2,1)S(1)}, bf16[32,6144]{1,0:T(8,128)(2,1)S(1)}, u32[]{:S(2)}, u32[]{:S(2)}) collective-permute-start(bf16[32,6144]{1,0:T(8,128)(2,1)S(1)} %pad_maximum_fusion.refs_8_), channel_id=1, source_target_pairs={{0,192},{16,208},{32,224},{48,240},{64,0},{80,16},{96,32},{112,48}... | collective-permute-start | bytes 1179656 | tf_op jit(solution)/shard_map/ppermute | solution.py:339
  59.6 3.4 %collective-permute-done.8.refs_5_ = bf16[32,6144]{1,0:T(8,128)(2,1)S(1)} collective-permute-done((bf16[32,6144]{1,0:T(8,128)(2,1)S(1)}, bf16[32,6144]{1,0:T(8,128)(2,1)S(1)}, u32[]{:S(2)}, u32[]{:S(2)}) %collective-permute-start.8) | collective-permute-done | bytes 393248 | tf_op jit(solution)/shard_map/ppermute | solution.py:339
  63.0 3.8 %collective-permute-start.13 = (bf16[32,6144]{1,0:T(8,128)(2,1)S(1)}, bf16[32,6144]{1,0:T(8,128)(2,1)}, u32[]{:S(2)}, u32[]{:S(2)}) collective-permute-start(bf16[32,6144]{1,0:T(8,128)(2,1)S(1)} %collective-permute-done.12.refs_3_), channel_id=1, source_target_pairs={{0,192},{16,208},{32,224},{48,240},{64,0},{80,16},{96,32},{112,48}... | collective-permute-start | bytes 1179656 | tf_op jit(solution)/shard_map/ppermute | solution.py:339
  66.8 3.2 %collective-permute-done.17.refs_3_ = bf16[32,6144]{1,0:T(8,128)(2,1)S(1)} collective-permute-done((bf16[32,6144]{1,0:T(8,128)(2,1)S(1)}, bf16[32,6144]{1,0:T(8,128)(2,1)S(1)}, u32[]{:S(2)}, u32[]{:S(2)}) %collective-permute-start.17) | collective-permute-done | bytes 393248 | tf_op jit(solution)/shard_map/ppermute | solution.py:339
  70.0 3.8 %collective-permute-done.15.refs_2_ = bf16[32,6144]{1,0:T(8,128)(2,1)} collective-permute-done((bf16[32,6144]{1,0:T(8,128)(2,1)S(1)}, bf16[32,6144]{1,0:T(8,128)(2,1)}, u32[]{:S(2)}, u32[]{:S(2)}) %collective-permute-start.15) | collective-permute-done | bytes 393248 | tf_op jit(solution)/shard_map/ppermute | solution.py:339
  74.7 2.4 %collective-permute-done.11.refs_0_ = bf16[32,6144]{1,0:T(8,128)(2,1)} collective-permute-done((bf16[32,6144]{1,0:T(8,128)(2,1)S(1)}, bf16[32,6144]{1,0:T(8,128)(2,1)}, u32[]{:S(2)}, u32[]{:S(2)}) %collective-permute-start.11) | collective-permute-done | bytes 393248 | tf_op jit(solution)/shard_map/ppermute | solution.py:339
  77.1 4.1 %all-to-all-start.1 = ((bf16[16,528,128]{2,1,0:T(8,128)(2,1)}), bf16[16,528,128]{2,1,0:T(8,128)(2,1)S(1)}, u32[]{:S(2)}, u32[]{:S(2)}) async-start(bf16[16,528,128]{2,1,0:T(8,128)(2,1)} %local_sums.1), calls=%async_computation.1 | async-start | bytes 4325376 | tf_op jit(solution)/shard_map/all_to_all | solution.py:419
  81.1 7.5 %experts.3 = (bf16[32,3072]{1,0:T(8,128)(2,1)}, bf16[32,3072]{1,0:T(8,128)(2,1)}, bf16[32,3072]{1,0:T(8,128)(2,1)}, bf16[32,3072]{1,0:T(8,128)(2,1)}) custom-call(bf16[32,6144]{1,0:T(8,128)(2,1)} %collective-permute-done.11.refs_0_, bf16[32,6144]{1,0:T(8,128)(2,1)} %collective-permute-done.13.refs_1_, bf16[32,6144]{1,0:T(8,128)(2,1)} %collective-permute-done.15.refs_2_, ...), custom_call_target="tpu_custom_call" | custom-call | flops 1132462080 | bytes 7667712 | tf_op jit(solution)/shard_map/experts/pallas_call | solution.py:240
  94.1 10.0 %experts.2 = (bf16[64,3072]{1,0:T(8,128)(2,1)}, bf16[64,3072]{1,0:T(8,128)(2,1)}, bf16[64,3072]{1,0:T(8,128)(2,1)}, bf16[64,3072]{1,0:T(8,128)(2,1)}, bf16[64,30...) custom-call(bf16[32,6144]{1,0:T(8,128)(2,1)} %copy-done.16, bf16[32,6144]{1,0:T(8,128)(2,1)} %copy-done.19, ...), custom_call_target="tpu_custom_call" | custom-call | flops 3397386240 | bytes 12386304 | tf_op jit(solution)/shard_map/experts/pallas_call | solution.py:240
  104.2 7.3 %collective-permute-done.18.refs_4_ = bf16[32,3072]{1,0:T(8,128)(2,1)S(1)} collective-permute-done((bf16[32,3072]{1,0:T(8,128)(2,1)}, bf16[32,3072]{1,0:T(8,128)(2,1)S(1)}, u32[]{:S(2)}, u32[]{:S(2)}) %collective-permute-start.18) | collective-permute-done | bytes 196640 | tf_op jit(solution)/shard_map/ppermute | solution.py:339
  113.1 2.8 %add_halves.1 = (bf16[64,3072]{1,0:T(8,128)(2,1)}, bf16[64,3072]{1,0:T(8,128)(2,1)}, bf16[64,3072]{1,0:T(8,128)(2,1)}, bf16[64,3072]{1,0:T(8,128)(2,1)}) custom-call(bf16[64,3072]{1,0:T(8,128)(2,1)} %get-tuple-element.54.refs_0_, bf16[64,3072]{1,0:T(8,128)(2,1)} %get-tuple-element.55.refs_1_, bf16[64,3072]{1,0:T(8,128)(2,1)} %get-tuple-element.56.refs_2_, ...), custom_call_target="tpu_custom_call" | custom-call | flops 786432 | bytes 4718592 | tf_op jit(solution)/shard_map/add_halves/pallas_call | solution.py:266
  118.8 1.8 collective-permute-start.24
  124.1 3.3 %collective-permute-done.22.refs_1_ = bf16[64,3072]{1,0:T(8,128)(2,1)S(1)} collective-permute-done((bf16[64,3072]{1,0:T(8,128)(2,1)}, bf16[64,3072]{1,0:T(8,128)(2,1)S(1)}, u32[]{:S(2)}, u32[]{:S(2)}) %collective-permute-start.22) | collective-permute-done | bytes 393248 | tf_op jit(solution)/shard_map/ppermute | solution.py:339
  127.5 2.1 %collective-permute-done.24.refs_4_ = bf16[64,3072]{1,0:T(8,128)(2,1)S(1)} collective-permute-done((bf16[64,3072]{1,0:T(8,128)(2,1)}, bf16[64,3072]{1,0:T(8,128)(2,1)S(1)}, u32[]{:S(2)}, u32[]{:S(2)}) %collective-permute-start.24) | collective-permute-done | bytes 393248 | tf_op jit(solution)/shard_map/ppermute | solution.py:339
  130.3 4.4 %all-to-all-start.2 = ((bf16[16,512,128]{2,1,0:T(8,128)(2,1)}), bf16[16,512,128]{2,1,0:T(8,128)(2,1)}, u32[]{:S(2)}, u32[]{:S(2)}) async-start(bf16[16,512,128]{2,1,0:T(8,128)(2,1)} %copy-done), calls=%async_computation.2 | async-start | bytes 4194304 | tf_op jit(solution)/shard_map/all_to_all | solution.py:441
  136.0 2.5 %collective-permute-start.26 = (bf16[16,3072]{1,0:T(8,128)(2,1)S(1)}, bf16[16,3072]{1,0:T(8,128)(2,1)S(1)}, u32[]{:S(2)}, u32[]{:S(2)}) collective-permute-start(bf16[16,3072]{1,0:T(8,128)(2,1)S(1)} %get-tuple-element.83), channel_id=1, source_target_pairs={{0,48},{16,0},{32,16},{48,32},{64,112},{80,64},{96,80},{112,96},{1... | collective-permute-start | bytes 294920 | tf_op jit(solution)/shard_map/ppermute | solution.py:339
  138.5 1.8 collective-permute-start.28
  140.3 2.4 %collective-permute-start.29 = (bf16[16,3072]{1,0:T(8,128)(2,1)S(1)}, bf16[16,3072]{1,0:T(8,128)(2,1)S(1)}, u32[]{:S(2)}, u32[]{:S(2)}) collective-permute-start(bf16[16,3072]{1,0:T(8,128)(2,1)S(1)} %get-tuple-element.87), channel_id=1, source_target_pairs={{0,192},{16,208},{32,224},{48,240},{64,0},{80,16},{96,32},{112,48}... | collective-permute-start | bytes 294920 | tf_op jit(solution)/shard_map/ppermute | solution.py:339
  142.8 17.4 %collective-permute-done.26.refs_1_ = bf16[16,3072]{1,0:T(8,128)(2,1)S(1)} collective-permute-done((bf16[16,3072]{1,0:T(8,128)(2,1)S(1)}, bf16[16,3072]{1,0:T(8,128)(2,1)S(1)}, u32[]{:S(2)}, u32[]{:S(2)}) %collective-permute-start.26) | collective-permute-done | bytes 98336 | tf_op jit(solution)/shard_map/ppermute | solution.py:339
  160.2 2.7 %collective-permute-start.31 = (bf16[16,3072]{1,0:T(8,128)(2,1)S(1)}, bf16[16,3072]{1,0:T(8,128)(2,1)S(1)}, u32[]{:S(2)}, u32[]{:S(2)}) collective-permute-start(bf16[16,3072]{1,0:T(8,128)(2,1)S(1)} %get-tuple-element.89), channel_id=1, source_target_pairs={{0,128},{16,144},{32,160},{48,176},{64,192},{80,208},{96,224},{112... | collective-permute-start | bytes 294920 | tf_op jit(solution)/shard_map/ppermute | solution.py:339
  163.9 2.6 %collective-permute-done.31.refs_7_ = bf16[16,3072]{1,0:T(8,128)(2,1)S(1)} collective-permute-done((bf16[16,3072]{1,0:T(8,128)(2,1)S(1)}, bf16[16,3072]{1,0:T(8,128)(2,1)S(1)}, u32[]{:S(2)}, u32[]{:S(2)}) %collective-permute-start.31) | collective-permute-done | bytes 98336 | tf_op jit(solution)/shard_map/ppermute | solution.py:339
  167.3 7.6 %all-to-all-start.3 = ((bf16[16,2,3072]{2,1,0:T(2,128)(2,1)}), bf16[16,2,3072]{2,1,0:T(2,128)(2,1)S(1)}, u32[]{:S(2)}, u32[]{:S(2)}) async-start(bf16[16,2,3072]{2,1,0:T(2,128)(2,1)} %add_last.1), calls=%async_computation.3 | async-start | bytes 393216 | tf_op jit(solution)/shard_map/all_to_all | solution.py:450
  175.0 11.5 %attention_grads.1 = (bf16[128,4096]{1,0:T(8,128)(2,1)}, bf16[128,4096]{1,0:T(8,128)(2,1)}, bf16[128,4096]{1,0:T(8,128)(2,1)}) custom-call(s32[1,4]{1,0:T(1,128)} %lengths_ref.3, s32[1]{0:T(128)} %bitcast.place_ref, f32[32,128]{1,0:T(8,128)} %bitcast.31, bf16[128,4096]{1,0:T(8,128)(2,1)} %bitcast.17, bf16[128,4096]{1,0:T(8,128)(2,1)} %bitcast.19, ...), custom_call_target="tpu_custom_call" | custom-call | flops 1073741824 | bytes 9437184 | tf_op jit(solution)/shard_map/attention_grads/pallas_call | solution.py:463
  (101 shorter events, 34.1 us)
Async XLA Ops:
  2.6 24.5 %all-to-all-start = ((bf16[16,2,6144]{2,1,0:T(2,128)(2,1)}), bf16[16,2,6144]{2,1,0:T(2,128)(2,1)S(1)}, u32[]{:S(2)}, u32[]{:S(2)}) async-start(bf16[16,2,6144]{2,1,0:T(2,128)(2,1)} %fill.1), calls=%async_computation | async-start | bytes 786432 | tf_op jit(solution)/shard_map/all_to_all | solution.py:378
  27.3 11.4 %collective-permute-start.6 = (bf16[16,6144]{1,0:T(8,128)(2,1)S(1)}, bf16[16,6144]{1,0:T(8,128)(2,1)S(1)}, u32[]{:S(2)}, u32[]{:S(2)}) collective-permute-start(bf16[16,6144]{1,0:T(8,128)(2,1)S(1)} %get-tuple-element.90), channel_id=1, source_target_pairs={{0,192},{16,208},{32,224},{48,240},{64,0},{80,16},{96,32},{112,48}... | collective-permute-start | bytes 589832 | tf_op jit(solution)/shard_map/ppermute | solution.py:339
  30.5 12.2 %collective-permute-start.9 = (bf16[16,6144]{1,0:T(8,128)(2,1)S(1)}, bf16[16,6144]{1,0:T(8,128)(2,1)S(1)}, u32[]{:S(2)}, u32[]{:S(2)}) collective-permute-start(bf16[16,6144]{1,0:T(8,128)(2,1)S(1)} %get-tuple-element.90), channel_id=1, source_target_pairs={{0,64},{16,80},{32,96},{48,112},{64,128},{80,144},{96,160},{112,17... | collective-permute-start | bytes 589832 | tf_op jit(solution)/shard_map/ppermute | solution.py:339
  31.2 12.9 %collective-permute-start.2 = (bf16[16,6144]{1,0:T(8,128)(2,1)S(1)}, bf16[16,6144]{1,0:T(8,128)(2,1)S(1)}, u32[]{:S(2)}, u32[]{:S(2)}) collective-permute-start(bf16[16,6144]{1,0:T(8,128)(2,1)S(1)} %get-tuple-element.91), channel_id=1, source_target_pairs={{0,48},{16,0},{32,16},{48,32},{64,112},{80,64},{96,80},{112,96},{1... | collective-permute-start | bytes 589832 | tf_op jit(solution)/shard_map/ppermute | solution.py:339
  33.7 10.4 %collective-permute-start.3 = (bf16[16,6144]{1,0:T(8,128)(2,1)S(1)}, bf16[16,6144]{1,0:T(8,128)(2,1)S(1)}, u32[]{:S(2)}, u32[]{:S(2)}) collective-permute-start(bf16[16,6144]{1,0:T(8,128)(2,1)S(1)} %get-tuple-element.91), channel_id=1, source_target_pairs={{0,32},{16,48},{32,0},{48,16},{64,96},{80,112},{96,64},{112,80},{1... | collective-permute-start | bytes 589832 | tf_op jit(solution)/shard_map/ppermute | solution.py:339
  40.0 10.6 %collective-permute-start.16 = (bf16[32,6144]{1,0:T(8,128)(2,1)S(1)}, bf16[32,6144]{1,0:T(8,128)(2,1)S(1)}, u32[]{:S(2)}, u32[]{:S(2)}) collective-permute-start(bf16[32,6144]{1,0:T(8,128)(2,1)S(1)} %constant_dynamic-update-slice_fusion.2.refs_11_), channel_id=1, source_target_pairs={{0,48},{16,0},{32,16},{48,32},{64,112},{80,64},{96,80},{112,96},{1... | collective-permute-start | bytes 1179656 | tf_op jit(solution)/shard_map/ppermute | solution.py:339
  42.8 11.8 %collective-permute-start.14 = (bf16[32,6144]{1,0:T(8,128)(2,1)S(1)}, bf16[32,6144]{1,0:T(8,128)(2,1)S(1)}, u32[]{:S(2)}, u32[]{:S(2)}) collective-permute-start(bf16[32,6144]{1,0:T(8,128)(2,1)S(1)} %pad_maximum_fusion.1.refs_10_), channel_id=1, source_target_pairs={{0,16},{16,32},{32,48},{48,0},{64,80},{80,96},{96,112},{112,64},{1... | collective-permute-start | bytes 1179656 | tf_op jit(solution)/shard_map/ppermute | solution.py:339
  44.1 12.1 %collective-permute-start.12 = (bf16[32,6144]{1,0:T(8,128)(2,1)S(1)}, bf16[32,6144]{1,0:T(8,128)(2,1)S(1)}, u32[]{:S(2)}, u32[]{:S(2)}) collective-permute-start(bf16[32,6144]{1,0:T(8,128)(2,1)S(1)} %constant_dynamic-update-slice_fusion.refs_9_), channel_id=1, source_target_pairs={{0,192},{16,208},{32,224},{48,240},{64,0},{80,16},{96,32},{112,48}... | collective-permute-start | bytes 1179656 | tf_op jit(solution)/shard_map/ppermute | solution.py:339
  46.6 11.8 %collective-permute-start.1 = (bf16[32,6144]{1,0:T(8,128)(2,1)S(1)}, bf16[32,6144]{1,0:T(8,128)(2,1)S(1)}, u32[]{:S(2)}, u32[]{:S(2)}) collective-permute-start(bf16[32,6144]{1,0:T(8,128)(2,1)S(1)} %pad_maximum_fusion.refs_8_), channel_id=1, source_target_pairs={{0,64},{16,80},{32,96},{48,112},{64,128},{80,144},{96,160},{112,17... | collective-permute-start | bytes 1179656 | tf_op jit(solution)/shard_map/ppermute | solution.py:339
  47.9 15.1 %collective-permute-start.8 = (bf16[32,6144]{1,0:T(8,128)(2,1)S(1)}, bf16[32,6144]{1,0:T(8,128)(2,1)S(1)}, u32[]{:S(2)}, u32[]{:S(2)}) collective-permute-start(bf16[32,6144]{1,0:T(8,128)(2,1)S(1)} %constant_dynamic-update-slice_fusion.2.refs_11_), channel_id=1, source_target_pairs={{0,16},{16,32},{32,48},{48,0},{64,80},{80,96},{96,112},{112,64},{1... | collective-permute-start | bytes 1179656 | tf_op jit(solution)/shard_map/ppermute | solution.py:339
  50.6 12.4 %collective-permute-start.10 = (bf16[32,6144]{1,0:T(8,128)(2,1)S(1)}, bf16[32,6144]{1,0:T(8,128)(2,1)S(1)}, u32[]{:S(2)}, u32[]{:S(2)}) collective-permute-start(bf16[32,6144]{1,0:T(8,128)(2,1)S(1)} %pad_maximum_fusion.1.refs_10_), channel_id=1, source_target_pairs={{0,48},{16,0},{32,16},{48,32},{64,112},{80,64},{96,80},{112,96},{1... | collective-permute-start | bytes 1179656 | tf_op jit(solution)/shard_map/ppermute | solution.py:339
  54.6 12.2 %collective-permute-start.4 = (bf16[32,6144]{1,0:T(8,128)(2,1)S(1)}, bf16[32,6144]{1,0:T(8,128)(2,1)S(1)}, u32[]{:S(2)}, u32[]{:S(2)}) collective-permute-start(bf16[32,6144]{1,0:T(8,128)(2,1)S(1)} %constant_dynamic-update-slice_fusion.refs_9_), channel_id=1, source_target_pairs={{0,64},{16,80},{32,96},{48,112},{64,128},{80,144},{96,160},{112,17... | collective-permute-start | bytes 1179656 | tf_op jit(solution)/shard_map/ppermute | solution.py:339
  56.2 10.6 %collective-permute-start.5 = (bf16[32,6144]{1,0:T(8,128)(2,1)S(1)}, bf16[32,6144]{1,0:T(8,128)(2,1)S(1)}, u32[]{:S(2)}, u32[]{:S(2)}) collective-permute-start(bf16[32,6144]{1,0:T(8,128)(2,1)S(1)} %pad_maximum_fusion.refs_8_), channel_id=1, source_target_pairs={{0,192},{16,208},{32,224},{48,240},{64,0},{80,16},{96,32},{112,48}... | collective-permute-start | bytes 1179656 | tf_op jit(solution)/shard_map/ppermute | solution.py:339
  58.4 11.6 %collective-permute-start.17 = (bf16[32,6144]{1,0:T(8,128)(2,1)S(1)}, bf16[32,6144]{1,0:T(8,128)(2,1)S(1)}, u32[]{:S(2)}, u32[]{:S(2)}) collective-permute-start(bf16[32,6144]{1,0:T(8,128)(2,1)S(1)} %collective-permute-done.16.refs_7_), channel_id=1, source_target_pairs={{0,48},{16,0},{32,16},{48,32},{64,112},{80,64},{96,80},{112,96},{1... | collective-permute-start | bytes 1179656 | tf_op jit(solution)/shard_map/ppermute | solution.py:339
  63.0 10.8 %collective-permute-start.15 = (bf16[32,6144]{1,0:T(8,128)(2,1)S(1)}, bf16[32,6144]{1,0:T(8,128)(2,1)}, u32[]{:S(2)}, u32[]{:S(2)}) collective-permute-start(bf16[32,6144]{1,0:T(8,128)(2,1)S(1)} %collective-permute-done.14.refs_4_), channel_id=1, source_target_pairs={{0,16},{16,32},{32,48},{48,0},{64,80},{80,96},{96,112},{112,64},{1... | collective-permute-start | bytes 1179656 | tf_op jit(solution)/shard_map/ppermute | solution.py:339
  63.0 11.6 %collective-permute-start.13 = (bf16[32,6144]{1,0:T(8,128)(2,1)S(1)}, bf16[32,6144]{1,0:T(8,128)(2,1)}, u32[]{:S(2)}, u32[]{:S(2)}) collective-permute-start(bf16[32,6144]{1,0:T(8,128)(2,1)S(1)} %collective-permute-done.12.refs_3_), channel_id=1, source_target_pairs={{0,192},{16,208},{32,224},{48,240},{64,0},{80,16},{96,32},{112,48}... | collective-permute-start | bytes 1179656 | tf_op jit(solution)/shard_map/ppermute | solution.py:339
  66.8 10.3 %collective-permute-start.11 = (bf16[32,6144]{1,0:T(8,128)(2,1)S(1)}, bf16[32,6144]{1,0:T(8,128)(2,1)}, u32[]{:S(2)}, u32[]{:S(2)}) collective-permute-start(bf16[32,6144]{1,0:T(8,128)(2,1)S(1)} %collective-permute-done.1.refs_0_), channel_id=1, source_target_pairs={{0,64},{16,80},{32,96},{48,112},{64,128},{80,144},{96,160},{112,17... | collective-permute-start | bytes 1179656 | tf_op jit(solution)/shard_map/ppermute | solution.py:339
  77.1 44.4 %all-to-all-start.1 = ((bf16[16,528,128]{2,1,0:T(8,128)(2,1)}), bf16[16,528,128]{2,1,0:T(8,128)(2,1)S(1)}, u32[]{:S(2)}, u32[]{:S(2)}) async-start(bf16[16,528,128]{2,1,0:T(8,128)(2,1)} %local_sums.1), calls=%async_computation.1 | async-start | bytes 4325376 | tf_op jit(solution)/shard_map/all_to_all | solution.py:419
  88.7 22.8 %collective-permute-start.18 = (bf16[32,3072]{1,0:T(8,128)(2,1)}, bf16[32,3072]{1,0:T(8,128)(2,1)S(1)}, u32[]{:S(2)}, u32[]{:S(2)}) collective-permute-start(bf16[32,3072]{1,0:T(8,128)(2,1)} %get-tuple-element.62), channel_id=1, source_target_pairs={{0,64},{16,80},{32,96},{48,112},{64,128},{80,144},{96,160},{112,17... | collective-permute-start | bytes 589832 | tf_op jit(solution)/shard_map/ppermute | solution.py:339
  90.1 21.3 %collective-permute-start.19 = (bf16[32,3072]{1,0:T(8,128)(2,1)}, bf16[32,3072]{1,0:T(8,128)(2,1)S(1)}, u32[]{:S(2)}, u32[]{:S(2)}) collective-permute-start(bf16[32,3072]{1,0:T(8,128)(2,1)} %get-tuple-element.63), channel_id=1, source_target_pairs={{0,192},{16,208},{32,224},{48,240},{64,0},{80,16},{96,32},{112,48}... | collective-permute-start | bytes 589832 | tf_op jit(solution)/shard_map/ppermute | solution.py:339
  91.4 20.9 %collective-permute-start.20 = (bf16[32,3072]{1,0:T(8,128)(2,1)}, bf16[32,3072]{1,0:T(8,128)(2,1)S(1)}, u32[]{:S(2)}, u32[]{:S(2)}) collective-permute-start(bf16[32,3072]{1,0:T(8,128)(2,1)} %get-tuple-element.64), channel_id=1, source_target_pairs={{0,16},{16,32},{32,48},{48,0},{64,80},{80,96},{96,112},{112,64},{1... | collective-permute-start | bytes 589832 | tf_op jit(solution)/shard_map/ppermute | solution.py:339
  92.8 19.6 %collective-permute-start.21 = (bf16[32,3072]{1,0:T(8,128)(2,1)}, bf16[32,3072]{1,0:T(8,128)(2,1)S(1)}, u32[]{:S(2)}, u32[]{:S(2)}) collective-permute-start(bf16[32,3072]{1,0:T(8,128)(2,1)} %get-tuple-element.65), channel_id=1, source_target_pairs={{0,48},{16,0},{32,16},{48,32},{64,112},{80,64},{96,80},{112,96},{1... | collective-permute-start | bytes 589832 | tf_op jit(solution)/shard_map/ppermute | solution.py:339
  115.9 11.6 %collective-permute-start.22 = (bf16[64,3072]{1,0:T(8,128)(2,1)}, bf16[64,3072]{1,0:T(8,128)(2,1)S(1)}, u32[]{:S(2)}, u32[]{:S(2)}) collective-permute-start(bf16[64,3072]{1,0:T(8,128)(2,1)} %get-tuple-element.66), channel_id=1, source_target_pairs={{0,64},{16,80},{32,96},{48,112},{64,128},{80,144},{96,160},{112,17... | collective-permute-start | bytes 1179656 | tf_op jit(solution)/shard_map/ppermute | solution.py:339
  117.6 9.9 %collective-permute-start.23 = (bf16[64,3072]{1,0:T(8,128)(2,1)}, bf16[64,3072]{1,0:T(8,128)(2,1)S(1)}, u32[]{:S(2)}, u32[]{:S(2)}) collective-permute-start(bf16[64,3072]{1,0:T(8,128)(2,1)} %get-tuple-element.67), channel_id=1, source_target_pairs={{0,192},{16,208},{32,224},{48,240},{64,0},{80,16},{96,32},{112,48}... | collective-permute-start | bytes 1179656 | tf_op jit(solution)/shard_map/ppermute | solution.py:339
  118.8 10.8 %collective-permute-start.24 = (bf16[64,3072]{1,0:T(8,128)(2,1)}, bf16[64,3072]{1,0:T(8,128)(2,1)S(1)}, u32[]{:S(2)}, u32[]{:S(2)}) collective-permute-start(bf16[64,3072]{1,0:T(8,128)(2,1)} %get-tuple-element.68), channel_id=1, source_target_pairs={{0,16},{16,32},{32,48},{48,0},{64,80},{80,96},{96,112},{112,64},{1... | collective-permute-start | bytes 1179656 | tf_op jit(solution)/shard_map/ppermute | solution.py:339
  130.3 32.5 %all-to-all-start.2 = ((bf16[16,512,128]{2,1,0:T(8,128)(2,1)}), bf16[16,512,128]{2,1,0:T(8,128)(2,1)}, u32[]{:S(2)}, u32[]{:S(2)}) async-start(bf16[16,512,128]{2,1,0:T(8,128)(2,1)} %copy-done), calls=%async_computation.2 | async-start | bytes 4194304 | tf_op jit(solution)/shard_map/all_to_all | solution.py:441
  136.0 24.1 %collective-permute-start.26 = (bf16[16,3072]{1,0:T(8,128)(2,1)S(1)}, bf16[16,3072]{1,0:T(8,128)(2,1)S(1)}, u32[]{:S(2)}, u32[]{:S(2)}) collective-permute-start(bf16[16,3072]{1,0:T(8,128)(2,1)S(1)} %get-tuple-element.83), channel_id=1, source_target_pairs={{0,48},{16,0},{32,16},{48,32},{64,112},{80,64},{96,80},{112,96},{1... | collective-permute-start | bytes 294920 | tf_op jit(solution)/shard_map/ppermute | solution.py:339
  138.5 25.4 %collective-permute-start.27 = (bf16[16,3072]{1,0:T(8,128)(2,1)S(1)}, bf16[16,3072]{1,0:T(8,128)(2,1)S(1)}, u32[]{:S(2)}, u32[]{:S(2)}) collective-permute-start(bf16[16,3072]{1,0:T(8,128)(2,1)S(1)} %get-tuple-element.84), channel_id=1, source_target_pairs={{0,16},{16,32},{32,48},{48,0},{64,80},{80,96},{96,112},{112,64},{1... | collective-permute-start | bytes 294920 | tf_op jit(solution)/shard_map/ppermute | solution.py:339
  138.5 25.4 %collective-permute-start.28 = (bf16[16,3072]{1,0:T(8,128)(2,1)S(1)}, bf16[16,3072]{1,0:T(8,128)(2,1)S(1)}, u32[]{:S(2)}, u32[]{:S(2)}) collective-permute-start(bf16[16,3072]{1,0:T(8,128)(2,1)S(1)} %get-tuple-element.85), channel_id=1, source_target_pairs={{0,32},{16,48},{32,0},{48,16},{64,96},{80,112},{96,64},{112,80},{1... | collective-permute-start | bytes 294920 | tf_op jit(solution)/shard_map/ppermute | solution.py:339
  140.3 23.6 %collective-permute-start.29 = (bf16[16,3072]{1,0:T(8,128)(2,1)S(1)}, bf16[16,3072]{1,0:T(8,128)(2,1)S(1)}, u32[]{:S(2)}, u32[]{:S(2)}) collective-permute-start(bf16[16,3072]{1,0:T(8,128)(2,1)S(1)} %get-tuple-element.87), channel_id=1, source_target_pairs={{0,192},{16,208},{32,224},{48,240},{64,0},{80,16},{96,32},{112,48}... | collective-permute-start | bytes 294920 | tf_op jit(solution)/shard_map/ppermute | solution.py:339
  142.7 21.2 %collective-permute-start.30 = (bf16[16,3072]{1,0:T(8,128)(2,1)S(1)}, bf16[16,3072]{1,0:T(8,128)(2,1)S(1)}, u32[]{:S(2)}, u32[]{:S(2)}) collective-permute-start(bf16[16,3072]{1,0:T(8,128)(2,1)S(1)} %get-tuple-element.88), channel_id=1, source_target_pairs={{0,64},{16,80},{32,96},{48,112},{64,128},{80,144},{96,160},{112,17... | collective-permute-start | bytes 294920 | tf_op jit(solution)/shard_map/ppermute | solution.py:339
  167.3 19.1 %all-to-all-start.3 = ((bf16[16,2,3072]{2,1,0:T(2,128)(2,1)}), bf16[16,2,3072]{2,1,0:T(2,128)(2,1)S(1)}, u32[]{:S(2)}, u32[]{:S(2)}) async-start(bf16[16,2,3072]{2,1,0:T(2,128)(2,1)} %add_last.1), calls=%async_computation.3 | async-start | bytes 393216 | tf_op jit(solution)/shard_map/all_to_all | solution.py:450
  (25 other events, 320.4 us)
